TPU v7x, 128 devices: a whole 4x4x4 slice. The times are simulated.
128 devices in a mesh: ctx: 32 (over y, x, core), head: 4 (over z).
Axes of the slice: x: 4, y: 4, z: 4, core: 2. Of those that a mesh axis runs over, the one named last changes fastest.
Arguments:
- queries: bfloat16 [8192, 8192], P('ctx', 'head'), may hold values from -6 to 6
- keys: bfloat16 [8192, 1024], P('ctx', 'head'), may hold values from -6 to 6
- values: bfloat16 [8192, 1024], P('ctx', 'head'), may hold values from -6 to 6
- d_out: bfloat16 [8192, 8192], P('ctx', 'head'), may hold values from -6 to 6
- w_key: bfloat16 [8192, 1024], P(None, 'head'), may hold values from -0.1875 to 0.1875
- w_value: bfloat16 [8192, 1024], P(None, 'head'), may hold values from -0.1875 to 0.1875
- pair_list: int32 [512, 2], P('ctx'), may hold values from 0 to 63, as said below
- span_slot: int32 [64], replicated, may hold values from 0 to 63, each once
Outputs:
- grad_q: bfloat16 [8192, 8192], P('ctx', 'head')
- grad_k: bfloat16 [8192, 1024], P('ctx', 'head')
- grad_v: bfloat16 [8192, 1024], P('ctx', 'head')
- grad_x: bfloat16 [8192, 8192], P(('ctx', 'head'))
Inputs may be any that keep to these rules, and one draw needn't show every extreme that they name: `pair_list`: each row is (query span, key span) with the key span no later than the query span; every span's diagonal pair (c, c) is a row; no pair appears twice; the spans 63 and 62 are paired with every key span up to themselves. The rows are stored in drawn order, not by the spans' slots. `span_slot`: slot s lies on index s // 2 of ctx.
All inputs are finite; a program needn't handle non-finite values.
Results may differ from a plain program's by a relative error of at most 0.0074.
Values may be sent and summed in bfloat16 or wider, within the bound.
A program may use at most 192 MiB of HBM per device.

v0:
```python
import jax
import jax.numpy as jnp
from jax import lax
from jax.sharding import PartitionSpec as P

HD = 128
CH = 128


neg_fill = -1e30


def block_scores(query_blk, key_blk, scale_value, on_diagonal):
    scores = (
        jnp.einsum("qkgd,ckd->kgqc", query_blk, key_blk, preferred_element_type=jnp.float32)
        * scale_value
    )
    row_ids = lax.broadcasted_iota(jnp.int32, scores.shape, 2)
    col_ids = lax.broadcasted_iota(jnp.int32, scores.shape, 3)
    keep = jnp.logical_or(row_ids >= col_ids, jnp.logical_not(on_diagonal))
    return (scores, keep)


def per_device(queries, keys, values, d_out, w_key, w_value, pair_list, span_slot):
    my_index = lax.axis_index("ctx")
    span = CH
    local_spans = queries.shape[0] // span
    kv_local = keys.shape[1] // HD
    kv_width = keys.shape[1]
    group = queries.shape[1] // kv_width
    total_slots = span_slot.shape[0]
    scale_value = HD ** (-0.5)
    query_four = queries.reshape(local_spans, span, kv_local, group, HD)
    grad_four = d_out.reshape(local_spans, span, kv_local, group, HD)
    my_first = my_index * local_spans
    all_pairs = lax.all_gather(pair_list, "ctx", axis=0, tiled=True)
    label_ids = jnp.arange(total_slots, dtype=jnp.int32)
    slot_table = (span_slot[:, None] == label_ids[None, :]).astype(jnp.float32)
    query_hot = (all_pairs[:, 0:1] == label_ids[None, :]).astype(jnp.float32)
    key_hot = (all_pairs[:, 1:2] == label_ids[None, :]).astype(jnp.float32)
    query_slots = jnp.dot(query_hot, slot_table, precision=lax.Precision.HIGHEST)
    key_slots = jnp.dot(key_hot, slot_table, precision=lax.Precision.HIGHEST)
    linked = jnp.einsum("pa,pb->ab", query_slots, key_slots, precision=lax.Precision.HIGHEST) > 0.5
    mine = lax.dynamic_slice_in_dim(linked, my_first, local_spans, 0)

    def first_block(state, local_pos, key_slot, key_blk, value_blk):

        def first_work(current):
            run_max, run_sum, run_mix = current
            scores, keep = block_scores(
                query_four[local_pos], key_blk, scale_value, key_slot == my_first + local_pos
            )
            scores = jnp.where(keep, scores, neg_fill)
            mixed = jnp.einsum(
                "qkgd,ckd->kgqc",
                grad_four[local_pos],
                value_blk,
                preferred_element_type=jnp.float32,
            )
            old_max = run_max[local_pos]
            new_max = jnp.maximum(old_max, jnp.max(scores, axis=3))
            factor = jnp.exp(old_max - new_max)
            weights = jnp.exp(scores - new_max[..., None])
            new_sum = run_sum[local_pos] * factor + jnp.sum(weights, axis=3)
            new_mix = run_mix[local_pos] * factor + jnp.sum(weights * mixed, axis=3)
            return (
                run_max.at[local_pos].set(new_max),
                run_sum.at[local_pos].set(new_sum),
                run_mix.at[local_pos].set(new_mix),
            )

        return lax.cond(mine[local_pos, key_slot], first_work, lambda current: current, state)

    stat_shape = (local_spans, kv_local, group, span)
    start_state = (
        jnp.full(stat_shape, neg_fill, jnp.float32),
        jnp.zeros(stat_shape, jnp.float32),
        jnp.zeros(stat_shape, jnp.float32),
    )

    def grad_core(stats, local_pos, key_slot, key_blk, value_blk):
        log_total, mean_mix = stats
        scores, keep = block_scores(
            query_four[local_pos], key_blk, scale_value, key_slot == my_first + local_pos
        )
        weights = jnp.exp(jnp.where(keep, scores - log_total[local_pos][..., None], neg_fill))
        weights_half = weights.astype(jnp.bfloat16)
        dprob = jnp.einsum(
            "qkgd,ckd->kgqc", grad_four[local_pos], value_blk, preferred_element_type=jnp.float32
        )
        dscore = (weights * (dprob - mean_mix[local_pos][..., None])).astype(jnp.bfloat16)
        return (weights_half, dscore)

    def key_terms(local_pos, weights_half, dscore):
        key_part = jnp.einsum(
            "kgqc,qkgd->ckd", dscore, query_four[local_pos], preferred_element_type=jnp.float32
        )
        value_part = jnp.einsum(
            "kgqc,qkgd->ckd", weights_half, grad_four[local_pos], preferred_element_type=jnp.float32
        )
        return jnp.concatenate(
            [key_part.reshape(span, kv_width), value_part.reshape(span, kv_width)], axis=1
        )

    def query_terms(dscore, key_blk):
        return jnp.einsum("kgqc,ckd->qkgd", dscore, key_blk, preferred_element_type=jnp.float32)

    query_zero = jnp.zeros((local_spans, span, kv_local, group, HD), jnp.float32)
    part_zero = jnp.zeros((total_slots * span, 2 * kv_width), jnp.float32)
    key_piece = lax.all_gather(keys, "ctx", axis=0, tiled=True)
    value_piece = lax.all_gather(values, "ctx", axis=0, tiled=True)
    blocks = key_piece.shape[0] // span
    key_blocks = key_piece.reshape(blocks, span, kv_local, HD)
    value_blocks = value_piece.reshape(blocks, span, kv_local, HD)

    def first_visit(step, current):
        block = step // local_spans
        return first_block(
            current, step % local_spans, block, key_blocks[block], value_blocks[block]
        )

    run_max, run_sum, run_mix = lax.fori_loop(0, blocks * local_spans, first_visit, start_state)
    stats = (run_max + jnp.log(run_sum), run_mix / run_sum)
    key_piece = lax.all_gather(keys, "ctx", axis=0, tiled=True)
    value_piece = lax.all_gather(values, "ctx", axis=0, tiled=True)
    blocks = key_piece.shape[0] // span
    both_key_blocks = key_piece.reshape(blocks, span, kv_local, HD)
    both_value_blocks = value_piece.reshape(blocks, span, kv_local, HD)

    def both_visit(step, current):
        block = step // local_spans
        local_pos = step % local_spans
        key_slot = block

        def visit_work(inner):
            q_acc, part_acc = inner
            weights_half, dscore = grad_core(
                stats, local_pos, key_slot, both_key_blocks[block], both_value_blocks[block]
            )
            q_acc = q_acc.at[local_pos].add(query_terms(dscore, both_key_blocks[block]))
            row_start = key_slot * span
            old_rows = lax.dynamic_slice_in_dim(part_acc, row_start, span, 0)
            part_acc = lax.dynamic_update_slice_in_dim(
                part_acc, old_rows + key_terms(local_pos, weights_half, dscore), row_start, 0
            )
            return (q_acc, part_acc)

        return lax.cond(mine[local_pos, key_slot], visit_work, lambda inner: inner, current)

    query_acc, partial_value = lax.fori_loop(
        0, blocks * local_spans, both_visit, (query_zero, part_zero)
    )
    summed = lax.psum_scatter(partial_value, "ctx", scatter_dimension=0, tiled=True)
    grad_q = (query_acc * scale_value).reshape(queries.shape).astype(jnp.bfloat16)
    grad_k = (summed[:, :kv_width] * scale_value).astype(jnp.bfloat16)
    grad_v = summed[:, kv_width:].astype(jnp.bfloat16)
    dims = (((1,), (1,)), ((), ()))
    grad_x = lax.psum_scatter(
        lax.dot_general(grad_k, w_key, dims, preferred_element_type=jnp.float32)
        + lax.dot_general(grad_v, w_value, dims, preferred_element_type=jnp.float32),
        "head",
        scatter_dimension=0,
        tiled=True,
    ).astype(jnp.bfloat16)
    return (grad_q, grad_k, grad_v, grad_x)


def solution(mesh):
    return jax.shard_map(
        per_device,
        mesh=mesh,
        in_specs=(
            P("ctx", "head"),
            P("ctx", "head"),
            P("ctx", "head"),
            P("ctx", "head"),
            P(None, "head"),
            P(None, "head"),
            P("ctx", None),
            P(),
        ),
        out_specs=(P("ctx", "head"), P("ctx", "head"), P("ctx", "head"), P(("ctx", "head"), None)),
        check_vma=False,
    )
```

profile of v0, /device:TPU:1, one launch (start us, length us, event | category | flops | bytes accessed | tf_op | source)
XLA Modules:
  0.0 1577.3 jit_solution(7414304274324287527)
XLA Ops:
  8.7 25.8 %all-gather = s32[32,16,2]{1,2,0:T(2,128)S(1)} all-gather(s32[1,16,2]{1,2,0:T(2,128)} %bitcast.158), channel_id=1, replica_groups=mesh['ctx'=32,'head'=4] {'ctx'}, dimensions={0}, use_global_device_ids=true | all-gather | bytes 4224 | tf_op jit(solution)/shard_map/all_gather | solution.py:36
  37.8 22.1 %all-gather.4.cloned.1.call-done = bf16[8192,256]{1,0:T(8,128)(2,1)} async-done(((bf16[256,256]{1,0:T(8,128)(2,1)}), bf16[8192,256]{1,0:T(8,128)(2,1)}) %all-gather.4.cloned.1.call-update) | async-done | bytes 4194320 | tf_op jit(solution)/shard_map/all_gather | solution.py:124
  59.9 6.9 reshape.222
  66.8 5.3 copy.52
  72.1 35.4 %all-gather.6.cloned.1.call-done = bf16[8192,256]{1,0:T(8,128)(2,1)} async-done(((bf16[256,256]{1,0:T(8,128)(2,1)}), bf16[8192,256]{1,0:T(8,128)(2,1)}) %all-gather.6.cloned.1.call-update) | async-done | bytes 4194320 | tf_op jit(solution)/shard_map/all_gather | solution.py:125
  107.5 6.9 reshape.223
  114.4 5.3 copy.51
  119.8 212.6 %while.40 = (s32[]{:T(128)}, f32[2,2,8,128]{3,2,1,0:T(8,128)S(1)}, f32[2,2,8,128]{3,2,1,0:T(8,128)S(1)}, f32[2,2,8,128]{3,2,1,0:T(8,128)S(1)}, pred[2,64]{1,0:T(...) while((s32[]{:T(128)}, f32[2,2,8,128]{3,2,1,0:T(8,128)S(1)}, ...), condition=%wide.region_7.8_spmd, body=%wide.region_0.7_spmd.sunk | while | flops 136853552 | bytes 4467267 | solution.py:122
  125.7 4.6 conditional.4
  133.9 4.5 conditional.4
  145.6 4.6 conditional.4
  154.9 4.6 conditional.4
  171.5 4.5 conditional.4
  197.6 4.6 conditional.4
  209.3 4.6 conditional.4
  217.5 4.6 conditional.4
  225.6 4.5 conditional.4
  247.0 4.5 conditional.4
  253.9 4.6 conditional.4
  280.0 4.6 conditional.4
  323.0 4.6 conditional.4
  333.5 7.8 broadcast_in_dim.28
  341.3 277.5 %while.41 = (s32[]{:T(128)}, f32[2,128,2,8,128]{1,4,3,2,0:T(8,128)S(1)}, f32[8192,512]{0,1:T(8,128)}, pred[2,64]{1,0:T(4,128)(4,1)S(1)}, bf16[64,128,2,128]{3,1,...) while((s32[]{:T(128)}, ...), condition=%wide.region_12.13_spmd, body=%wide.region_8.0_spmd.sunk | while | flops 338559008 | bytes 14404338 | solution.py:150
  347.9 8.3 conditional.5
  360.2 8.3 conditional.5
  364.2 1.8 fusion.29
  376.4 8.3 conditional.5
  389.9 8.3 conditional.5
  394.0 1.8 fusion.29
  411.5 8.3 conditional.5
  415.6 1.8 fusion.29
  443.7 8.3 conditional.5
  447.8 1.8 fusion.29
  459.9 8.3 conditional.5
  472.2 8.3 conditional.5
  476.2 1.8 fusion.29
  484.4 8.3 conditional.5
  488.5 1.8 fusion.29
  511.3 8.3 conditional.5
  522.2 8.3 conditional.5
  554.4 8.3 conditional.5
  605.2 8.3 conditional.5
  618.8 17.4 %copy.57 = f32[8192,512]{1,0:T(8,128)} copy(f32[8192,512]{0,1:T(8,128)} %get-tuple-element.732) | data formatting | bytes 33554432 | tf_op jit(solution)/shard_map/while | solution.py:150
  636.4 839.9 %reduce-scatter.3.cloned.1.call-done = f32[256,512]{1,0:T(8,128)} async-done(((f32[8192,512]{1,0:T(8,128)}), f32[256,512]{1,0:T(8,128)}) %reduce-scatter.3.cloned.1.call-update) | async-done | bytes 524304 | tf_op jit(solution)/shard_map/reduce_scatter | solution.py:153
  1477.3 3.6 fusion.65
  1481.9 4.5 convolution_add_fusion
  1489.0 79.1 %reduce-scatter.5.cloned.1.call-done = f32[64,8192]{1,0:T(8,128)} async-done(((f32[256,8192]{1,0:T(8,128)}), f32[64,8192]{1,0:T(8,128)}) %reduce-scatter.5.cloned.1.call-update) | async-done | bytes 2097168 | tf_op jit(solution)/shard_map/reduce_scatter | solution.py:158
  1568.1 2.7 convert_element_type.51
  (742 shorter events, 326.0 us)
Async XLA Ops:
  7.2 29.2 %copy-start.3 = (bf16[256,2048]{1,0:T(8,128)(2,1)S(1)}, bf16[256,2048]{1,0:T(8,128)(2,1)}, u32[]{:S(2)}) copy-start(bf16[256,2048]{1,0:T(8,128)(2,1)} %param.27) | copy-start | bytes 3145732
  7.2 52.7 %all-gather.4.cloned.1.call-start = ((), (), s32[]{:S(2)}) async-start(), calls=%async_computation.2 | async-start | bytes 4325376 | tf_op jit(solution)/shard_map/all_gather | solution.py:124
  7.9 99.6 %all-gather.6.cloned.1.call-start = ((), (), s32[]{:S(2)}) async-start(), calls=%async_computation.3 | async-start | bytes 4325376 | tf_op jit(solution)/shard_map/all_gather | solution.py:125
  8.7 1467.6 %reduce-scatter.3.cloned.1.call-start = ((), (), s32[]{:S(2)}) async-start(), calls=%async_computation.4 | async-start | bytes 17301504 | tf_op jit(solution)/shard_map/reduce_scatter | solution.py:153
  34.6 2.3 copy-start.6
  332.3 1.0 copy-start
  349.3 4.8 copy-start.1
  361.6 4.8 copy-start.1
  377.8 4.8 copy-start.1
  391.4 4.8 copy-start.1
  412.9 4.8 copy-start.1
  445.1 4.8 copy-start.1
  461.3 4.8 copy-start.1
  473.6 4.8 copy-start.1
  485.8 4.8 copy-start.1
  512.7 4.8 copy-start.1
  523.6 4.8 copy-start.1
  555.8 4.8 copy-start.1
  606.7 4.8 copy-start.1
  636.3 931.8 %reduce-scatter.5.cloned.1.call-start = ((), (), s32[]{:S(2)}) async-start(), calls=%async_computation.5 | async-start | bytes 10485760 | tf_op jit(solution)/shard_map/reduce_scatter | solution.py:158
  1477.2 3.7 copy-start.4
  1477.3 4.6 copy-start.2
  1481.9 4.5 copy-start.5
Sparse Core Ops, SparseCore 0:
  10.3 49.5 all-gather.3
  62.1 45.3 all-gather.5
  636.4 839.7 reduce-scatter.2
  1486.6 81.5 reduce-scatter.4
where the time goes:
time: 1600 us; the launch traced here: 1580 us
  waiting for transfers between devices  978 us (61%)
  local copies, waits for them, and re-layouts  215 us (13%)
  loops' own time  167 us (10%)
  matrix products  106 us (7%)
  other arithmetic  71.4 us (4%)
  blocking collectives  25.8 us (2%)
    reduce_scatter x1, waiting for transfers between devices, per_device(): lax.psum_scatter(partial_value, 'ctx', scatter_dimension=0, tiled=True)  840 us
    another operation x1, loops' own time, per_device(): lax.fori_loop(0, blocks * local_spans, both_visit, (query_zero, part_zero))  84.7 us
    dynamic_slice x128, local copies, waits for them, and re-layouts, both_visit(): mine[local_pos, key_slot]  83.2 us
    reduce_scatter x1, waiting for transfers between devices, per_device(): lax.psum_scatter(lax.dot_general(grad_k, w_key, dims, preferred_element_t...  79.1 us
    another operation x1, loops' own time, per_device(): lax.fori_loop(0, blocks * local_spans, first_visit, start_state)  77.5 us
    dynamic_slice x128, local copies, waits for them, and re-layouts, first_block(): mine[local_pos, key_slot]  74.5 us
    all_gather x1, waiting for transfers between devices, per_device(): value_piece = lax.all_gather(values, 'ctx', axis=0, tiled=True)  35.4 us
    another operation x26, other arithmetic  34.8 us
  transfers between devices with their start and end apart: 4, of which 4 were waited for; matrix products, arithmetic and copies ran while one was open for 1% of the time, Pallas kernels for 0%

commit v1 on v0

v1 whole, which is shorter than its diff:
```python
import functools

import jax
import jax.numpy as jnp
from jax import lax
from jax.experimental import pallas as pl
from jax.experimental.pallas import tpu as pltpu
from jax.sharding import PartitionSpec as P

MESH = pl.DeviceIdType.MESH
HD = 128
CH = 128
SPANS = 64
NX = 4
NY = 4
NZ = 4
NCTX = NX * NY * 2
NPAD = 16
SCALE = HD ** -0.5
EXP_SCALE = SCALE * 1.4426950408889634
neg_fill = -1e30
QB = 512
MIB = 1024 * 1024


def ctx_coords():
    me = lax.axis_index("ctx")
    return me // (2 * NX), lax.rem(me // 2, NX), lax.rem(me, 2)


def ctx_id(y, x, core):
    return (y * NX + x) * 2 + core


def turn(pos, step, size):
    return lax.rem(pos + step + size, size)


class Plane:
    def __init__(self, first):
        self.y, self.x, self.core = ctx_coords()
        self.first = first

    def at(self, da, db, flip=False):
        dy, dx = (da, db) if self.first == "y" else (db, da)
        core = 1 - self.core if flip else self.core
        return ctx_id(turn(self.y, dy, NY), turn(self.x, dx, NX), core)


def barrier_with(targets):
    barrier = pltpu.get_barrier_semaphore()
    for device in targets:
        pl.semaphore_signal(barrier, inc=1, device_id=device, device_id_type=MESH)
    pl.semaphore_wait(barrier, len(targets))


def ctx_targets():
    plane = Plane("x")
    steps = [(1, 0), (2, 0), (3, 0), (0, 1), (0, 2), (0, 3)]
    return [{"ctx": plane.at(da, db)} for da, db in steps] + [{"ctx": plane.at(0, 0, True)}]


class Copies:
    def __init__(self, send, recv):
        self.send, self.recv, self.started = send, recv, []

    def start(self, src, dst, index, device):
        copy = pltpu.make_async_remote_copy(
            src_ref=src, dst_ref=dst, send_sem=self.send.at[index], recv_sem=self.recv.at[index],
            device_id=device, device_id_type=MESH,
        )
        copy.start()
        self.started.append(copy)

    def landed(self, dst, index, device):
        pltpu.make_async_remote_copy(
            src_ref=dst, dst_ref=dst, send_sem=self.send.at[index], recv_sem=self.recv.at[index],
            device_id=device, device_id_type=MESH,
        ).wait_recv()

    def finish(self):
        for copy in self.started:
            copy.wait_send()


DA_OF = (0, -1, 1, 2)


class Gather:
    def __init__(self, first, own, out, send, recv, half):
        self.plane = Plane(first)
        self.own, self.out, self.half = own, out, half
        self.copies = Copies(send, recv)
        self.rows = out.shape[1]

    def dev(self, da, db, flip=False):
        return {"ctx": self.plane.at(da, db, flip)}

    def region(self, da, db, flip=False):
        return self.out.at[self.plane.at(da, db, flip)]

    def part(self, ref, which):
        return ref.at[pl.ds(0, self.half)] if which == 0 else ref.at[pl.ds(self.half, self.rows - self.half)]

    def spread(self, m, src):
        dst = self.region(DA_OF[m], 0)
        self.copies.start(src, dst, 4 + 4 * m, self.dev(0, 1))
        self.copies.start(src, dst, 5 + 4 * m, self.dev(0, -1))
        self.cross(m, 0, src)

    def cross(self, m, db, src):
        dst = self.region(DA_OF[m], db)
        self.copies.start(src, dst, 20 + 4 * m + (db % 4), self.dev(0, 0, True))

    def begin(self):
        dst = self.region(0, 0)
        self.copies.start(self.own, dst, 0, self.dev(1, 0))
        self.copies.start(self.own, dst, 1, self.dev(-1, 0))
        self.spread(0, self.own)

    def got_a(self, step):
        index = 0 if step < 0 else 1
        region = self.region(step, 0)
        self.copies.landed(region, index, self.dev(step, 0))
        piece = self.part(region, index)
        self.copies.start(piece, piece, 2 + index, self.dev(-step, 0))
        self.spread(1 + index, region)

    def got_a_far(self):
        region = self.region(2, 0)
        self.copies.landed(self.part(region, 0), 2, self.dev(-1, 0))
        self.copies.landed(self.part(region, 1), 3, self.dev(1, 0))
        self.spread(3, region)

    def got_b(self, m, step):
        index = 0 if step < 0 else 1
        region = self.region(DA_OF[m], step)
        self.copies.landed(region, 4 + 4 * m + index, self.dev(0, step))
        piece = self.part(region, index)
        self.copies.start(piece, piece, 6 + 4 * m + index, self.dev(0, -step))
        self.cross(m, step, region)

    def got_b_far(self, m):
        region = self.region(DA_OF[m], 2)
        self.copies.landed(self.part(region, 0), 6 + 4 * m, self.dev(0, -1))
        self.copies.landed(self.part(region, 1), 7 + 4 * m, self.dev(0, 1))
        self.cross(m, 2, region)

    def got_cross(self):
        for m in range(4):
            for db in (0, -1, 1, 2):
                self.copies.landed(self.region(DA_OF[m], db, True), 20 + 4 * m + (db % 4), self.dev(0, 0, True))


def gather_kernel(
    keys_ref, values_ref, q_ref, do_ref, sel_ref, kg_ref, vg_ref, unit_ref,
    give, held, from_core, first_in, mid, last_in,
    k_send, k_recv, v_send, v_recv, u_send, u_recv, own_sem,
):
    barrier_with(ctx_targets())
    y, x, core = ctx_coords()
    plane = Plane("x")
    gathers = [
        Gather("x", keys_ref, kg_ref, k_send, k_recv, 144),
        Gather("y", values_ref, vg_ref, v_send, v_recv, 128),
    ]
    for gather in gathers:
        gather.begin()
    me = plane.at(0, 0)
    own_copies = [
        pltpu.make_async_copy(keys_ref, kg_ref.at[me], own_sem.at[0]),
        pltpu.make_async_copy(values_ref, vg_ref.at[me], own_sem.at[1]),
    ]
    for copy in own_copies:
        copy.start()

    def pick(dst, which):
        first = sel_ref[which, 0:1, :]
        second = sel_ref[which, 1:2, :]

        def head(j, carry):
            cols = pl.ds(pl.multiple_of(j * HD, HD), HD)
            for n, ref in enumerate((q_ref, do_ref)):
                dst[n, j // NX, lax.rem(j, NX)] = ref[0:CH, cols] * first + ref[CH:2 * CH, cols] * second
            return carry

        lax.fori_loop(0, NX * NY, head, 0)

    units = Copies(u_send, u_recv)
    pick(give, 1 - core)
    sibling = {"ctx": plane.at(0, 0, True)}
    units.start(give, from_core, 0, sibling)
    pick(held, core)

    for gather in gathers:
        gather.got_a(-1)
        gather.got_a(1)

    units.landed(from_core, 0, sibling)

    def add_core(j, carry):
        for n in range(2):
            held[n, j // NX, lax.rem(j, NX)] += from_core[n, j // NX, lax.rem(j, NX)]
        return carry

    lax.fori_loop(0, NX * NY, add_core, 0)
    for d in (1, 2, 3):
        far_x, far_y = turn(x, d, NX), turn(y, d, NY)
        units.start(held.at[0, :, far_x], first_in.at[0, d - 1], d, {"ctx": plane.at(d, 0)})
        units.start(held.at[1, far_y], first_in.at[1, d - 1], 3 + d, {"ctx": plane.at(0, d)})

    for gather in gathers:
        gather.got_b(0, -1)
        gather.got_b(0, 1)
    for gather in gathers:
        gather.got_a_far()

    for d in (1, 2, 3):
        units.landed(first_in.at[0, d - 1], d, {"ctx": plane.at(-d, 0)})
        units.landed(first_in.at[1, d - 1], 3 + d, {"ctx": plane.at(0, -d)})
    for n in range(4):
        mid[0, n] = held[0, n, x] + first_in[0, 0, n] + first_in[0, 1, n] + first_in[0, 2, n]
        mid[1, n] = held[1, y, n] + first_in[1, 0, n] + first_in[1, 1, n] + first_in[1, 2, n]
    for d in (1, 2, 3):
        units.start(mid.at[0, turn(y, d, NY)], last_in.at[0, d - 1], 6 + d, {"ctx": plane.at(0, d)})
        units.start(mid.at[1, turn(x, d, NX)], last_in.at[1, d - 1], 9 + d, {"ctx": plane.at(d, 0)})

    for m in (1, 2, 3):
        for gather in gathers:
            gather.got_b(m, -1)
            gather.got_b(m, 1)

    for d in (1, 2, 3):
        units.landed(last_in.at[0, d - 1], 6 + d, {"ctx": plane.at(0, -d)})
        units.landed(last_in.at[1, d - 1], 9 + d, {"ctx": plane.at(-d, 0)})
    unit_ref[0] = mid[0, y] + last_in[0, 0] + last_in[0, 1] + last_in[0, 2]
    unit_ref[1] = mid[1, x] + last_in[1, 0] + last_in[1, 1] + last_in[1, 2]

    for m in range(4):
        for gather in gathers:
            gather.got_b_far(m)
    for gather in gathers:
        gather.got_cross()
    for gather in gathers:
        gather.copies.finish()
    units.finish()
    for copy in own_copies:
        copy.wait()


def gather_all(keys_pad, values, queries, d_out, select):
    vmem = pl.BlockSpec(memory_space=pltpu.VMEM)
    anyspace = pl.BlockSpec(memory_space=pl.ANY)
    blk = jnp.bfloat16
    return pl.pallas_call(
        gather_kernel,
        out_shape=(
            jax.ShapeDtypeStruct((NCTX,) + keys_pad.shape, blk),
            jax.ShapeDtypeStruct((NCTX,) + values.shape, blk),
            jax.ShapeDtypeStruct((2, CH, HD), blk),
        ),
        in_specs=[anyspace, anyspace, vmem, vmem, vmem],
        out_specs=(anyspace, anyspace, vmem),
        scratch_shapes=[
            pltpu.VMEM((2, NY, NX, CH, HD), blk),
            pltpu.VMEM((2, NY, NX, CH, HD), blk),
            pltpu.VMEM((2, NY, NX, CH, HD), blk),
            pltpu.VMEM((2, 3, 4, CH, HD), blk),
            pltpu.VMEM((2, 4, CH, HD), blk),
            pltpu.VMEM((2, 3, CH, HD), blk),
            pltpu.SemaphoreType.DMA((36,)),
            pltpu.SemaphoreType.DMA((36,)),
            pltpu.SemaphoreType.DMA((36,)),
            pltpu.SemaphoreType.DMA((36,)),
            pltpu.SemaphoreType.DMA((13,)),
            pltpu.SemaphoreType.DMA((13,)),
            pltpu.SemaphoreType.DMA((2,)),
        ],
        compiler_params=pltpu.CompilerParams(
            collective_id=0, has_side_effects=True, vmem_limit_bytes=32 * MIB
        ),
        name="gather_kv",
    )(keys_pad, values, queries, d_out, select)


def dot_nt(a, b):
    return lax.dot_general(a, b, (((1,), (1,)), ((), ())), preferred_element_type=jnp.float32)


def dot_nn(a, b):
    return lax.dot_general(a, b, (((1,), (0,)), ((), ())), preferred_element_type=jnp.float32)


def dot_tn(a, b):
    return lax.dot_general(a, b, (((0,), (0,)), ((), ())), preferred_element_type=jnp.float32)


def attend_kernel(
    mine, span_slot, slot_label, q_hbm, do_hbm, kg_hbm, vg_hbm, unit_ref,
    gq_ref, hdq_ref, pk_hbm, pv_hbm,
    kg, vg, qs, ds, probs, dprob, tops, stat, acck, accv, dqt, todo, sems, qsems,
):
    me = lax.axis_index("ctx")
    core = lax.rem(me, 2)
    unit = me // 2
    loads = [
        pltpu.make_async_copy(kg_hbm, kg, sems.at[0]),
        pltpu.make_async_copy(vg_hbm, vg, sems.at[1]),
    ]
    for copy in loads:
        copy.start()
    stacks = []
    for i in range(2):
        for h in range(16):
            for n, (src, dst) in enumerate(((q_hbm, qs), (do_hbm, ds))):
                stacks.append(
                    pltpu.make_async_copy(
                        src.at[pl.ds(i * CH, CH), pl.ds(h * HD, HD)],
                        dst.at[i, pl.ds(h * CH, CH)],
                        qsems.at[n, i * 16 + h],
                    )
                )
    for copy in stacks:
        copy.start()
    for copy in loads:
        copy.wait()

    def row_minus_col(width):
        rows = lax.broadcasted_iota(jnp.int32, (CH, width), 0)
        cols = lax.rem(lax.broadcasted_iota(jnp.int32, (CH, width), 1), CH)
        return rows - cols

    hcols = pl.ds(pl.multiple_of((unit // 8) * HD, HD), HD)
    ocols = pl.ds(pl.multiple_of((1 - unit // 8) * HD, HD), HD)
    label = SPANS - 2 + core
    q_unit = unit_ref[0]
    do_unit = unit_ref[1]

    def place(t):
        return pl.ds(pl.multiple_of(lax.rem(t, 4) * HD, HD), HD)

    def unit_first(t, carry):
        top, total, mix = carry
        scores = dot_nt(kg[t, 0:2 * CH, hcols], q_unit) * EXP_SCALE
        diff = row_minus_col(HD)
        low = jnp.where(diff <= (label - slot_label[2 * t]) * CH, scores[0:CH], neg_fill)
        high = jnp.where(diff <= (label - slot_label[2 * t + 1]) * CH, scores[CH:2 * CH], neg_fill)
        scores = jnp.concatenate([low, high], axis=0)
        mixed = dot_nt(vg[t, :, hcols], do_unit)
        new_top = jnp.maximum(top, jnp.max(scores, axis=0, keepdims=True))
        weights = jnp.exp2(scores - new_top)
        factor = jnp.exp2(top - new_top)
        probs[t // 4, :, place(t)] = weights
        dprob[t // 4, :, place(t)] = mixed
        tops[t, :, 0:HD] = new_top
        return (
            new_top,
            total * factor + jnp.sum(weights, axis=0, keepdims=True),
            mix * factor + jnp.sum(weights * mixed, axis=0, keepdims=True),
        )

    zero_row = jnp.zeros((1, HD), jnp.float32)
    top, total, mix = lax.fori_loop(
        0, NCTX, unit_first, (jnp.full((1, HD), neg_fill, jnp.float32), zero_row, zero_row)
    )
    over = 1.0 / total
    delta = mix * over

    def unit_second(t, acc):
        factor = jnp.exp2(tops[t, :, 0:HD] - top) * over
        weights = probs[t // 4, :, place(t)] * factor
        dscore = (weights * (dprob[t // 4, :, place(t)] - delta)).astype(jnp.bfloat16)
        accv[t, :, hcols] = dot_nn(weights.astype(jnp.bfloat16), do_unit)
        acck[t, :, hcols] = dot_nn(dscore, q_unit)
        accv[t, :, ocols] = jnp.zeros((2 * CH, HD), jnp.float32)
        acck[t, :, ocols] = jnp.zeros((2 * CH, HD), jnp.float32)
        return acc + dot_tn(kg[t, 0:2 * CH, hcols], dscore)

    acc = lax.fori_loop(0, NCTX, unit_second, jnp.zeros((HD, CH), jnp.float32))
    hdq_ref[...] = (acc * SCALE).T.astype(jnp.bfloat16)

    for copy in stacks:
        copy.wait()

    def span_work(i, carry):
        own_slot = 2 * me + i
        own_label = slot_label[own_slot]

        @pl.when(own_label < SPANS - 2)
        def _():
            todo[0] = own_slot

            def note(c, n):
                todo[n] = span_slot[c]
                wanted = jnp.logical_and(mine[i * SPANS + c] > 0, c != own_label)
                return n + wanted.astype(jnp.int32)

            count = lax.fori_loop(0, SPANS, note, jnp.int32(1))
            todo[count] = own_slot

            def block_of(ref, slot, cols):
                return ref[slot // 2, pl.ds(pl.multiple_of(lax.rem(slot, 2) * CH, CH), CH), cols]

            def both(ref, t, cols):
                return jnp.concatenate(
                    [block_of(ref, todo[2 * t], cols), block_of(ref, todo[2 * t + 1], cols)], axis=0
                )

            def combo(m, inner):
                cols = pl.ds(pl.multiple_of((m // 2) * HD, HD), HD)
                rows = pl.ds(pl.multiple_of(m * QB, QB), QB)
                stat[0:1, :] = jnp.full((1, QB), neg_fill, jnp.float32)
                stat[1:2, :] = jnp.zeros((1, QB), jnp.float32)
                stat[2:3, :] = jnp.zeros((1, QB), jnp.float32)

                def first(t, limits=None):
                    scores = dot_nt(both(kg, t, cols), qs[i, rows, :]) * EXP_SCALE
                    if limits is not None:
                        diff = row_minus_col(QB)
                        low = jnp.where(diff <= limits[0], scores[0:CH], neg_fill)
                        high = jnp.where(diff <= limits[1], scores[CH:2 * CH], neg_fill)
                        scores = jnp.concatenate([low, high], axis=0)
                    mixed = dot_nt(both(vg, t, cols), ds[i, rows, :])
                    old_top = stat[0:1, :]
                    new_top = jnp.maximum(old_top, jnp.max(scores, axis=0, keepdims=True))
                    weights = jnp.exp2(scores - new_top)
                    factor = jnp.exp2(old_top - new_top)
                    probs[t] = weights
                    dprob[t] = mixed
                    tops[t] = new_top
                    stat[0:1, :] = new_top
                    stat[1:2, :] = stat[1:2, :] * factor + jnp.sum(weights, axis=0, keepdims=True)
                    stat[2:3, :] = stat[2:3, :] * factor + jnp.sum(weights * mixed, axis=0, keepdims=True)

                first(0, (0, jnp.where(count >= 2, CH, -CH)))

                def plain(t, c):
                    first(t)
                    return c

                lax.fori_loop(1, count // 2, plain, 0)

                @pl.when(jnp.logical_and(lax.rem(count, 2) == 1, count > 1))
                def _():
                    first(count // 2, (CH, -CH))

                top_row = stat[0:1, :]
                over_row = 1.0 / stat[1:2, :]
                delta_row = stat[2:3, :] * over_row
                dqt[...] = jnp.zeros_like(dqt)

                def second(t, c):
                    factor = jnp.exp2(tops[t] - top_row) * over_row
                    weights = probs[t] * factor
                    dscore = (weights * (dprob[t] - delta_row)).astype(jnp.bfloat16)
                    value_part = dot_nn(weights.astype(jnp.bfloat16), ds[i, rows, :])
                    key_part = dot_nn(dscore, qs[i, rows, :])
                    for u in range(2):
                        slot = todo[2 * t + u]
                        at = pl.ds(pl.multiple_of(lax.rem(slot, 2) * CH, CH), CH)
                        accv[slot // 2, at, cols] += value_part[u * CH:(u + 1) * CH]
                        acck[slot // 2, at, cols] += key_part[u * CH:(u + 1) * CH]
                    dqt[...] += dot_tn(both(kg, t, cols), dscore)
                    return c

                lax.fori_loop(0, (count + 1) // 2, second, 0)
                for r in range(QB // CH):
                    part = (dqt[:, r * CH:(r + 1) * CH] * SCALE).T
                    gq_ref[
                        pl.ds(pl.multiple_of(i * CH, CH), CH),
                        pl.ds(pl.multiple_of(m * QB + r * HD, HD), HD),
                    ] = part.astype(jnp.bfloat16)
                return inner

            lax.fori_loop(0, 16 * CH // QB, combo, 0)

        return carry

    lax.fori_loop(0, 2, span_work, 0)

    stores = []
    step = 8
    for s in range(NCTX // step):
        def narrow(t, carry):
            kg[t, 0:2 * CH, :] = acck[t].astype(jnp.bfloat16)
            vg[t] = accv[t].astype(jnp.bfloat16)
            return carry

        lax.fori_loop(s * step, (s + 1) * step, narrow, 0)
        part = pl.ds(s * step, step)
        stores.append(pltpu.make_async_copy(kg.at[part, pl.ds(0, 2 * CH)], pk_hbm.at[part], qsems.at[0, s]))
        stores.append(pltpu.make_async_copy(vg.at[part], pv_hbm.at[part], qsems.at[1, s]))
        stores[-1].start()
        stores[-2].start()
    for copy in stores:
        copy.wait()


def attend(mine, span_slot, slot_label, queries, d_out, kg, vg, unit):
    vmem = pl.BlockSpec(memory_space=pltpu.VMEM)
    smem = pl.BlockSpec(memory_space=pltpu.SMEM)
    anyspace = pl.BlockSpec(memory_space=pl.ANY)
    blk = jnp.bfloat16
    return pl.pallas_call(
        attend_kernel,
        out_shape=(
            jax.ShapeDtypeStruct((2 * CH, 16 * HD), blk),
            jax.ShapeDtypeStruct((CH, HD), blk),
            jax.ShapeDtypeStruct((NCTX, 2 * CH, 2 * HD), blk),
            jax.ShapeDtypeStruct((NCTX, 2 * CH, 2 * HD), blk),
        ),
        in_specs=[smem, smem, smem, anyspace, anyspace, anyspace, anyspace, vmem],
        out_specs=(vmem, vmem, anyspace, anyspace),
        scratch_shapes=[
            pltpu.VMEM(kg.shape, blk),
            pltpu.VMEM(vg.shape, blk),
            pltpu.VMEM((2, 16 * CH, HD), blk),
            pltpu.VMEM((2, 16 * CH, HD), blk),
            pltpu.VMEM((31, 2 * CH, QB), jnp.float32),
            pltpu.VMEM((31, 2 * CH, QB), jnp.float32),
            pltpu.VMEM((32, 1, QB), jnp.float32),
            pltpu.VMEM((8, QB), jnp.float32),
            pltpu.VMEM((NCTX, 2 * CH, 2 * HD), jnp.float32),
            pltpu.VMEM((NCTX, 2 * CH, 2 * HD), jnp.float32),
            pltpu.VMEM((HD, QB), jnp.float32),
            pltpu.SMEM((SPANS + 8,), jnp.int32),
            pltpu.SemaphoreType.DMA((2,)),
            pltpu.SemaphoreType.DMA((2, 32)),
        ],
        compiler_params=pltpu.CompilerParams(vmem_limit_bytes=63 * MIB),
        cost_estimate=pl.CostEstimate(flops=8 * 10**9, bytes_accessed=32 * 10**6, transcendentals=4 * 10**6),
        name="attend",
    )(mine, span_slot, slot_label, queries, d_out, kg, vg, unit)


def plus(a, b):
    return (a.astype(jnp.float32) + b.astype(jnp.float32)).astype(jnp.bfloat16)


class Scatter:
    def __init__(self, first, parts, cross_in, near, full, near_b, full_b, send, recv):
        self.plane = Plane(first)
        self.parts, self.cross_in = parts, cross_in
        self.near, self.full, self.near_b, self.full_b = near, full, near_b, full_b
        self.copies = Copies(send, recv)

    def dev(self, da, db, flip=False):
        return {"ctx": self.plane.at(da, db, flip)}

    def cross(self, q):
        for e in range(4):
            self.copies.start(
                self.parts.at[self.plane.at(e, q, True)], self.cross_in.at[q, e], 4 * q + e, self.dev(0, 0, True)
            )

    def add_cross(self, q, e):
        self.copies.landed(self.cross_in.at[q, e], 4 * q + e, self.dev(0, 0, True))
        self.cross_in[q, e] = plus(self.cross_in[q, e], self.parts[self.plane.at(e, q)])

    def far(self, q):
        self.add_cross(q, 2)
        self.copies.start(self.cross_in.at[q, 2, pl.ds(0, CH)], self.near.at[q, 0], 16 + 4 * q, self.dev(1, 0))
        self.copies.start(self.cross_in.at[q, 2, pl.ds(CH, CH)], self.near.at[q, 1], 17 + 4 * q, self.dev(-1, 0))

    def next(self, q):
        self.add_cross(q, 1)
        self.add_cross(q, 3)
        self.copies.landed(self.near.at[q, 0], 16 + 4 * q, self.dev(-1, 0))
        self.cross_in[q, 1, 0:CH] = plus(self.cross_in[q, 1, 0:CH], self.near[q, 0])
        self.copies.start(self.cross_in.at[q, 1], self.full.at[q, 0], 18 + 4 * q, self.dev(1, 0))
        self.copies.landed(self.near.at[q, 1], 17 + 4 * q, self.dev(1, 0))
        self.cross_in[q, 3, CH:2 * CH] = plus(self.cross_in[q, 3, CH:2 * CH], self.near[q, 1])
        self.copies.start(self.cross_in.at[q, 3], self.full.at[q, 1], 19 + 4 * q, self.dev(-1, 0))

    def last(self, q):
        self.add_cross(q, 0)
        self.copies.landed(self.full.at[q, 0], 18 + 4 * q, self.dev(-1, 0))
        self.copies.landed(self.full.at[q, 1], 19 + 4 * q, self.dev(1, 0))
        return (
            self.cross_in[q, 0].astype(jnp.float32)
            + self.full[q, 0].astype(jnp.float32)
            + self.full[q, 1].astype(jnp.float32)
        )

    def last_far(self):
        self.cross_in[2, 0] = self.last(2).astype(jnp.bfloat16)
        self.copies.start(self.cross_in.at[2, 0, pl.ds(0, CH)], self.near_b.at[0], 32, self.dev(0, 1))
        self.copies.start(self.cross_in.at[2, 0, pl.ds(CH, CH)], self.near_b.at[1], 33, self.dev(0, -1))

    def last_near(self, q):
        index = 0 if q == 1 else 1
        step = 1 if q == 1 else -1
        rows = slice(index * CH, (index + 1) * CH)
        total = self.last(q)
        self.copies.landed(self.near_b.at[index], 32 + index, self.dev(0, -step))
        self.cross_in[q, 0] = total.astype(jnp.bfloat16)
        self.cross_in[q, 0, rows] = (total[rows] + self.near_b[index].astype(jnp.float32)).astype(jnp.bfloat16)
        self.copies.start(self.cross_in.at[q, 0], self.full_b.at[index], 34 + index, self.dev(0, step))

    def finish(self):
        total = self.last(0)
        self.copies.landed(self.full_b.at[0], 34, self.dev(0, -1))
        self.copies.landed(self.full_b.at[1], 35, self.dev(0, 1))
        return total + self.full_b[0].astype(jnp.float32) + self.full_b[1].astype(jnp.float32)


def scatter_kernel(
    pk_ref, pv_ref, gk_ref, gv_ref,
    k_cross, k_near, k_full, k_near_b, k_full_b,
    v_cross, v_near, v_full, v_near_b, v_full_b,
    k_send, k_recv, v_send, v_recv,
):
    barrier_with(ctx_targets())
    ways = [
        Scatter("y", pk_ref, k_cross, k_near, k_full, k_near_b, k_full_b, k_send, k_recv),
        Scatter("x", pv_ref, v_cross, v_near, v_full, v_near_b, v_full_b, v_send, v_recv),
    ]
    order = (2, 1, 3, 0)
    for q in order:
        for way in ways:
            way.cross(q)
    for q in order:
        for way in ways:
            way.far(q)
    for q in order:
        for way in ways:
            way.next(q)
    for way in ways:
        way.last_far()
    for way in ways:
        way.last_near(1)
    for way in ways:
        way.last_near(3)
    gk_ref[...] = (ways[0].finish() * SCALE).astype(jnp.bfloat16)
    gv_ref[...] = ways[1].finish().astype(jnp.bfloat16)
    for way in ways:
        way.copies.finish()


def scatter_sums(pk, pv):
    vmem = pl.BlockSpec(memory_space=pltpu.VMEM)
    blk = jnp.bfloat16
    one = [
        pltpu.VMEM((4, 4, 2 * CH, 2 * HD), blk),
        pltpu.VMEM((4, 2, CH, 2 * HD), blk),
        pltpu.VMEM((4, 2, 2 * CH, 2 * HD), blk),
        pltpu.VMEM((2, CH, 2 * HD), blk),
        pltpu.VMEM((2, 2 * CH, 2 * HD), blk),
    ]
    return pl.pallas_call(
        scatter_kernel,
        out_shape=(jax.ShapeDtypeStruct((2 * CH, 2 * HD), blk),) * 2,
        in_specs=[vmem] * 2,
        out_specs=(vmem,) * 2,
        scratch_shapes=one + one + [pltpu.SemaphoreType.DMA((36,))] * 4,
        compiler_params=pltpu.CompilerParams(
            collective_id=1, has_side_effects=True, vmem_limit_bytes=40 * MIB
        ),
        name="scatter_dkv",
    )(pk, pv)


def project_kernel(
    gk_ref, gv_ref, hdq_ref, wk_hbm, wv_hbm, r1, r2, r3, s1, s2, s3, gx_ref, hg_ref,
    grads, weights, total, half, g_send, g_recv, o_send, o_recv, h_send, h_recv, w_sem, own_sem,
):
    me_z = lax.axis_index("head")
    y, x, core = ctx_coords()
    plane = Plane("x")
    barrier_with(
        [{"head": turn(me_z, d, NZ)} for d in (1, 2, 3)] + ctx_targets()
    )
    width = weights.shape[2]
    piece = width // 2
    sends = Copies(g_send, g_recv)
    for d in (1, 2, 3):
        sends.start(gk_ref, grads.at[d, 0], 2 * d - 2, {"head": turn(me_z, d, NZ)})
        sends.start(gv_ref, grads.at[d, 1], 2 * d - 1, {"head": turn(me_z, d, NZ)})

    units = Copies(h_send, h_recv)
    me = plane.at(0, 0)
    rows = [pl.ds(0, CH // 2), pl.ds(CH // 2, CH // 2)]
    own_copy = pltpu.make_async_copy(hdq_ref, hg_ref.at[y, x, core], own_sem.at[4])
    own_copy.start()
    own_copy.wait()
    for d in (1, 2, 3):
        for n, (da, db) in enumerate(((d, 0), (0, d))):
            units.start(
                hg_ref.at[y, x, core, rows[n]], hg_ref.at[y, x, core, rows[n]], 2 * d - 2 + n,
                {"ctx": plane.at(da, db)},
            )

    wrows = pl.ds(pl.multiple_of(me_z * width, width), width)
    fetches = [[
        pltpu.make_async_copy(wk_hbm.at[wrows], weights.at[0, 0], w_sem.at[0]),
        pltpu.make_async_copy(wv_hbm.at[wrows], weights.at[0, 1], w_sem.at[1]),
    ]]
    mine_rows = pl.ds(pl.multiple_of(core * piece, piece), piece)
    other_rows = pl.ds(pl.multiple_of((1 - core) * piece, piece), piece)
    for d, (near, far) in enumerate(((r1, s1), (r2, s2), (r3, s3)), start=1):
        fetches.append([
            pltpu.make_async_copy(near, weights.at[d, :, mine_rows], w_sem.at[2 * d]),
            pltpu.make_async_copy(far, weights.at[d, :, other_rows], w_sem.at[2 * d + 1]),
        ])
    for pair in fetches:
        for copy in pair:
            copy.start()

    def partial(d, cols):
        left = (gk_ref[...], gv_ref[...]) if d == 0 else (grads[d, 0], grads[d, 1])
        return dot_nt(left[0], weights[d, 0, cols, :]) + dot_nt(left[1], weights[d, 1, cols, :])

    step = 512
    for copy in fetches[0]:
        copy.wait()

    def own_part(n, carry):
        cols = pl.ds(pl.multiple_of(n * step, step), step)
        total[:, cols] = partial(0, cols)
        return carry

    lax.fori_loop(0, width // step, own_part, 0)

    for d in (1, 2, 3):
        for n, (da, db) in enumerate(((-d, 0), (0, -d))):
            at = hg_ref.at[turn(y, db, NY), turn(x, da, NX), core, rows[n]]
            units.landed(at, 2 * d - 2 + n, {"ctx": plane.at(da, db)})
    for d in (1, 2, 3):
        units.start(
            hg_ref.at[y, :, core, rows[0]], hg_ref.at[y, :, core, rows[0]], 4 + 2 * d, {"ctx": plane.at(0, d)}
        )
        units.start(
            hg_ref.at[:, x, core, rows[1]], hg_ref.at[:, x, core, rows[1]], 5 + 2 * d, {"ctx": plane.at(d, 0)}
        )

    for d in (1, 3):
        for n in range(2):
            sends.landed(grads.at[d, n], 2 * d - 2 + n, {"head": turn(me_z, -d, NZ)})
        for copy in fetches[d]:
            copy.wait()

        def next_part(n, carry):
            cols = pl.ds(pl.multiple_of(n * step, step), step)
            total[:, cols] += partial(d, cols)
            return carry

        lax.fori_loop(0, width // step, next_part, 0)

    for n in range(2):
        sends.landed(grads.at[2, n], 2 + n, {"head": turn(me_z, -2, NZ)})
    for copy in fetches[2]:
        copy.wait()
    outs = Copies(o_send, o_recv)
    quarter = half.shape[0] // NZ
    own_copies = []
    for n in range(width // step):
        cols = pl.ds(n * step, step)
        half[:, n * step:(n + 1) * step] = (total[:, n * step:(n + 1) * step] + partial(2, cols)).astype(jnp.bfloat16)
        out_cols = pl.ds(pl.multiple_of(me_z * width + n * step, step), step)
        for d in (1, 2, 3):
            to = turn(me_z, d, NZ)
            outs.start(
                half.at[pl.ds(pl.multiple_of(to * quarter, quarter), quarter), cols],
                gx_ref.at[:, out_cols], 4 * (d - 1) + n, {"head": to},
            )
        own = pltpu.make_async_copy(
            half.at[pl.ds(pl.multiple_of(me_z * quarter, quarter), quarter), cols],
            gx_ref.at[:, out_cols], own_sem.at[n],
        )
        own.start()
        own_copies.append(own)

    for d in (1, 2, 3):
        units.landed(
            hg_ref.at[turn(y, -d, NY), :, core, rows[0]], 4 + 2 * d, {"ctx": plane.at(0, -d)}
        )
        units.landed(
            hg_ref.at[:, turn(x, -d, NX), core, rows[1]], 5 + 2 * d, {"ctx": plane.at(-d, 0)}
        )
    sibling = {"ctx": plane.at(0, 0, True)}
    units.start(hg_ref.at[:, :, core], hg_ref.at[:, :, core], 12, sibling)
    units.landed(hg_ref.at[:, :, 1 - core], 12, sibling)

    for n in range(width // step):
        for d in (1, 2, 3):
            origin = turn(me_z, -d, NZ)
            out_cols = pl.ds(pl.multiple_of(origin * width + n * step, step), step)
            outs.landed(gx_ref.at[:, out_cols], 4 * (d - 1) + n, {"head": origin})
    sends.finish()
    outs.finish()
    units.finish()
    for copy in own_copies:
        copy.wait()


def project(gk, gv, hdq, w_key, w_value, near, far):
    vmem = pl.BlockSpec(memory_space=pltpu.VMEM)
    anyspace = pl.BlockSpec(memory_space=pl.ANY)
    blk = jnp.bfloat16
    depth = w_key.shape[0]
    width = depth // NZ
    return pl.pallas_call(
        project_kernel,
        out_shape=(
            jax.ShapeDtypeStruct((2 * CH // NZ, depth), blk),
            jax.ShapeDtypeStruct((NY, NX, 2, CH, HD), blk),
        ),
        in_specs=[vmem, vmem, vmem] + [anyspace] * 8,
        out_specs=(vmem, vmem),
        scratch_shapes=[
            pltpu.VMEM((NZ, 2, 2 * CH, 2 * HD), blk),
            pltpu.VMEM((NZ, 2, width, 2 * HD), blk),
            pltpu.VMEM((2 * CH, width), jnp.float32),
            pltpu.VMEM((2 * CH, width), blk),
            pltpu.SemaphoreType.DMA((6,)),
            pltpu.SemaphoreType.DMA((6,)),
            pltpu.SemaphoreType.DMA((12,)),
            pltpu.SemaphoreType.DMA((12,)),
            pltpu.SemaphoreType.DMA((13,)),
            pltpu.SemaphoreType.DMA((13,)),
            pltpu.SemaphoreType.DMA((8,)),
            pltpu.SemaphoreType.DMA((5,)),
        ],
        compiler_params=pltpu.CompilerParams(
            collective_id=2, has_side_effects=True, vmem_limit_bytes=40 * MIB
        ),
        name="project",
    )(gk, gv, hdq, w_key, w_value, *near, *far)


def per_device(queries, keys, values, d_out, w_key, w_value, pair_list, span_slot):
    me = lax.axis_index("ctx")
    me_z = lax.axis_index("head")
    core = lax.rem(me, 2)
    depth = w_key.shape[0]
    width = depth // NZ
    piece = width // 2

    near, far = [], []
    for d in (1, 2, 3):
        start = lax.rem(me_z + d, NZ) * width + core * piece
        block = jnp.stack([
            lax.dynamic_slice_in_dim(w_key, start, piece, 0),
            lax.dynamic_slice_in_dim(w_value, start, piece, 0),
        ])
        got = lax.ppermute(block, "head", [(i, (i + d) % NZ) for i in range(NZ)])
        near.append(got)
        far.append(lax.ppermute(got, "ctx", [(i, i ^ 1) for i in range(NCTX)]))

    label_ids = jnp.arange(SPANS, dtype=jnp.int32)
    slot_label = jnp.sum(
        jnp.where(span_slot[None, :] == label_ids[:, None], label_ids[None, :], 0), axis=1, dtype=jnp.int32
    )
    own_slots = 2 * me + jnp.arange(2, dtype=jnp.int32)
    own_labels = jnp.sum(
        jnp.where(span_slot[None, :] == own_slots[:, None], label_ids[None, :], 0), axis=1, dtype=jnp.int32
    )
    dense = jnp.arange(SPANS - 2, SPANS, dtype=jnp.int32)
    select = jnp.broadcast_to(
        (own_labels[None, :, None] == dense[:, None, None]).astype(jnp.bfloat16), (2, 2, HD)
    )
    pair_rows = jnp.pad(pair_list.astype(jnp.bfloat16), ((0, 0), (0, keys.shape[1] - 2)))
    keys_pad = jnp.concatenate([keys, pair_rows], axis=0)
    kg, vg, unit = gather_all(keys_pad, values, queries, d_out, select)
    pairs = kg[:, 2 * CH:, :2].reshape(-1, 2).astype(jnp.int32)
    mine = jnp.max(
        jnp.where(
            jnp.logical_and(
                pairs[None, None, :, 0] == own_labels[:, None, None],
                pairs[None, None, :, 1] == label_ids[None, :, None],
            ),
            1, 0,
        ).astype(jnp.int32),
        axis=2,
    ).reshape(-1)
    gq, hdq, pk, pv = attend(mine, span_slot, slot_label, queries, d_out, kg, vg, unit)
    grad_k, grad_v = scatter_sums(pk, pv)
    grad_x, units = project(grad_k, grad_v, hdq, w_key, w_value, near, far)
    heads = units.reshape(NX * NY, 2, CH, HD)
    rows = []
    for i in range(2):
        which = jnp.clip(own_labels[i] - (SPANS - 2), 0, 1)
        picked = lax.dynamic_index_in_dim(heads, which, 1, keepdims=False)
        picked = picked.transpose(1, 0, 2).reshape(CH, NX * NY * HD)
        rows.append(jnp.where(own_labels[i] >= SPANS - 2, picked, gq[i * CH:(i + 1) * CH]))
    grad_q = jnp.concatenate(rows, axis=0)
    return (grad_q, grad_k, grad_v, grad_x)


def solution(mesh):
    return jax.shard_map(
        per_device,
        mesh=mesh,
        in_specs=(
            P("ctx", "head"),
            P("ctx", "head"),
            P("ctx", "head"),
            P("ctx", "head"),
            P(None, "head"),
            P(None, "head"),
            P("ctx", None),
            P(),
        ),
        out_specs=(P("ctx", "head"), P("ctx", "head"), P("ctx", "head"), P(("ctx", "head"), None)),
        check_vma=False,
    )
```

time: 1600 us -> 192 us (0.12); the launches traced: 1580 us -> 192 us
  waiting for transfers between devices: 978 us -> 0.02 us
  local copies, waits for them, and re-layouts: 215 us -> 14.7 us
  loops' own time: 167 us -> 0 us
  Pallas kernels: 0 us -> 161 us
  matrix products: 106 us -> 0 us
  other arithmetic: 71.4 us -> 4.69 us
  blocking collectives: 25.8 us -> 0 us
    reduce_scatter x2 -> x0, waiting for transfers between devices: 919 us -> none  [the longest x1 840 us: per_device(): lax.psum_scatter(partial_value, 'ctx', scatter_dimension=0, tiled=True)]
    another operation x258 -> x0, loops' own time: 167 us -> none  [the longest x1 84.7 us: per_device(): lax.fori_loop(0, blocks * local_spans, both_visit, (query_zero, part_zero))]
    pallas_call x0 -> x4, Pallas kernels: none -> 161 us  [the longest x1 52.8 us: attend(): pl.pallas_call(attend_kernel, out_shape=(jax.ShapeDtypeStruct((2 * CH, 16...]
    dynamic_slice x256 -> x0, local copies, waits for them, and re-layouts: 158 us -> none  [the longest x128 83.2 us: both_visit(): mine[local_pos, key_slot]]
    dot_general x96 -> x0, matrix products: 106 us -> none  [the longest x26 34.8 us: block_scores(): jnp.einsum('qkgd,ckd->kgqc', query_blk, key_blk, preferred_element_type=j...]
    all_gather x2 -> x0, waiting for transfers between devices: 57.5 us -> none  [the longest x1 35.4 us: per_device(): value_piece = lax.all_gather(values, 'ctx', axis=0, tiled=True)]
    another operation x26 -> x3, other arithmetic: 34.8 us -> 2.22 us  [per_device(): jnp.stack([lax.dynamic_slice_in_dim(w_key, start, piece, 0), lax.dynamic_...]
    while x5 -> x0, local copies, waits for them, and re-layouts: 28.6 us -> none  [the longest x3 23 us: per_device(): lax.fori_loop(0, blocks * local_spans, both_visit, (query_zero, part_zero))]
  transfers between devices with their start and end apart: 4 -> 6, of which waited for: 4 -> 0; matrix products, arithmetic and copies ran while one was open for 1% -> 2% of each run, Pallas kernels for 0% -> 69%
where the time goes in v1:
time: 192 us
  Pallas kernels  161 us (84%)
  local copies, waits for them, and re-layouts  14.7 us (8%)
  starting transfers between devices  7.43 us (4%)
  other arithmetic  4.69 us (2%)
  between operations  3.49 us (2%)
    pallas_call x1, Pallas kernels, attend(): pl.pallas_call(attend_kernel, out_shape=(jax.ShapeDtypeStruct((2 * CH, 16...  52.8 us
    pallas_call x1, Pallas kernels, scatter_sums(): pl.pallas_call(scatter_kernel, out_shape=(jax.ShapeDtypeStruct((2 * CH, 2...  39.9 us
    pallas_call x1, Pallas kernels, gather_all(): pl.pallas_call(gather_kernel, out_shape=(jax.ShapeDtypeStruct((NCTX,) + k...  39.5 us
    pallas_call x1, Pallas kernels, project(): pl.pallas_call(project_kernel, out_shape=(jax.ShapeDtypeStruct((2 * CH //...  29.1 us
    unnamed x34, local copies, waits for them, and re-layouts  11.1 us
    ppermute x3, starting transfers between devices, per_device(): got = lax.ppermute(block, 'head', [(i, (i + d) % NZ) for i in range(NZ)])  6.58 us
  transfers between devices with their start and end apart: 6, of which 0 were waited for; matrix products, arithmetic and copies ran while one was open for 2% of the time, Pallas kernels for 69%

profile of v1, /device:TPU:1, one launch (start us, length us, event | category | flops | bytes accessed | tf_op | source)
XLA Modules:
  0.0 191.6 jit_solution(14787402299313096598)
XLA Ops:
  0.7 2.0 %dynamic-slice_bitcast_fusion.2 = (bf16[1,1024,256]{2,1,0:T(8,128)(2,1)S(1)}, bf16[1,1024,256]{2,1,0:T(8,128)(2,1)S(1)}, bf16[1,1024,256]{2,1,0:T(8,128)(2,1)S(1...) fusion(bf16[8192,256]{1,0:T(8,128)(2,1)} %wv_hbm.1, ...), kind=kLoop, calls=%fused_computation.8 | loop fusion | bytes 6291468 | tf_op jit(solution)/shard_map/stack | solution.py:842
  2.7 0.0 copy-start.13
  2.7 0.0 copy-start.12
  2.7 0.0 copy-start.11
  2.7 0.0 copy-start.3
  2.8 0.0 copy-start.4
  2.8 0.0 copy-start.5
  2.8 1.1 pad_maximum_fusion
  3.8 2.5 %collective-permute-start = (bf16[2,1024,256]{2,1,0:T(8,128)(2,1)}, bf16[2,1024,256]{2,1,0:T(8,128)(2,1)}, u32[]{:S(2)}, u32[]{:S(2)}) collective-permute-start(bf16[2,1024,256]{2,1,0:T(8,128)(2,1)} %pad_maximum_fusion), channel_id=1, source_target_pairs={{0,1},{1,2},{2,3},{3,0},{4,5},{5,6},{6,7},{7,4},{8,9},{9,10},{10,1... | collective-permute-start | bytes 3145736 | tf_op jit(solution)/shard_map/ppermute | solution.py:846
  6.3 0.1 pad_maximum_fusion.1
  6.4 3.4 %collective-permute-start.1 = (bf16[2,1024,256]{2,1,0:T(8,128)(2,1)S(1)}, bf16[2,1024,256]{2,1,0:T(8,128)(2,1)}, u32[]{:S(2)}, u32[]{:S(2)}) collective-permute-start(bf16[2,1024,256]{2,1,0:T(8,128)(2,1)S(1)} %pad_maximum_fusion.1), channel_id=1, source_target_pairs={{0,2},{1,3},{2,0},{3,1},{4,6},{5,7},{6,4},{7,5},{8,10},{9,11},{10,... | collective-permute-start | bytes 3145736 | tf_op jit(solution)/shard_map/ppermute | solution.py:846
  9.8 1.1 pad_maximum_fusion.2
  10.9 0.7 collective-permute-start.2
  11.6 0.2 fusion.2
  11.8 0.1 compare_convert_fusion
  11.9 0.1 copy.27
  12.0 0.1 broadcast_in_dim.49.sel_ref
  12.1 39.5 %gather_kv.1 = (bf16[32,272,256]{2,1,0:T(8,128)(2,1)S(1)}, bf16[32,256,256]{2,1,0:T(8,128)(2,1)S(1)}, bf16[2,128,128]{2,1,0:T(8,128)(2,1)S(1)}) custom-call(bf16[272,256]{1,0:T(8,128)(2,1)S(1)} %fusion.1.keys_ref, bf16[256,256]{1,0:T(8,128)(2,1)S(1)} %copy-done.5, bf16[256,2048]{1,0:T(8,128)(2,1)S(1)} %copy-done.3, bf16[256,2048]{1,0:T(8,128)(2,1)S(1)} %copy-done.4, ...), custom_call_target="tpu_custom_call" | custom-call | tf_op jit(solution)/shard_map/gather_kv/pallas_call | solution.py:255
  51.5 2.0 %copy-done.8 = bf16[32,256,256]{2,1,0:T(8,128)(2,1)} copy-done((bf16[32,256,256]{2,1,0:T(8,128)(2,1)}, bf16[32,256,256]{2,1,0:T(8,128)(2,1)S(1)}, u32[]{:S(2)}) %copy-start.8) | copy-done | bytes 4194328
  53.6 2.0 %copy-done.7 = bf16[32,272,256]{2,1,0:T(8,128)(2,1)} copy-done((bf16[32,272,256]{2,1,0:T(8,128)(2,1)}, bf16[32,272,256]{2,1,0:T(8,128)(2,1)S(1)}, u32[]{:S(2)}) %copy-start.7) | copy-done | bytes 4456472
  55.6 0.0 copy-done.9
  55.7 0.1 fusion.3
  55.8 0.1 copy.35
  55.9 0.1 copy.34
  56.1 0.1 broadcast_compare_fusion
  56.2 0.0 collective-permute-done.r1
  56.2 0.1 collective-permute-start.3
  56.3 0.0 collective-permute-done.1.r2
  56.3 0.5 collective-permute-start.4
  56.8 0.3 collective-permute-start.5
  57.0 0.6 fusion.4
  60.2 0.1 select_reduce_fusion
  60.4 0.6 reshape.140.mine
  61.0 0.6 select_reduce_fusion.1.slot_label
  61.6 52.8 %attend.1 = (bf16[256,2048]{1,0:T(8,128)(2,1)}, bf16[128,128]{1,0:T(8,128)(2,1)}, bf16[32,256,256]{2,1,0:T(8,128)(2,1)}, bf16[32,256,256]{2,1,0:T(8,128)(2,1)}) custom-call(s32[128]{0:T(128)} %reshape.140.mine, s32[64]{0:T(128)} %span_slot.1, s32[64]{0:T(128)} %select_reduce_fusion.1.slot_label, bf16[256,2048]{1,0:T(8,128)(2,1)} %q_hbm.1, ...), custom_call_target="tpu_custom_call" | custom-call | flops 8000000000 | bytes 32000000 | tf_op jit(solution)/shard_map/attend/pallas_call | solution.py:504
  114.5 2.2 %copy-done.1 = bf16[32,256,256]{2,1,0:T(8,128)(2,1)S(1)} copy-done((bf16[32,256,256]{2,1,0:T(8,128)(2,1)S(1)}, bf16[32,256,256]{2,1,0:T(8,128)(2,1)}, u32[]{:S(2)}) %copy-start.1) | copy-done | bytes 4194328
  116.7 2.2 %copy-done.2 = bf16[32,256,256]{2,1,0:T(8,128)(2,1)S(1)} copy-done((bf16[32,256,256]{2,1,0:T(8,128)(2,1)S(1)}, bf16[32,256,256]{2,1,0:T(8,128)(2,1)}, u32[]{:S(2)}) %copy-start.2) | copy-done | bytes 4194328
  118.8 39.9 %scatter_dkv.1 = (bf16[256,256]{1,0:T(8,128)(2,1)S(1)}, bf16[256,256]{1,0:T(8,128)(2,1)S(1)}) custom-call(bf16[32,256,256]{2,1,0:T(8,128)(2,1)S(1)} %copy-done.1, bf16[32,256,256]{2,1,0:T(8,128)(2,1)S(1)} %copy-done.2), custom_call_target="tpu_custom_call" | custom-call | tf_op jit(solution)/shard_map/scatter_dkv/pallas_call | solution.py:650
  158.7 0.0 collective-permute-done.3.s1
  158.7 0.0 collective-permute-done.4.s2
  158.8 0.0 copy-start.10
  158.8 29.1 %project.1 = (bf16[64,8192]{1,0:T(8,128)(2,1)S(1)}, bf16[4,4,2,128,128]{4,3,2,1,0:T(8,128)(2,1)S(1)}) custom-call(bf16[256,256]{1,0:T(8,128)(2,1)S(1)} %get-tuple-element.48.gk_ref, bf16[256,256]{1,0:T(8,128)(2,1)S(1)} %get-tuple-element.49.gv_ref, bf16[128,128]{1,0:T(8,128)(2,1)S(1)} %copy-done.6, bf16[8192,256]{1,0:T(8,128)(2,1)S(1)} %copy-done, ...), custom_call_target="tpu_custom_call" | custom-call | tf_op jit(solution)/shard_map/project/pallas_call | solution.py:802
  187.9 0.1 dynamic-slice_bitcast_fusion.1
  188.1 0.2 bitcast_select_fusion.1
  188.2 1.1 pad_maximum_fusion.3
  189.3 0.7 copy.45
  190.0 0.7 copy.46
  190.6 1.0 copy.47
  (25 shorter events, 0.1 us)
Async XLA Ops:
  2.7 8.9 %copy-start.13 = (s32[64]{0:T(128)S(1)}, s32[64]{0:T(128)}, u32[]{:S(2)}) copy-start(s32[64]{0:T(128)} %span_slot.1) | copy-start | bytes 772
  2.7 9.1 %copy-start.12 = (s32[16,2]{0,1:T(2,128)S(1)}, s32[16,2]{0,1:T(2,128)}, u32[]{:S(2)}) copy-start(s32[16,2]{0,1:T(2,128)} %param.14) | copy-start | bytes 388
  2.7 9.2 %copy-start.11 = (bf16[256,256]{1,0:T(8,128)(2,1)S(1)}, bf16[256,256]{1,0:T(8,128)(2,1)}, u32[]{:S(2)}) copy-start(bf16[256,256]{1,0:T(8,128)(2,1)} %param.9) | copy-start | bytes 393220
  2.7 9.3 %copy-start.3 = (bf16[256,2048]{1,0:T(8,128)(2,1)S(1)}, bf16[256,2048]{1,0:T(8,128)(2,1)}, u32[]{:S(2)}) copy-start(bf16[256,2048]{1,0:T(8,128)(2,1)} %q_hbm.1) | copy-start | bytes 3145732
  2.8 9.3 %copy-start.4 = (bf16[256,2048]{1,0:T(8,128)(2,1)S(1)}, bf16[256,2048]{1,0:T(8,128)(2,1)}, u32[]{:S(2)}) copy-start(bf16[256,2048]{1,0:T(8,128)(2,1)} %do_hbm.1) | copy-start | bytes 3145732
  2.8 9.3 %copy-start.5 = (bf16[256,256]{1,0:T(8,128)(2,1)S(1)}, bf16[256,256]{1,0:T(8,128)(2,1)}, u32[]{:S(2)}) copy-start(bf16[256,256]{1,0:T(8,128)(2,1)} %values_ref.1) | copy-start | bytes 393220
  3.8 52.3 %collective-permute-start = (bf16[2,1024,256]{2,1,0:T(8,128)(2,1)}, bf16[2,1024,256]{2,1,0:T(8,128)(2,1)}, u32[]{:S(2)}, u32[]{:S(2)}) collective-permute-start(bf16[2,1024,256]{2,1,0:T(8,128)(2,1)} %pad_maximum_fusion), channel_id=1, source_target_pairs={{0,1},{1,2},{2,3},{3,0},{4,5},{5,6},{6,7},{7,4},{8,9},{9,10},{10,1... | collective-permute-start | bytes 3145736 | tf_op jit(solution)/shard_map/ppermute | solution.py:846
  6.4 49.9 %collective-permute-start.1 = (bf16[2,1024,256]{2,1,0:T(8,128)(2,1)S(1)}, bf16[2,1024,256]{2,1,0:T(8,128)(2,1)}, u32[]{:S(2)}, u32[]{:S(2)}) collective-permute-start(bf16[2,1024,256]{2,1,0:T(8,128)(2,1)S(1)} %pad_maximum_fusion.1), channel_id=1, source_target_pairs={{0,2},{1,3},{2,0},{3,1},{4,6},{5,7},{6,4},{7,5},{8,10},{9,11},{10,... | collective-permute-start | bytes 3145736 | tf_op jit(solution)/shard_map/ppermute | solution.py:846
  10.9 45.9 %collective-permute-start.2 = (bf16[2,1024,256]{2,1,0:T(8,128)(2,1)}, bf16[2,1024,256]{2,1,0:T(8,128)(2,1)}, u32[]{:S(2)}, u32[]{:S(2)}) collective-permute-start(bf16[2,1024,256]{2,1,0:T(8,128)(2,1)} %pad_maximum_fusion.2), channel_id=1, source_target_pairs={{0,3},{1,0},{2,1},{3,2},{4,7},{5,4},{6,5},{7,6},{8,11},{9,8},{10,9... | collective-permute-start | bytes 3145736 | tf_op jit(solution)/shard_map/ppermute | solution.py:846
  51.5 2.0 %copy-start.8 = (bf16[32,256,256]{2,1,0:T(8,128)(2,1)}, bf16[32,256,256]{2,1,0:T(8,128)(2,1)S(1)}, u32[]{:S(2)}) copy-start(bf16[32,256,256]{2,1,0:T(8,128)(2,1)S(1)} %get-tuple-element.16.vg_hbm) | copy-start | bytes 12582916
  53.6 2.0 %copy-start.7 = (bf16[32,272,256]{2,1,0:T(8,128)(2,1)}, bf16[32,272,256]{2,1,0:T(8,128)(2,1)S(1)}, u32[]{:S(2)}) copy-start(bf16[32,272,256]{2,1,0:T(8,128)(2,1)S(1)} %get-tuple-element.15.kg_hbm) | copy-start | bytes 13369348
  53.6 2.1 %copy-start.9 = (bf16[2,128,128]{2,1,0:T(8,128)(2,1)}, bf16[2,128,128]{2,1,0:T(8,128)(2,1)S(1)}, u32[]{:S(2)}) copy-start(bf16[2,128,128]{2,1,0:T(8,128)(2,1)S(1)} %get-tuple-element.17.unit_ref) | copy-start | bytes 196612
  56.2 102.6 %collective-permute-start.3 = (bf16[2,1024,256]{2,1,0:T(8,128)(2,1)}, bf16[2,1024,256]{2,1,0:T(8,128)(2,1)}, u32[]{:S(2)}, u32[]{:S(2)}) collective-permute-start(bf16[2,1024,256]{2,1,0:T(8,128)(2,1)} %collective-permute-done.r1), channel_id=1, source_target_pairs={{0,4},{4,0},{8,12},{12,8},{16,20},{20,16},{24,28},{28,24},{32,36},... | collective-permute-start | bytes 3145736 | tf_op jit(solution)/shard_map/ppermute | solution.py:848
  56.3 102.5 %collective-permute-start.4 = (bf16[2,1024,256]{2,1,0:T(8,128)(2,1)}, bf16[2,1024,256]{2,1,0:T(8,128)(2,1)}, u32[]{:S(2)}, u32[]{:S(2)}) collective-permute-start(bf16[2,1024,256]{2,1,0:T(8,128)(2,1)} %collective-permute-done.1.r2), channel_id=1, source_target_pairs={{0,4},{4,0},{8,12},{12,8},{16,20},{20,16},{24,28},{28,24},{32,36},... | collective-permute-start | bytes 3145736 | tf_op jit(solution)/shard_map/ppermute | solution.py:848
  56.8 102.0 %collective-permute-start.5 = (bf16[2,1024,256]{2,1,0:T(8,128)(2,1)}, bf16[2,1024,256]{2,1,0:T(8,128)(2,1)}, u32[]{:S(2)}, u32[]{:S(2)}) collective-permute-start(bf16[2,1024,256]{2,1,0:T(8,128)(2,1)} %collective-permute-done.2.r3), channel_id=1, source_target_pairs={{0,4},{4,0},{8,12},{12,8},{16,20},{20,16},{24,28},{28,24},{32,36},... | collective-permute-start | bytes 3145736 | tf_op jit(solution)/shard_map/ppermute | solution.py:848
  114.5 2.2 %copy-start.1 = (bf16[32,256,256]{2,1,0:T(8,128)(2,1)S(1)}, bf16[32,256,256]{2,1,0:T(8,128)(2,1)}, u32[]{:S(2)}) copy-start(bf16[32,256,256]{2,1,0:T(8,128)(2,1)} %get-tuple-element.18.pk_ref) | copy-start | bytes 12582916
  116.7 2.2 %copy-start.2 = (bf16[32,256,256]{2,1,0:T(8,128)(2,1)S(1)}, bf16[32,256,256]{2,1,0:T(8,128)(2,1)}, u32[]{:S(2)}) copy-start(bf16[32,256,256]{2,1,0:T(8,128)(2,1)} %get-tuple-element.19.pv_ref) | copy-start | bytes 12582916
  118.8 39.9 %copy-start = (bf16[8192,256]{1,0:T(8,128)(2,1)S(1)}, bf16[8192,256]{1,0:T(8,128)(2,1)}, u32[]{:S(2)}) copy-start(bf16[8192,256]{1,0:T(8,128)(2,1)} %wk_hbm.1) | copy-start | bytes 12582916
  118.8 39.9 %copy-start.6 = (bf16[128,128]{1,0:T(8,128)(2,1)S(1)}, bf16[128,128]{1,0:T(8,128)(2,1)}, u32[]{:S(2)}) copy-start(bf16[128,128]{1,0:T(8,128)(2,1)} %get-tuple-element.22.hdq_ref) | copy-start | bytes 98308
  158.8 29.3 %copy-start.10 = (bf16[256,2048]{1,0:T(8,128)(2,1)S(1)}, bf16[256,2048]{1,0:T(8,128)(2,1)}, u32[]{:S(2)}) copy-start(bf16[256,2048]{1,0:T(8,128)(2,1)} %get-tuple-element.24) | copy-start | bytes 3145732

commit v2 on v1

--- a/solution.py
+++ b/solution.py
@@ -19,8 +19,9 @@
 SCALE = HD ** -0.5
 EXP_SCALE = SCALE * 1.4426950408889634
 neg_fill = -1e30
-QB = 512
+QB = 1024
 MIB = 1024 * 1024
+VMEM_MIB = 62
 
 
 def ctx_coords():
@@ -58,6 +59,11 @@
     plane = Plane("x")
     steps = [(1, 0), (2, 0), (3, 0), (0, 1), (0, 2), (0, 3)]
     return [{"ctx": plane.at(da, db)} for da, db in steps] + [{"ctx": plane.at(0, 0, True)}]
+
+
+def head_targets(steps):
+    me_z = lax.axis_index("head")
+    return [{"head": turn(me_z, d, NZ)} for d in steps]
 
 
 class Copies:
@@ -153,11 +159,11 @@
 
 
 def gather_kernel(
-    keys_ref, values_ref, q_ref, do_ref, sel_ref, kg_ref, vg_ref, unit_ref,
+    keys_ref, values_ref, q_ref, do_ref, sel_ref, wk_hbm, wv_hbm, kg_ref, vg_ref, unit_ref, near_ref, relay_ref,
     give, held, from_core, first_in, mid, last_in,
-    k_send, k_recv, v_send, v_recv, u_send, u_recv, own_sem,
+    k_send, k_recv, v_send, v_recv, u_send, u_recv, w_send, w_recv, own_sem,
 ):
-    barrier_with(ctx_targets())
+    barrier_with(ctx_targets() + head_targets((1, 3)))
     y, x, core = ctx_coords()
     plane = Plane("x")
     gathers = [
@@ -174,6 +180,23 @@
     for copy in own_copies:
         copy.start()
 
+    me_z = lax.axis_index("head")
+    piece = near_ref.shape[2]
+    moves = Copies(w_send, w_recv)
+    for n, ref in enumerate((wk_hbm, wv_hbm)):
+        for side, step in enumerate((1, -1)):
+            to = turn(me_z, step, NZ)
+            start = pl.multiple_of((2 * to + core) * piece, piece)
+            moves.start(ref.at[pl.ds(start, piece)], near_ref.at[side, n], 2 * side + n, {"head": to})
+    for n, ref in enumerate((wk_hbm, wv_hbm)):
+        for side, step in enumerate((1, -1)):
+            start = (2 * turn(me_z, 2, NZ) + core) * piece + side * (piece // 2)
+            start = pl.multiple_of(start, piece // 2)
+            moves.start(
+                ref.at[pl.ds(start, piece // 2)], relay_ref.at[side, n], 4 + 2 * side + n,
+                {"head": turn(me_z, step, NZ)},
+            )
+
     def pick(dst, which):
         first = sel_ref[which, 0:1, :]
         second = sel_ref[which, 1:2, :]
@@ -241,26 +264,36 @@
             gather.got_b_far(m)
     for gather in gathers:
         gather.got_cross()
+    for n in range(2):
+        for side, step in enumerate((1, -1)):
+            origin = {"head": turn(me_z, -step, NZ)}
+            moves.landed(near_ref.at[side, n], 2 * side + n, origin)
+            moves.landed(relay_ref.at[side, n], 4 + 2 * side + n, origin)
     for gather in gathers:
         gather.copies.finish()
     units.finish()
+    moves.finish()
     for copy in own_copies:
         copy.wait()
 
 
-def gather_all(keys_pad, values, queries, d_out, select):
+def gather_all(keys_pad, values, queries, d_out, select, w_key, w_value):
     vmem = pl.BlockSpec(memory_space=pltpu.VMEM)
     anyspace = pl.BlockSpec(memory_space=pl.ANY)
+    hbm = pl.BlockSpec(memory_space=pl.ANY)
     blk = jnp.bfloat16
+    piece = w_key.shape[0] // NZ // 2
     return pl.pallas_call(
         gather_kernel,
         out_shape=(
             jax.ShapeDtypeStruct((NCTX,) + keys_pad.shape, blk),
             jax.ShapeDtypeStruct((NCTX,) + values.shape, blk),
             jax.ShapeDtypeStruct((2, CH, HD), blk),
+            jax.ShapeDtypeStruct((2, 2, piece) + w_key.shape[1:], blk),
+            jax.ShapeDtypeStruct((2, 2, piece // 2) + w_key.shape[1:], blk),
         ),
-        in_specs=[anyspace, anyspace, vmem, vmem, vmem],
-        out_specs=(anyspace, anyspace, vmem),
+        in_specs=[anyspace, anyspace, vmem, vmem, vmem, hbm, hbm],
+        out_specs=(hbm, hbm, vmem, hbm, hbm),
         scratch_shapes=[
             pltpu.VMEM((2, NY, NX, CH, HD), blk),
             pltpu.VMEM((2, NY, NX, CH, HD), blk),
@@ -274,13 +307,15 @@
             pltpu.SemaphoreType.DMA((36,)),
             pltpu.SemaphoreType.DMA((13,)),
             pltpu.SemaphoreType.DMA((13,)),
+            pltpu.SemaphoreType.DMA((8,)),
+            pltpu.SemaphoreType.DMA((8,)),
             pltpu.SemaphoreType.DMA((2,)),
         ],
         compiler_params=pltpu.CompilerParams(
-            collective_id=0, has_side_effects=True, vmem_limit_bytes=32 * MIB
+            collective_id=0, has_side_effects=True, vmem_limit_bytes=VMEM_MIB * MIB
         ),
         name="gather_kv",
-    )(keys_pad, values, queries, d_out, select)
+    )(keys_pad, values, queries, d_out, select, w_key, w_value)
 
 
 def dot_nt(a, b):
@@ -296,19 +331,30 @@
 
 
 def attend_kernel(
-    mine, span_slot, slot_label, q_hbm, do_hbm, kg_hbm, vg_hbm, unit_ref,
+    span_slot, q_hbm, do_hbm, kg_hbm, vg_hbm, unit_ref,
     gq_ref, hdq_ref, pk_hbm, pv_hbm,
-    kg, vg, qs, ds, probs, dprob, tops, stat, acck, accv, dqt, todo, sems, qsems,
+    kg, vg, qs, ds, tops, stat, acck, accv, dqt, found, flags, slot_label, todo, flag_sem, qsems, load_sems, store_sems,
 ):
     me = lax.axis_index("ctx")
     core = lax.rem(me, 2)
     unit = me // 2
-    loads = [
-        pltpu.make_async_copy(kg_hbm, kg, sems.at[0]),
-        pltpu.make_async_copy(vg_hbm, vg, sems.at[1]),
-    ]
-    for copy in loads:
-        copy.start()
+    hcols = pl.ds(pl.multiple_of((unit // 8) * HD, HD), HD)
+    ocols = pl.ds(pl.multiple_of((1 - unit // 8) * HD, HD), HD)
+    quarter = NCTX // 4
+    pair_copy = pltpu.make_async_copy(
+        kg_hbm.at[:, pl.ds(2 * CH, NPAD)], kg.at[:, pl.ds(2 * CH, NPAD)], load_sems.at[4, 0]
+    )
+    pair_copy.start()
+    loads, late = [], []
+    for n in range(4):
+        part = pl.ds(n * quarter, quarter)
+        for side, (src, dst) in enumerate(((kg_hbm, kg), (vg_hbm, vg))):
+            at = (part, pl.ds(0, 2 * CH), hcols)
+            loads.append(pltpu.make_async_copy(src.at[at], dst.at[at], load_sems.at[n, side]))
+            loads[-1].start()
+    for side, (src, dst) in enumerate(((kg_hbm, kg), (vg_hbm, vg))):
+        at = (slice(None), pl.ds(0, 2 * CH), ocols)
+        late.append(pltpu.make_async_copy(src.at[at], dst.at[at], load_sems.at[5, side]))
     stacks = []
     for i in range(2):
         for h in range(16):
@@ -320,39 +366,48 @@
                         qsems.at[n, i * 16 + h],
                     )
                 )
-    for copy in stacks:
+    for copy in stacks + late:
         copy.start()
-    for copy in loads:
-        copy.wait()
-
-    def row_minus_col(width):
-        rows = lax.broadcasted_iota(jnp.int32, (CH, width), 0)
-        cols = lax.rem(lax.broadcasted_iota(jnp.int32, (CH, width), 1), CH)
-        return rows - cols
-
-    hcols = pl.ds(pl.multiple_of((unit // 8) * HD, HD), HD)
-    ocols = pl.ds(pl.multiple_of((1 - unit // 8) * HD, HD), HD)
+
+    def name_slot(c, carry):
+        slot_label[span_slot[c]] = c
+        return carry
+
+    lax.fori_loop(0, SPANS, name_slot, 0)
+
+    pair_copy.wait()
+    pair_rows = kg[:, 2 * CH:2 * CH + NPAD, 0:HD].reshape(NCTX * NPAD, HD).astype(jnp.float32)
+    lanes = lax.broadcasted_iota(jnp.int32, (1, HD), 1).astype(jnp.float32)
+    for i in range(2):
+        own = slot_label[2 * me + i].astype(jnp.float32)
+        hit = jnp.logical_and(pair_rows[:, 0:1] == own, pair_rows[:, 1:2] == lanes)
+        found[i:i + 1, :] = jnp.max(jnp.where(hit, 1.0, 0.0), axis=0, keepdims=True).astype(jnp.int32)
+    flag_copy = pltpu.make_async_copy(found, flags, flag_sem.at[0])
+    flag_copy.start()
+
     label = SPANS - 2 + core
     q_unit = unit_ref[0]
     do_unit = unit_ref[1]
 
-    def place(t):
-        return pl.ds(pl.multiple_of(lax.rem(t, 4) * HD, HD), HD)
+    def four(ref, t, cols):
+        return jnp.concatenate([ref[2 * t, 0:2 * CH, cols], ref[2 * t + 1, 0:2 * CH, cols]], axis=0)
 
     def unit_first(t, carry):
         top, total, mix = carry
-        scores = dot_nt(kg[t, 0:2 * CH, hcols], q_unit) * EXP_SCALE
-        diff = row_minus_col(HD)
-        low = jnp.where(diff <= (label - slot_label[2 * t]) * CH, scores[0:CH], neg_fill)
-        high = jnp.where(diff <= (label - slot_label[2 * t + 1]) * CH, scores[CH:2 * CH], neg_fill)
-        scores = jnp.concatenate([low, high], axis=0)
-        mixed = dot_nt(vg[t, :, hcols], do_unit)
+        scores = dot_nt(four(kg, t, hcols), q_unit) * EXP_SCALE
+        mixed = dot_nt(four(vg, t, hcols), do_unit)
+        diff = lax.broadcasted_iota(jnp.int32, (CH, HD), 0) - lax.broadcasted_iota(jnp.int32, (CH, HD), 1)
+        scores = jnp.concatenate([
+            jnp.where(diff <= (label - slot_label[4 * t + u]) * CH, scores[u * CH:(u + 1) * CH], neg_fill)
+            for u in range(4)
+        ], axis=0)
         new_top = jnp.maximum(top, jnp.max(scores, axis=0, keepdims=True))
         weights = jnp.exp2(scores - new_top)
         factor = jnp.exp2(top - new_top)
-        probs[t // 4, :, place(t)] = weights
-        dprob[t // 4, :, place(t)] = mixed
-        tops[t, :, 0:HD] = new_top
+        for u in range(2):
+            acck[2 * t + u, :, ocols] = weights[2 * u * CH:2 * (u + 1) * CH]
+            accv[2 * t + u, :, ocols] = mixed[2 * u * CH:2 * (u + 1) * CH]
+        tops[t] = new_top
         return (
             new_top,
             total * factor + jnp.sum(weights, axis=0, keepdims=True),
@@ -360,26 +415,34 @@
         )
 
     zero_row = jnp.zeros((1, HD), jnp.float32)
-    top, total, mix = lax.fori_loop(
-        0, NCTX, unit_first, (jnp.full((1, HD), neg_fill, jnp.float32), zero_row, zero_row)
-    )
+    state = (jnp.full((1, HD), neg_fill, jnp.float32), zero_row, zero_row)
+    for n in range(4):
+        for copy in loads[2 * n:2 * n + 2]:
+            copy.wait()
+        state = lax.fori_loop(n * quarter // 2, (n + 1) * quarter // 2, unit_first, state)
+    top, total, mix = state
     over = 1.0 / total
     delta = mix * over
 
     def unit_second(t, acc):
-        factor = jnp.exp2(tops[t, :, 0:HD] - top) * over
-        weights = probs[t // 4, :, place(t)] * factor
-        dscore = (weights * (dprob[t // 4, :, place(t)] - delta)).astype(jnp.bfloat16)
-        accv[t, :, hcols] = dot_nn(weights.astype(jnp.bfloat16), do_unit)
-        acck[t, :, hcols] = dot_nn(dscore, q_unit)
-        accv[t, :, ocols] = jnp.zeros((2 * CH, HD), jnp.float32)
-        acck[t, :, ocols] = jnp.zeros((2 * CH, HD), jnp.float32)
-        return acc + dot_tn(kg[t, 0:2 * CH, hcols], dscore)
-
-    acc = lax.fori_loop(0, NCTX, unit_second, jnp.zeros((HD, CH), jnp.float32))
+        factor = jnp.exp2(tops[t] - top) * over
+        weights = four(acck, t, ocols) * factor
+        mixed = four(accv, t, ocols)
+        dscore = (weights * (mixed - delta)).astype(jnp.bfloat16)
+        value_part = dot_nn(weights.astype(jnp.bfloat16), do_unit)
+        key_part = dot_nn(dscore, q_unit)
+        for u in range(2):
+            accv[2 * t + u, :, hcols] = value_part[2 * u * CH:2 * (u + 1) * CH]
+            acck[2 * t + u, :, hcols] = key_part[2 * u * CH:2 * (u + 1) * CH]
+            accv[2 * t + u, :, ocols] = jnp.zeros((2 * CH, HD), jnp.float32)
+            acck[2 * t + u, :, ocols] = jnp.zeros((2 * CH, HD), jnp.float32)
+        return acc + dot_tn(four(kg, t, hcols), dscore)
+
+    acc = lax.fori_loop(0, NCTX // 2, unit_second, jnp.zeros((HD, CH), jnp.float32))
     hdq_ref[...] = (acc * SCALE).T.astype(jnp.bfloat16)
 
-    for copy in stacks:
+    flag_copy.wait()
+    for copy in stacks + late:
         copy.wait()
 
     def span_work(i, carry):
@@ -392,111 +455,112 @@
 
             def note(c, n):
                 todo[n] = span_slot[c]
-                wanted = jnp.logical_and(mine[i * SPANS + c] > 0, c != own_label)
+                wanted = jnp.logical_and(flags[i, c] > 0, c != own_label)
                 return n + wanted.astype(jnp.int32)
 
             count = lax.fori_loop(0, SPANS, note, jnp.int32(1))
             todo[count] = own_slot
 
-            def block_of(ref, slot, cols):
-                return ref[slot // 2, pl.ds(pl.multiple_of(lax.rem(slot, 2) * CH, CH), CH), cols]
+            def rows_at(slot):
+                return pl.ds(pl.multiple_of(lax.rem(slot, 2) * CH, CH), CH)
 
             def both(ref, t, cols):
-                return jnp.concatenate(
-                    [block_of(ref, todo[2 * t], cols), block_of(ref, todo[2 * t + 1], cols)], axis=0
-                )
-
-            def combo(m, inner):
-                cols = pl.ds(pl.multiple_of((m // 2) * HD, HD), HD)
-                rows = pl.ds(pl.multiple_of(m * QB, QB), QB)
-                stat[0:1, :] = jnp.full((1, QB), neg_fill, jnp.float32)
-                stat[1:2, :] = jnp.zeros((1, QB), jnp.float32)
-                stat[2:3, :] = jnp.zeros((1, QB), jnp.float32)
-
-                def first(t, limits=None):
-                    scores = dot_nt(both(kg, t, cols), qs[i, rows, :]) * EXP_SCALE
+                a, b = todo[2 * t], todo[2 * t + 1]
+                return jnp.concatenate([ref[a // 2, rows_at(a), cols], ref[b // 2, rows_at(b), cols]], axis=0)
+
+            cols = [pl.ds(g * HD, HD) for g in range(2)]
+            rows = [pl.ds(g * QB, QB) for g in range(2)]
+            limits = (0, jnp.where(count >= 2, CH, -CH))
+            tail = (CH, -CH)
+            odd = jnp.logical_and(lax.rem(count, 2) == 1, count > 1)
+
+            def dots(t, limits):
+                out = []
+                for g in range(2):
+                    scores = dot_nt(both(kg, t, cols[g]), qs[i, rows[g], :]) * EXP_SCALE
                     if limits is not None:
-                        diff = row_minus_col(QB)
-                        low = jnp.where(diff <= limits[0], scores[0:CH], neg_fill)
-                        high = jnp.where(diff <= limits[1], scores[CH:2 * CH], neg_fill)
-                        scores = jnp.concatenate([low, high], axis=0)
-                    mixed = dot_nt(both(vg, t, cols), ds[i, rows, :])
-                    old_top = stat[0:1, :]
+                        diff = lax.broadcasted_iota(jnp.int32, (CH, QB), 0) - lax.rem(
+                            lax.broadcasted_iota(jnp.int32, (CH, QB), 1), CH
+                        )
+                        scores = jnp.concatenate([
+                            jnp.where(diff <= limits[u], scores[u * CH:(u + 1) * CH], neg_fill) for u in range(2)
+                        ], axis=0)
+                    out.append((scores, dot_nt(both(vg, t, cols[g]), ds[i, rows[g], :])))
+                return out
+
+            def first(t, limits=None):
+                for g, (scores, mixed) in enumerate(dots(t, limits)):
+                    old_top = stat[g, 0:1, :]
                     new_top = jnp.maximum(old_top, jnp.max(scores, axis=0, keepdims=True))
                     weights = jnp.exp2(scores - new_top)
                     factor = jnp.exp2(old_top - new_top)
-                    probs[t] = weights
-                    dprob[t] = mixed
-                    tops[t] = new_top
-                    stat[0:1, :] = new_top
-                    stat[1:2, :] = stat[1:2, :] * factor + jnp.sum(weights, axis=0, keepdims=True)
-                    stat[2:3, :] = stat[2:3, :] * factor + jnp.sum(weights * mixed, axis=0, keepdims=True)
-
-                first(0, (0, jnp.where(count >= 2, CH, -CH)))
-
-                def plain(t, c):
-                    first(t)
-                    return c
-
-                lax.fori_loop(1, count // 2, plain, 0)
-
-                @pl.when(jnp.logical_and(lax.rem(count, 2) == 1, count > 1))
-                def _():
-                    first(count // 2, (CH, -CH))
-
-                top_row = stat[0:1, :]
-                over_row = 1.0 / stat[1:2, :]
-                delta_row = stat[2:3, :] * over_row
-                dqt[...] = jnp.zeros_like(dqt)
-
-                def second(t, c):
-                    factor = jnp.exp2(tops[t] - top_row) * over_row
-                    weights = probs[t] * factor
-                    dscore = (weights * (dprob[t] - delta_row)).astype(jnp.bfloat16)
-                    value_part = dot_nn(weights.astype(jnp.bfloat16), ds[i, rows, :])
-                    key_part = dot_nn(dscore, qs[i, rows, :])
+                    stat[g, 0:1, :] = new_top
+                    stat[g, 1:2, :] = stat[g, 1:2, :] * factor + jnp.sum(weights, axis=0, keepdims=True)
+                    stat[g, 2:3, :] = stat[g, 2:3, :] * factor + jnp.sum(weights * mixed, axis=0, keepdims=True)
+
+            def second(t, limits=None):
+                for g, (scores, mixed) in enumerate(dots(t, limits)):
+                    weights = jnp.exp2(scores - stat[g, 3:4, :])
+                    dscore = (weights * (mixed - stat[g, 4:5, :])).astype(jnp.bfloat16)
+                    value_part = dot_nn(weights.astype(jnp.bfloat16), ds[i, rows[g], :])
+                    key_part = dot_nn(dscore, qs[i, rows[g], :])
                     for u in range(2):
                         slot = todo[2 * t + u]
-                        at = pl.ds(pl.multiple_of(lax.rem(slot, 2) * CH, CH), CH)
-                        accv[slot // 2, at, cols] += value_part[u * CH:(u + 1) * CH]
-                        acck[slot // 2, at, cols] += key_part[u * CH:(u + 1) * CH]
-                    dqt[...] += dot_tn(both(kg, t, cols), dscore)
+                        accv[slot // 2, rows_at(slot), cols[g]] += value_part[u * CH:(u + 1) * CH]
+                        acck[slot // 2, rows_at(slot), cols[g]] += key_part[u * CH:(u + 1) * CH]
+                    dqt[g] += dot_tn(both(kg, t, cols[g]), dscore)
+
+            def sweep(work):
+                work(0, limits)
+
+                def plain(t, c):
+                    work(t)
                     return c
 
-                lax.fori_loop(0, (count + 1) // 2, second, 0)
+                lax.fori_loop(1, count // 2, plain, 0)
+
+                @pl.when(odd)
+                def _():
+                    work(count // 2, tail)
+
+            for g in range(2):
+                stat[g, 0:1, :] = jnp.full((1, QB), neg_fill, jnp.float32)
+                stat[g, 1:3, :] = jnp.zeros((2, QB), jnp.float32)
+            sweep(first)
+            for g in range(2):
+                total_row = stat[g, 1:2, :]
+                stat[g, 3:4, :] = stat[g, 0:1, :] + jnp.log2(total_row)
+                stat[g, 4:5, :] = stat[g, 2:3, :] / total_row
+                dqt[g] = jnp.zeros((HD, QB), jnp.float32)
+            sweep(second)
+            for g in range(2):
                 for r in range(QB // CH):
-                    part = (dqt[:, r * CH:(r + 1) * CH] * SCALE).T
                     gq_ref[
-                        pl.ds(pl.multiple_of(i * CH, CH), CH),
-                        pl.ds(pl.multiple_of(m * QB + r * HD, HD), HD),
-                    ] = part.astype(jnp.bfloat16)
-                return inner
-
-            lax.fori_loop(0, 16 * CH // QB, combo, 0)
+                        pl.ds(pl.multiple_of(i * CH, CH), CH), pl.ds(g * QB + r * HD, HD),
+                    ] = (dqt[g, :, r * CH:(r + 1) * CH] * SCALE).T.astype(jnp.bfloat16)
 
         return carry
 
     lax.fori_loop(0, 2, span_work, 0)
 
     stores = []
-    step = 8
-    for s in range(NCTX // step):
+    for n in range(4):
+        part = pl.ds(n * quarter, quarter)
+
         def narrow(t, carry):
             kg[t, 0:2 * CH, :] = acck[t].astype(jnp.bfloat16)
             vg[t] = accv[t].astype(jnp.bfloat16)
             return carry
 
-        lax.fori_loop(s * step, (s + 1) * step, narrow, 0)
-        part = pl.ds(s * step, step)
-        stores.append(pltpu.make_async_copy(kg.at[part, pl.ds(0, 2 * CH)], pk_hbm.at[part], qsems.at[0, s]))
-        stores.append(pltpu.make_async_copy(vg.at[part], pv_hbm.at[part], qsems.at[1, s]))
-        stores[-1].start()
-        stores[-2].start()
+        lax.fori_loop(n * quarter, (n + 1) * quarter, narrow, 0)
+        for side, (src, dst) in enumerate(((kg.at[part, pl.ds(0, 2 * CH)], pk_hbm), (vg.at[part], pv_hbm))):
+            stores.append(pltpu.make_async_copy(src, dst.at[part], store_sems.at[n, side]))
+            stores[-1].start()
     for copy in stores:
         copy.wait()
 
 
-def attend(mine, span_slot, slot_label, queries, d_out, kg, vg, unit):
+def attend(span_slot, queries, d_out, kg, vg, unit):
     vmem = pl.BlockSpec(memory_space=pltpu.VMEM)
     smem = pl.BlockSpec(memory_space=pltpu.SMEM)
     anyspace = pl.BlockSpec(memory_space=pl.ANY)
@@ -509,28 +573,31 @@
             jax.ShapeDtypeStruct((NCTX, 2 * CH, 2 * HD), blk),
             jax.ShapeDtypeStruct((NCTX, 2 * CH, 2 * HD), blk),
         ),
-        in_specs=[smem, smem, smem, anyspace, anyspace, anyspace, anyspace, vmem],
+        in_specs=[smem, anyspace, anyspace, anyspace, anyspace, vmem],
         out_specs=(vmem, vmem, anyspace, anyspace),
         scratch_shapes=[
             pltpu.VMEM(kg.shape, blk),
             pltpu.VMEM(vg.shape, blk),
             pltpu.VMEM((2, 16 * CH, HD), blk),
             pltpu.VMEM((2, 16 * CH, HD), blk),
-            pltpu.VMEM((31, 2 * CH, QB), jnp.float32),
-            pltpu.VMEM((31, 2 * CH, QB), jnp.float32),
-            pltpu.VMEM((32, 1, QB), jnp.float32),
-            pltpu.VMEM((8, QB), jnp.float32),
+            pltpu.VMEM((16, 1, HD), jnp.float32),
+            pltpu.VMEM((2, 8, QB), jnp.float32),
             pltpu.VMEM((NCTX, 2 * CH, 2 * HD), jnp.float32),
             pltpu.VMEM((NCTX, 2 * CH, 2 * HD), jnp.float32),
-            pltpu.VMEM((HD, QB), jnp.float32),
+            pltpu.VMEM((2, HD, QB), jnp.float32),
+            pltpu.VMEM((8, HD), jnp.int32),
+            pltpu.SMEM((8, HD), jnp.int32),
+            pltpu.SMEM((SPANS,), jnp.int32),
             pltpu.SMEM((SPANS + 8,), jnp.int32),
-            pltpu.SemaphoreType.DMA((2,)),
+            pltpu.SemaphoreType.DMA((1,)),
             pltpu.SemaphoreType.DMA((2, 32)),
+            pltpu.SemaphoreType.DMA((6, 2)),
+            pltpu.SemaphoreType.DMA((4, 2)),
         ],
-        compiler_params=pltpu.CompilerParams(vmem_limit_bytes=63 * MIB),
+        compiler_params=pltpu.CompilerParams(vmem_limit_bytes=VMEM_MIB * MIB),
         cost_estimate=pl.CostEstimate(flops=8 * 10**9, bytes_accessed=32 * 10**6, transcendentals=4 * 10**6),
         name="attend",
-    )(mine, span_slot, slot_label, queries, d_out, kg, vg, unit)
+    )(span_slot, queries, d_out, kg, vg, unit)
 
 
 def plus(a, b):
@@ -538,9 +605,9 @@
 
 
 class Scatter:
-    def __init__(self, first, parts, cross_in, near, full, near_b, full_b, send, recv):
+    def __init__(self, first, parts, own, cross_in, near, full, near_b, full_b, send, recv, own_sem):
         self.plane = Plane(first)
-        self.parts, self.cross_in = parts, cross_in
+        self.parts, self.own, self.cross_in, self.own_sem = parts, own, cross_in, own_sem
         self.near, self.full, self.near_b, self.full_b = near, full, near_b, full_b
         self.copies = Copies(send, recv)
 
@@ -552,10 +619,17 @@
             self.copies.start(
                 self.parts.at[self.plane.at(e, q, True)], self.cross_in.at[q, e], 4 * q + e, self.dev(0, 0, True)
             )
+            self.own_copy(q, e).start()
+
+    def own_copy(self, q, e):
+        return pltpu.make_async_copy(
+            self.parts.at[self.plane.at(e, q)], self.own.at[q, e], self.own_sem.at[4 * q + e]
+        )
 
     def add_cross(self, q, e):
         self.copies.landed(self.cross_in.at[q, e], 4 * q + e, self.dev(0, 0, True))
-        self.cross_in[q, e] = plus(self.cross_in[q, e], self.parts[self.plane.at(e, q)])
+        self.own_copy(q, e).wait()
+        self.cross_in[q, e] = plus(self.cross_in[q, e], self.own[q, e])
 
     def far(self, q):
         self.add_cross(q, 2)
@@ -605,26 +679,37 @@
 
 
 def scatter_kernel(
-    pk_ref, pv_ref, gk_ref, gv_ref,
-    k_cross, k_near, k_full, k_near_b, k_full_b,
-    v_cross, v_near, v_full, v_near_b, v_full_b,
-    k_send, k_recv, v_send, v_recv,
+    pk_ref, pv_ref, near_ref, relay_ref, gk_ref, gv_ref, mid_ref, far_ref,
+    k_own, k_cross, k_near, k_full, k_near_b, k_full_b,
+    v_own, v_cross, v_near, v_full, v_near_b, v_full_b,
+    k_send, k_recv, v_send, v_recv, w_send, w_recv, own_sems,
 ):
-    barrier_with(ctx_targets())
+    barrier_with(ctx_targets() + head_targets((1, 3)))
     ways = [
-        Scatter("y", pk_ref, k_cross, k_near, k_full, k_near_b, k_full_b, k_send, k_recv),
-        Scatter("x", pv_ref, v_cross, v_near, v_full, v_near_b, v_full_b, v_send, v_recv),
+        Scatter("y", pk_ref, k_own, k_cross, k_near, k_full, k_near_b, k_full_b, k_send, k_recv, own_sems.at[0]),
+        Scatter("x", pv_ref, v_own, v_cross, v_near, v_full, v_near_b, v_full_b, v_send, v_recv, own_sems.at[1]),
     ]
     order = (2, 1, 3, 0)
     for q in order:
         for way in ways:
             way.cross(q)
+    me_z = lax.axis_index("head")
+    piece = relay_ref.shape[2]
+    halves = [mid_ref.at[:, pl.ds(side * piece, piece)] for side in range(2)]
+    sibling = {"ctx": Plane("x").at(0, 0, True)}
+    moves = Copies(w_send, w_recv)
+    for side, step in enumerate((1, -1)):
+        moves.start(relay_ref.at[side], halves[side], side, {"head": turn(me_z, step, NZ)})
+        moves.start(near_ref.at[side], far_ref.at[2 * side], 2 + side, sibling)
     for q in order:
         for way in ways:
             way.far(q)
     for q in order:
         for way in ways:
             way.next(q)
+    for side, step in enumerate((1, -1)):
+        moves.landed(halves[side], side, {"head": turn(me_z, -step, NZ)})
+    moves.start(mid_ref, far_ref.at[1], 4, sibling)
     for way in ways:
         way.last_far()
     for way in ways:
@@ -633,14 +718,20 @@
         way.last_near(3)
     gk_ref[...] = (ways[0].finish() * SCALE).astype(jnp.bfloat16)
     gv_ref[...] = ways[1].finish().astype(jnp.bfloat16)
+    for side in range(2):
+        moves.landed(far_ref.at[2 * side], 2 + side, sibling)
+    moves.landed(far_ref.at[1], 4, sibling)
     for way in ways:
         way.copies.finish()
-
-
-def scatter_sums(pk, pv):
+    moves.finish()
+
+
+def scatter_sums(pk, pv, near, relay):
     vmem = pl.BlockSpec(memory_space=pltpu.VMEM)
+    hbm = pl.BlockSpec(memory_space=pl.ANY)
     blk = jnp.bfloat16
     one = [
+        pltpu.VMEM((4, 4, 2 * CH, 2 * HD), blk),
         pltpu.VMEM((4, 4, 2 * CH, 2 * HD), blk),
         pltpu.VMEM((4, 2, CH, 2 * HD), blk),
         pltpu.VMEM((4, 2, 2 * CH, 2 * HD), blk),
@@ -649,19 +740,23 @@
     ]
     return pl.pallas_call(
         scatter_kernel,
-        out_shape=(jax.ShapeDtypeStruct((2 * CH, 2 * HD), blk),) * 2,
-        in_specs=[vmem] * 2,
-        out_specs=(vmem,) * 2,
-        scratch_shapes=one + one + [pltpu.SemaphoreType.DMA((36,))] * 4,
+        out_shape=(jax.ShapeDtypeStruct((2 * CH, 2 * HD), blk),) * 2 + (
+            jax.ShapeDtypeStruct(near.shape[1:], blk),
+            jax.ShapeDtypeStruct((3,) + near.shape[1:], blk),
+        ),
+        in_specs=[hbm] * 4,
+        out_specs=(vmem,) * 2 + (hbm,) * 2,
+        scratch_shapes=one + one + [pltpu.SemaphoreType.DMA((36,))] * 4 + [pltpu.SemaphoreType.DMA((5,))] * 2
+        + [pltpu.SemaphoreType.DMA((2, 16))],
         compiler_params=pltpu.CompilerParams(
-            collective_id=1, has_side_effects=True, vmem_limit_bytes=40 * MIB
+            collective_id=1, has_side_effects=True, vmem_limit_bytes=VMEM_MIB * MIB
         ),
         name="scatter_dkv",
-    )(pk, pv)
+    )(pk, pv, near, relay)
 
 
 def project_kernel(
-    gk_ref, gv_ref, hdq_ref, wk_hbm, wv_hbm, r1, r2, r3, s1, s2, s3, gx_ref, hg_ref,
+    gk_ref, gv_ref, hdq_ref, wk_hbm, wv_hbm, near_ref, mid_ref, far_ref, gx_ref, hg_ref,
     grads, weights, total, half, g_send, g_recv, o_send, o_recv, h_send, h_recv, w_sem, own_sem,
 ):
     me_z = lax.axis_index("head")
@@ -697,7 +792,9 @@
     ]]
     mine_rows = pl.ds(pl.multiple_of(core * piece, piece), piece)
     other_rows = pl.ds(pl.multiple_of((1 - core) * piece, piece), piece)
-    for d, (near, far) in enumerate(((r1, s1), (r2, s2), (r3, s3)), start=1):
+    nears = (near_ref.at[0], mid_ref, near_ref.at[1])
+    for d, near in enumerate(nears, start=1):
+        far = far_ref.at[d - 1]
         fetches.append([
             pltpu.make_async_copy(near, weights.at[d, :, mine_rows], w_sem.at[2 * d]),
             pltpu.make_async_copy(far, weights.at[d, :, other_rows], w_sem.at[2 * d + 1]),
@@ -793,9 +890,9 @@
         copy.wait()
 
 
-def project(gk, gv, hdq, w_key, w_value, near, far):
+def project(gk, gv, hdq, w_key, w_value, near, mid, far):
     vmem = pl.BlockSpec(memory_space=pltpu.VMEM)
-    anyspace = pl.BlockSpec(memory_space=pl.ANY)
+    hbm = pl.BlockSpec(memory_space=pl.ANY)
     blk = jnp.bfloat16
     depth = w_key.shape[0]
     width = depth // NZ
@@ -805,7 +902,7 @@
             jax.ShapeDtypeStruct((2 * CH // NZ, depth), blk),
             jax.ShapeDtypeStruct((NY, NX, 2, CH, HD), blk),
         ),
-        in_specs=[vmem, vmem, vmem] + [anyspace] * 8,
+        in_specs=[vmem, vmem, vmem] + [hbm] * 5,
         out_specs=(vmem, vmem),
         scratch_shapes=[
             pltpu.VMEM((NZ, 2, 2 * CH, 2 * HD), blk),
@@ -822,35 +919,15 @@
             pltpu.SemaphoreType.DMA((5,)),
         ],
         compiler_params=pltpu.CompilerParams(
-            collective_id=2, has_side_effects=True, vmem_limit_bytes=40 * MIB
+            collective_id=2, has_side_effects=True, vmem_limit_bytes=VMEM_MIB * MIB
         ),
         name="project",
-    )(gk, gv, hdq, w_key, w_value, *near, *far)
+    )(gk, gv, hdq, w_key, w_value, near, mid, far)
 
 
 def per_device(queries, keys, values, d_out, w_key, w_value, pair_list, span_slot):
     me = lax.axis_index("ctx")
-    me_z = lax.axis_index("head")
-    core = lax.rem(me, 2)
-    depth = w_key.shape[0]
-    width = depth // NZ
-    piece = width // 2
-
-    near, far = [], []
-    for d in (1, 2, 3):
-        start = lax.rem(me_z + d, NZ) * width + core * piece
-        block = jnp.stack([
-            lax.dynamic_slice_in_dim(w_key, start, piece, 0),
-            lax.dynamic_slice_in_dim(w_value, start, piece, 0),
-        ])
-        got = lax.ppermute(block, "head", [(i, (i + d) % NZ) for i in range(NZ)])
-        near.append(got)
-        far.append(lax.ppermute(got, "ctx", [(i, i ^ 1) for i in range(NCTX)]))
-
     label_ids = jnp.arange(SPANS, dtype=jnp.int32)
-    slot_label = jnp.sum(
-        jnp.where(span_slot[None, :] == label_ids[:, None], label_ids[None, :], 0), axis=1, dtype=jnp.int32
-    )
     own_slots = 2 * me + jnp.arange(2, dtype=jnp.int32)
     own_labels = jnp.sum(
         jnp.where(span_slot[None, :] == own_slots[:, None], label_ids[None, :], 0), axis=1, dtype=jnp.int32
@@ -861,21 +938,10 @@
     )
     pair_rows = jnp.pad(pair_list.astype(jnp.bfloat16), ((0, 0), (0, keys.shape[1] - 2)))
     keys_pad = jnp.concatenate([keys, pair_rows], axis=0)
-    kg, vg, unit = gather_all(keys_pad, values, queries, d_out, select)
-    pairs = kg[:, 2 * CH:, :2].reshape(-1, 2).astype(jnp.int32)
-    mine = jnp.max(
-        jnp.where(
-            jnp.logical_and(
-                pairs[None, None, :, 0] == own_labels[:, None, None],
-                pairs[None, None, :, 1] == label_ids[None, :, None],
-            ),
-            1, 0,
-        ).astype(jnp.int32),
-        axis=2,
-    ).reshape(-1)
-    gq, hdq, pk, pv = attend(mine, span_slot, slot_label, queries, d_out, kg, vg, unit)
-    grad_k, grad_v = scatter_sums(pk, pv)
-    grad_x, units = project(grad_k, grad_v, hdq, w_key, w_value, near, far)
+    kg, vg, unit, near, relay = gather_all(keys_pad, values, queries, d_out, select, w_key, w_value)
+    gq, hdq, pk, pv = attend(span_slot, queries, d_out, kg, vg, unit)
+    grad_k, grad_v, mid, far = scatter_sums(pk, pv, near, relay)
+    grad_x, units = project(grad_k, grad_v, hdq, w_key, w_value, near, mid, far)
     heads = units.reshape(NX * NY, 2, CH, HD)
     rows = []
     for i in range(2):

time: 192 us -> 181 us (0.943)
  local copies, waits for them, and re-layouts: 14.7 us -> 4.96 us
  starting transfers between devices: 7.43 us -> 0 us
  Pallas kernels: 161 us -> 168 us
    unnamed x34 -> x12, local copies, waits for them, and re-layouts: 11.1 us -> 3.64 us
    pallas_call x1, Pallas kernels: 29.1 us -> 36.6 us  [project(): pl.pallas_call(project_kernel, out_shape=(jax.ShapeDtypeStruct((2 * CH //...]
    ppermute x6 -> x0, starting transfers between devices: 7.43 us -> none  [the longest x3 6.58 us: per_device(): got = lax.ppermute(block, 'head', [(i, (i + d) % NZ) for i in range(NZ)])]
    pallas_call x1, Pallas kernels: 39.5 us -> 45.6 us  [gather_all(): pl.pallas_call(gather_kernel, out_shape=(jax.ShapeDtypeStruct((NCTX,) + k...]
    pallas_call x1, Pallas kernels: 39.9 us -> 36.1 us  [scatter_sums(): pl.pallas_call(scatter_kernel, out_shape=(jax.ShapeDtypeStruct((2 * CH, 2...]
    pallas_call x1, Pallas kernels: 52.8 us -> 49.9 us  [attend(): pl.pallas_call(attend_kernel, out_shape=(jax.ShapeDtypeStruct((2 * CH, 16...]
    another operation x3 -> x0, other arithmetic: 2.22 us -> none  [per_device(): jnp.stack([lax.dynamic_slice_in_dim(w_key, start, piece, 0), lax.dynamic_...]
    another operation x1 -> x0, local copies, waits for them, and re-layouts: 2.05 us -> none  [per_device(): jnp.stack([lax.dynamic_slice_in_dim(w_key, start, piece, 0), lax.dynamic_...]
  transfers between devices with their start and end apart: 6 -> 0, of which waited for: 0 -> 0; matrix products, arithmetic and copies ran while one was open for 2% -> 0% of each run, Pallas kernels for 69% -> 0%
where the time goes in v2:
time: 181 us
  Pallas kernels  168 us (93%)
  local copies, waits for them, and re-layouts  4.96 us (3%)
  other arithmetic  4.49 us (2%)
  between operations  3.34 us (2%)
    pallas_call x1, Pallas kernels, attend(): pl.pallas_call(attend_kernel, out_shape=(jax.ShapeDtypeStruct((2 * CH, 16...  49.9 us
    pallas_call x1, Pallas kernels, gather_all(): pl.pallas_call(gather_kernel, out_shape=(jax.ShapeDtypeStruct((NCTX,) + k...  45.6 us
    pallas_call x1, Pallas kernels, project(): pl.pallas_call(project_kernel, out_shape=(jax.ShapeDtypeStruct((2 * CH //...  36.6 us
    pallas_call x1, Pallas kernels, scatter_sums(): pl.pallas_call(scatter_kernel, out_shape=(jax.ShapeDtypeStruct((2 * CH, 2...  36.1 us
    unnamed x12, local copies, waits for them, and re-layouts  3.64 us

profile of v2, /device:TPU:1, one launch (start us, length us, event | category | flops | bytes accessed | tf_op | source)
XLA Modules:
  0.0 181.0 jit_solution(7171759223196700743)
XLA Ops:
  0.6 0.8 fusion.2
  1.5 0.1 compare_convert_fusion
  1.6 0.6 broadcast_in_dim.24.sel_ref
  2.2 0.7 convert_element_type.13
  2.9 0.1 copy.23
  3.0 1.6 fusion.1.keys_ref
  4.6 45.6 %gather_kv.1 = (bf16[32,272,256]{2,1,0:T(8,128)(2,1)}, bf16[32,256,256]{2,1,0:T(8,128)(2,1)}, bf16[2,128,128]{2,1,0:T(8,128)(2,1)}, bf16[2,2,1024,256]{3,2,1,0:T(8,128)(2,1)}, bf16[2,2,512,256]{3,2,1,0:T(8,128)(2,1)}) custom-call(bf16[272,256]{1,0:T(8,128)(2,1)} %fusion.1.keys_ref, bf16[256,256]{1,0:T(8,128)(2,1)} %values_ref.1, bf16[256,2048]{1,0:T(8,128)(2,1)} %q_hbm.1, ...), custom_call_target="tpu_custom_call" | custom-call | tf_op jit(solution)/shard_map/gather_kv/pallas_call | solution.py:286
  50.2 49.9 %attend.1 = (bf16[256,2048]{1,0:T(8,128)(2,1)}, bf16[128,128]{1,0:T(8,128)(2,1)}, bf16[32,256,256]{2,1,0:T(8,128)(2,1)}, bf16[32,256,256]{2,1,0:T(8,128)(2,1)}) custom-call(s32[64]{0:T(128)} %span_slot.1, bf16[256,2048]{1,0:T(8,128)(2,1)} %q_hbm.1, bf16[256,2048]{1,0:T(8,128)(2,1)} %do_hbm.1, bf16[32,272,256]{2,1,0:T(8,128)(2,1)} %get-tuple-element.19.kg_hbm, ...), custom_call_target="tpu_custom_call" | custom-call | flops 8000000000 | bytes 32000000 | tf_op jit(solution)/shard_map/attend/pallas_call | solution.py:568
  100.1 36.1 %scatter_dkv.1 = (bf16[256,256]{1,0:T(8,128)(2,1)}, bf16[256,256]{1,0:T(8,128)(2,1)}, bf16[2,1024,256]{2,1,0:T(8,128)(2,1)}, bf16[3,2,1024,256]{3,2,1,0:T(8,128)(2,1)}) custom-call(bf16[32,256,256]{2,1,0:T(8,128)(2,1)} %get-tuple-element.22.pk_ref, bf16[32,256,256]{2,1,0:T(8,128)(2,1)} %get-tuple-element.23.pv_ref, ...), custom_call_target="tpu_custom_call" | custom-call | tf_op jit(solution)/shard_map/scatter_dkv/pallas_call | solution.py:741
  136.2 0.0 copy-start
  136.3 36.6 %project.1 = (bf16[64,8192]{1,0:T(8,128)(2,1)}, bf16[4,4,2,128,128]{4,3,2,1,0:T(8,128)(2,1)}) custom-call(bf16[256,256]{1,0:T(8,128)(2,1)} %get-tuple-element.45.gk_ref, bf16[256,256]{1,0:T(8,128)(2,1)} %get-tuple-element.46.gv_ref, bf16[128,128]{1,0:T(8,128)(2,1)} %get-tuple-element.28.hdq_ref, bf16[8192,256]{1,0:T(8,128)(2,1)} %wk_hbm.3, ...), custom_call_target="tpu_custom_call" | custom-call | tf_op jit(solution)/shard_map/project/pallas_call | solution.py:899
  172.8 0.0 copy-start.3
  172.8 0.0 copy-start.2
  172.8 0.0 copy-start.1
  172.8 0.6 fusion.3
  174.7 1.3 dynamic-slice_bitcast_fusion.1
  177.4 0.0 copy-done
  177.4 0.2 bitcast_select_fusion.1
  177.6 1.1 pad_maximum_fusion
  178.7 0.0 copy-done.3
  178.7 0.7 copy.37
  179.4 0.0 copy-done.2
  179.4 0.7 copy.38
  180.0 0.0 copy-done.1
  180.0 1.0 copy.39
  (2 shorter events, 0.0 us)
Async XLA Ops:
  136.2 41.2 %copy-start = (bf16[256,2048]{1,0:T(8,128)(2,1)S(1)}, bf16[256,2048]{1,0:T(8,128)(2,1)}, u32[]{:S(2)}) copy-start(bf16[256,2048]{1,0:T(8,128)(2,1)} %get-tuple-element.32) | copy-start | bytes 3145732
  172.8 5.9 %copy-start.3 = (bf16[256,256]{1,0:T(8,128)(2,1)S(1)}, bf16[256,256]{1,0:T(8,128)(2,1)}, u32[]{:S(2)}) copy-start(bf16[256,256]{1,0:T(8,128)(2,1)} %get-tuple-element.45.gk_ref) | copy-start | bytes 393220
  172.8 6.6 %copy-start.2 = (bf16[256,256]{1,0:T(8,128)(2,1)S(1)}, bf16[256,256]{1,0:T(8,128)(2,1)}, u32[]{:S(2)}) copy-start(bf16[256,256]{1,0:T(8,128)(2,1)} %get-tuple-element.46.gv_ref) | copy-start | bytes 393220
  172.8 7.2 %copy-start.1 = (bf16[64,8192]{1,0:T(8,128)(2,1)S(1)}, bf16[64,8192]{1,0:T(8,128)(2,1)}, u32[]{:S(2)}) copy-start(bf16[64,8192]{1,0:T(8,128)(2,1)} %get-tuple-element.47) | copy-start | bytes 3145732

commit v3 on v2

v3 whole, which is shorter than its diff:
```python
import functools

import jax
import jax.numpy as jnp
from jax import lax
from jax.experimental import pallas as pl
from jax.experimental.pallas import tpu as pltpu
from jax.sharding import PartitionSpec as P

MESH = pl.DeviceIdType.MESH
HD = 128
CH = 128
SPANS = 64
NX = 4
NY = 4
NZ = 4
NCTX = NX * NY * 2
CHIPS = NX * NY
GROUP = 8
NPAD = 16
SCALE = HD ** -0.5
EXP_SCALE = SCALE * 1.4426950408889634
neg_fill = -1e30
QB = 1024
MIB = 1024 * 1024
VMEM_MIB = 62


def ctx_coords():
    me = lax.axis_index("ctx")
    return me // (2 * NX), lax.rem(me // 2, NX), lax.rem(me, 2)


def ctx_id(y, x, core):
    return (y * NX + x) * 2 + core


def turn(pos, step, size):
    return lax.rem(pos + step + size, size)


class Plane:
    def __init__(self, first):
        self.y, self.x, self.core = ctx_coords()
        self.first = first

    def at(self, da, db, flip=False):
        dy, dx = (da, db) if self.first == "y" else (db, da)
        core = 1 - self.core if flip else self.core
        return ctx_id(turn(self.y, dy, NY), turn(self.x, dx, NX), core)

    def chip(self, da, db):
        dy, dx = (da, db) if self.first == "y" else (db, da)
        return turn(self.y, dy, NY) * NX + turn(self.x, dx, NX)


def barrier_with(targets):
    barrier = pltpu.get_barrier_semaphore()
    for device in targets:
        pl.semaphore_signal(barrier, inc=1, device_id=device, device_id_type=MESH)
    pl.semaphore_wait(barrier, len(targets))


def ctx_targets():
    plane = Plane("x")
    steps = [(1, 0), (2, 0), (3, 0), (0, 1), (0, 2), (0, 3)]
    return [{"ctx": plane.at(da, db)} for da, db in steps] + [{"ctx": plane.at(0, 0, True)}]


def head_targets(steps):
    me_z = lax.axis_index("head")
    return [{"head": turn(me_z, d, NZ)} for d in steps]


class Copies:
    def __init__(self, send, recv):
        self.send, self.recv, self.started = send, recv, []

    def start(self, src, dst, index, device):
        copy = pltpu.make_async_remote_copy(
            src_ref=src, dst_ref=dst, send_sem=self.send.at[index], recv_sem=self.recv.at[index],
            device_id=device, device_id_type=MESH,
        )
        copy.start()
        self.started.append(copy)

    def landed(self, dst, index, device):
        pltpu.make_async_remote_copy(
            src_ref=dst, dst_ref=dst, send_sem=self.send.at[index], recv_sem=self.recv.at[index],
            device_id=device, device_id_type=MESH,
        ).wait_recv()

    def finish(self):
        for copy in self.started:
            copy.wait_send()


DA_OF = (0, -1, 1, 2)


class Gather:
    def __init__(self, first, out, send, recv):
        self.plane = Plane(first)
        self.out = out
        self.copies = Copies(send, recv)

    def dev(self, da, db):
        return {"ctx": self.plane.at(da, db)}

    def region(self, da, db):
        return self.out.at[self.plane.chip(da, db)]

    def send(self, region, index, da, db):
        self.copies.start(region, region, index, self.dev(da, db))

    def begin_a(self):
        self.send(self.region(0, 0), 0, 1, 0)
        self.send(self.region(0, 0), 1, -1, 0)

    def spread(self, m):
        region = self.region(DA_OF[m], 0)
        self.send(region, 4 + 4 * m, 0, 1)
        self.send(region, 5 + 4 * m, 0, -1)

    def got_a(self, step):
        index = 0 if step < 0 else 1
        region = self.region(step, 0)
        self.copies.landed(region, index, self.dev(step, 0))
        self.send(region.at[index], 2 + index, -step, 0)

    def got_a_far(self):
        region = self.region(2, 0)
        self.copies.landed(region.at[0], 2, self.dev(-1, 0))
        self.copies.landed(region.at[1], 3, self.dev(1, 0))

    def got_b(self, m, step):
        index = 0 if step < 0 else 1
        region = self.region(DA_OF[m], step)
        self.copies.landed(region, 4 + 4 * m + index, self.dev(0, step))
        self.send(region.at[index], 6 + 4 * m + index, 0, -step)

    def got_b_far(self, m):
        region = self.region(DA_OF[m], 2)
        self.copies.landed(region.at[0], 6 + 4 * m, self.dev(0, -1))
        self.copies.landed(region.at[1], 7 + 4 * m, self.dev(0, 1))


def gather_kernel(
    keys_ref, values_ref, q_ref, do_ref, sel_ref, wk_hbm, wv_hbm,
    kg_ref, vg_ref, unit_ref, qx_ref, dox_ref, near_ref,
    give, held, from_core, first_in, mid, last_in,
    k_send, k_recv, v_send, v_recv, u_send, u_recv, w_send, w_recv, c_send, c_recv, own_sem,
):
    barrier_with(ctx_targets() + head_targets((1, 3)))
    y, x, core = ctx_coords()
    plane = Plane("x")
    chip = plane.chip(0, 0)
    sibling = {"ctx": plane.at(0, 0, True)}
    gathers = [
        Gather("x", kg_ref, k_send, k_recv),
        Gather("y", vg_ref, v_send, v_recv),
    ]

    def group_cols(which, width):
        return pl.ds(pl.multiple_of(which * width, width), width)

    cross = Copies(c_send, c_recv)
    other = group_cols(1 - core, HD)
    cross.start(keys_ref.at[:, other], kg_ref.at[chip, core], 0, sibling)
    cross.start(values_ref.at[:, other], vg_ref.at[chip, core], 1, sibling)
    mine = group_cols(core, HD)
    own_copies = [
        pltpu.make_async_copy(keys_ref.at[:, mine], kg_ref.at[chip, core], own_sem.at[0]),
        pltpu.make_async_copy(values_ref.at[:, mine], vg_ref.at[chip, core], own_sem.at[1]),
    ]
    for copy in own_copies:
        copy.start()

    def pick(dst, group):
        def unit(j, carry):
            cols = pl.ds(pl.multiple_of((group * GROUP + lax.rem(j, GROUP)) * HD, HD), HD)
            first = sel_ref[j // GROUP, 0:1, :]
            second = sel_ref[j // GROUP, 1:2, :]
            for n, ref in enumerate((q_ref, do_ref)):
                dst[n, j // NX, lax.rem(j, NX)] = ref[0:CH, cols] * first + ref[CH:2 * CH, cols] * second
            return carry

        lax.fori_loop(0, CHIPS, unit, 0)

    units = Copies(u_send, u_recv)
    pick(give, 1 - core)
    units.start(give, from_core, 0, sibling)

    for copy in own_copies:
        copy.wait()
    cross.landed(kg_ref.at[chip, 1 - core], 0, sibling)
    cross.landed(vg_ref.at[chip, 1 - core], 1, sibling)
    for gather in gathers:
        gather.begin_a()
    for gather in gathers:
        gather.spread(0)

    me_z = lax.axis_index("head")
    piece = near_ref.shape[2]
    moves = Copies(w_send, w_recv)
    for n, ref in enumerate((wk_hbm, wv_hbm)):
        for side, step in enumerate((1, -1)):
            to = turn(me_z, step, NZ)
            start = pl.multiple_of((2 * to + core) * piece, piece)
            moves.start(ref.at[pl.ds(start, piece)], near_ref.at[side, n], 2 * side + n, {"head": to})

    qcols = group_cols(1 - core, GROUP * HD)
    cross.start(q_ref.at[:, qcols], qx_ref, 2, sibling)
    cross.start(do_ref.at[:, qcols], dox_ref, 3, sibling)

    pick(held, core)
    units.landed(from_core, 0, sibling)

    def add_core(j, carry):
        for n in range(2):
            held[n, j // NX, lax.rem(j, NX)] += from_core[n, j // NX, lax.rem(j, NX)]
        return carry

    lax.fori_loop(0, CHIPS, add_core, 0)
    for d in (1, 2, 3):
        far_x, far_y = turn(x, d, NX), turn(y, d, NY)
        units.start(held.at[0, :, far_x], first_in.at[0, d - 1], d, {"ctx": plane.at(d, 0)})
        units.start(held.at[1, far_y], first_in.at[1, d - 1], 3 + d, {"ctx": plane.at(0, d)})

    for gather in gathers:
        gather.got_a(-1)
        gather.got_a(1)
    for gather in gathers:
        gather.spread(1)
        gather.spread(2)
    for gather in gathers:
        gather.got_b(0, -1)
        gather.got_b(0, 1)
    for gather in gathers:
        gather.got_a_far()
        gather.spread(3)

    for d in (1, 2, 3):
        units.landed(first_in.at[0, d - 1], d, {"ctx": plane.at(-d, 0)})
        units.landed(first_in.at[1, d - 1], 3 + d, {"ctx": plane.at(0, -d)})
    for n in range(4):
        mid[0, n] = held[0, n, x] + first_in[0, 0, n] + first_in[0, 1, n] + first_in[0, 2, n]
        mid[1, n] = held[1, y, n] + first_in[1, 0, n] + first_in[1, 1, n] + first_in[1, 2, n]
    for d in (1, 2, 3):
        units.start(mid.at[0, turn(y, d, NY)], last_in.at[0, d - 1], 6 + d, {"ctx": plane.at(0, d)})
        units.start(mid.at[1, turn(x, d, NX)], last_in.at[1, d - 1], 9 + d, {"ctx": plane.at(d, 0)})

    for m in (1, 2, 3):
        for gather in gathers:
            gather.got_b(m, -1)
            gather.got_b(m, 1)

    for d in (1, 2, 3):
        units.landed(last_in.at[0, d - 1], 6 + d, {"ctx": plane.at(0, -d)})
        units.landed(last_in.at[1, d - 1], 9 + d, {"ctx": plane.at(-d, 0)})
    unit_ref[0] = mid[0, y] + last_in[0, 0] + last_in[0, 1] + last_in[0, 2]
    unit_ref[1] = mid[1, x] + last_in[1, 0] + last_in[1, 1] + last_in[1, 2]

    cross.landed(qx_ref, 2, sibling)
    cross.landed(dox_ref, 3, sibling)
    for n in range(2):
        for side, step in enumerate((1, -1)):
            moves.landed(near_ref.at[side, n], 2 * side + n, {"head": turn(me_z, -step, NZ)})
    for m in range(4):
        for gather in gathers:
            gather.got_b_far(m)
    for gather in gathers:
        gather.copies.finish()
    cross.finish()
    units.finish()
    moves.finish()


def gather_all(keys_pad, values, queries, d_out, select, w_key, w_value):
    vmem = pl.BlockSpec(memory_space=pltpu.VMEM)
    anyspace = pl.BlockSpec(memory_space=pl.ANY)
    blk = jnp.bfloat16
    piece = w_key.shape[0] // NZ // 2
    return pl.pallas_call(
        gather_kernel,
        out_shape=(
            jax.ShapeDtypeStruct((CHIPS, 2, keys_pad.shape[0], HD), blk),
            jax.ShapeDtypeStruct((CHIPS, 2, values.shape[0], HD), blk),
            jax.ShapeDtypeStruct((2, CH, HD), blk),
            jax.ShapeDtypeStruct((2 * CH, GROUP * HD), blk),
            jax.ShapeDtypeStruct((2 * CH, GROUP * HD), blk),
            jax.ShapeDtypeStruct((2, 2, piece) + w_key.shape[1:], blk),
        ),
        in_specs=[vmem] * 5 + [anyspace] * 2,
        out_specs=(anyspace, anyspace, vmem, anyspace, anyspace, anyspace),
        scratch_shapes=[
            pltpu.VMEM((2, NY, NX, CH, HD), blk),
            pltpu.VMEM((2, NY, NX, CH, HD), blk),
            pltpu.VMEM((2, NY, NX, CH, HD), blk),
            pltpu.VMEM((2, 3, 4, CH, HD), blk),
            pltpu.VMEM((2, 4, CH, HD), blk),
            pltpu.VMEM((2, 3, CH, HD), blk),
            pltpu.SemaphoreType.DMA((20,)),
            pltpu.SemaphoreType.DMA((20,)),
            pltpu.SemaphoreType.DMA((20,)),
            pltpu.SemaphoreType.DMA((20,)),
            pltpu.SemaphoreType.DMA((13,)),
            pltpu.SemaphoreType.DMA((13,)),
            pltpu.SemaphoreType.DMA((4,)),
            pltpu.SemaphoreType.DMA((4,)),
            pltpu.SemaphoreType.DMA((4,)),
            pltpu.SemaphoreType.DMA((4,)),
            pltpu.SemaphoreType.DMA((2,)),
        ],
        compiler_params=pltpu.CompilerParams(
            collective_id=0, has_side_effects=True, vmem_limit_bytes=VMEM_MIB * MIB
        ),
        name="gather_kv",
    )(keys_pad, values, queries, d_out, select, w_key, w_value)


def dot_nt(a, b):
    return lax.dot_general(a, b, (((1,), (1,)), ((), ())), preferred_element_type=jnp.float32)


def dot_nn(a, b):
    return lax.dot_general(a, b, (((1,), (0,)), ((), ())), preferred_element_type=jnp.float32)


def dot_tn(a, b):
    return lax.dot_general(a, b, (((0,), (0,)), ((), ())), preferred_element_type=jnp.float32)


def attend_kernel(
    span_slot, q_hbm, do_hbm, qx_hbm, dox_hbm, kg_hbm, vg_hbm, unit_ref,
    gq_ref, gqx_ref, hdq_ref, pk_hbm, pv_hbm,
    kg, vg, qs, ds, gq_all, probs, dprob, tops, stat, acck, accv, dqt, found, flags, slot_label, todo,
    flag_sem, qsems, load_sems, store_sems,
):
    me = lax.axis_index("ctx")
    core = lax.rem(me, 2)
    unit = me // 2
    quarter = NCTX // 4
    pair_copy = pltpu.make_async_copy(
        kg_hbm.at[:, pl.ds(2 * CH, NPAD)], kg.at[:, pl.ds(2 * CH, NPAD)], load_sems.at[4, 0]
    )
    pair_copy.start()
    loads = []
    for n in range(4):
        part = pl.ds(n * quarter, quarter)
        for side, (src, dst) in enumerate(((kg_hbm, kg), (vg_hbm, vg))):
            at = (part, pl.ds(0, 2 * CH))
            loads.append(pltpu.make_async_copy(src.at[at], dst.at[at], load_sems.at[n, side]))
            loads[-1].start()
    stacks = []
    for u in range(4):
        for r in range(GROUP):
            rows = pl.ds((u % 2) * CH, CH)
            own_cols = pl.ds(pl.multiple_of((core * GROUP + r) * HD, HD), HD)
            for n, (own, other, dst) in enumerate(((q_hbm, qx_hbm, qs), (do_hbm, dox_hbm, ds))):
                src = own.at[rows, own_cols] if u < 2 else other.at[rows, pl.ds(r * HD, HD)]
                stacks.append(pltpu.make_async_copy(src, dst.at[u, pl.ds(r * CH, CH)], qsems.at[n, u * GROUP + r]))
    for copy in stacks:
        copy.start()

    def name_slot(c, carry):
        slot_label[span_slot[c]] = c
        return carry

    lax.fori_loop(0, SPANS, name_slot, 0)

    def slot_of(u):
        return 2 * (2 * unit + lax.rem(core + u // 2, 2)) + lax.rem(u, 2)

    pair_copy.wait()
    pair_rows = kg[:, 2 * CH:2 * CH + NPAD, :].reshape(NCTX * NPAD, HD).astype(jnp.float32)
    lanes = lax.broadcasted_iota(jnp.int32, (1, HD), 1).astype(jnp.float32)
    for u in range(4):
        own = slot_label[slot_of(u)].astype(jnp.float32)
        hit = jnp.logical_and(pair_rows[:, 0:1] == own, pair_rows[:, 1:2] == lanes)
        found[u:u + 1, :] = jnp.max(jnp.where(hit, 1.0, 0.0), axis=0, keepdims=True).astype(jnp.int32)
    flag_copy = pltpu.make_async_copy(found, flags, flag_sem.at[0])
    flag_copy.start()

    label = SPANS - 2 + unit // GROUP
    q_unit = unit_ref[0]
    do_unit = unit_ref[1]

    def four(ref, t):
        return jnp.concatenate([ref[2 * t, 0:2 * CH, :], ref[2 * t + 1, 0:2 * CH, :]], axis=0)

    def unit_first(t, carry):
        top, total, mix = carry
        scores = dot_nt(four(kg, t), q_unit) * EXP_SCALE
        mixed = dot_nt(four(vg, t), do_unit)
        diff = lax.broadcasted_iota(jnp.int32, (CH, HD), 0) - lax.broadcasted_iota(jnp.int32, (CH, HD), 1)
        scores = jnp.concatenate([
            jnp.where(diff <= (label - slot_label[4 * t + u]) * CH, scores[u * CH:(u + 1) * CH], neg_fill)
            for u in range(4)
        ], axis=0)
        new_top = jnp.maximum(top, jnp.max(scores, axis=0, keepdims=True))
        weights = jnp.exp2(scores - new_top)
        factor = jnp.exp2(top - new_top)
        probs[t] = weights
        dprob[t] = mixed
        tops[t] = new_top
        return (
            new_top,
            total * factor + jnp.sum(weights, axis=0, keepdims=True),
            mix * factor + jnp.sum(weights * mixed, axis=0, keepdims=True),
        )

    zero_row = jnp.zeros((1, HD), jnp.float32)
    state = (jnp.full((1, HD), neg_fill, jnp.float32), zero_row, zero_row)
    for n in range(4):
        for copy in loads[2 * n:2 * n + 2]:
            copy.wait()
        state = lax.fori_loop(n * quarter // 2, (n + 1) * quarter // 2, unit_first, state)
    top, total, mix = state
    over = 1.0 / total
    delta = mix * over

    def unit_second(t, acc):
        factor = jnp.exp2(tops[t] - top) * over
        weights = probs[t] * factor
        dscore = (weights * (dprob[t] - delta)).astype(jnp.bfloat16)
        value_part = dot_nn(weights.astype(jnp.bfloat16), do_unit)
        key_part = dot_nn(dscore, q_unit)
        for u in range(2):
            accv[2 * t + u] = value_part[2 * u * CH:2 * (u + 1) * CH]
            acck[2 * t + u] = key_part[2 * u * CH:2 * (u + 1) * CH]
        return acc + dot_tn(four(kg, t), dscore)

    acc = lax.fori_loop(0, NCTX // 2, unit_second, jnp.zeros((HD, CH), jnp.float32))
    hdq_ref[...] = (acc * SCALE).T.astype(jnp.bfloat16)

    flag_copy.wait()
    for copy in stacks:
        copy.wait()

    def span_work(u, carry):
        own_slot = slot_of(u)
        own_label = slot_label[own_slot]

        @pl.when(own_label < SPANS - 2)
        def _():
            todo[0] = own_slot

            def note(c, n):
                todo[n] = span_slot[c]
                wanted = jnp.logical_and(flags[u, c] > 0, c != own_label)
                return n + wanted.astype(jnp.int32)

            count = lax.fori_loop(0, SPANS, note, jnp.int32(1))
            todo[count] = own_slot

            def rows_at(slot):
                return pl.ds(pl.multiple_of(lax.rem(slot, 2) * CH, CH), CH)

            def both(ref, t):
                a, b = todo[2 * t], todo[2 * t + 1]
                return jnp.concatenate([ref[a // 2, rows_at(a), :], ref[b // 2, rows_at(b), :]], axis=0)

            limits = (0, jnp.where(count >= 2, CH, -CH))
            tail = (CH, -CH)
            odd = jnp.logical_and(lax.rem(count, 2) == 1, count > 1)

            def dots(t, limits):
                scores = dot_nt(both(kg, t), qs[u]) * EXP_SCALE
                if limits is not None:
                    diff = lax.broadcasted_iota(jnp.int32, (CH, QB), 0) - lax.rem(
                        lax.broadcasted_iota(jnp.int32, (CH, QB), 1), CH
                    )
                    scores = jnp.concatenate([
                        jnp.where(diff <= limits[v], scores[v * CH:(v + 1) * CH], neg_fill) for v in range(2)
                    ], axis=0)
                return scores, dot_nt(both(vg, t), ds[u])

            def first(t, limits=None):
                scores, mixed = dots(t, limits)
                old_top = stat[0:1, :]
                new_top = jnp.maximum(old_top, jnp.max(scores, axis=0, keepdims=True))
                weights = jnp.exp2(scores - new_top)
                factor = jnp.exp2(old_top - new_top)
                stat[0:1, :] = new_top
                stat[1:2, :] = stat[1:2, :] * factor + jnp.sum(weights, axis=0, keepdims=True)
                stat[2:3, :] = stat[2:3, :] * factor + jnp.sum(weights * mixed, axis=0, keepdims=True)

            def second(t, limits=None):
                scores, mixed = dots(t, limits)
                weights = jnp.exp2(scores - stat[3:4, :])
                dscore = (weights * (mixed - stat[4:5, :])).astype(jnp.bfloat16)
                value_part = dot_nn(weights.astype(jnp.bfloat16), ds[u])
                key_part = dot_nn(dscore, qs[u])
                for v in range(2):
                    slot = todo[2 * t + v]
                    accv[slot // 2, rows_at(slot), :] += value_part[v * CH:(v + 1) * CH]
                    acck[slot // 2, rows_at(slot), :] += key_part[v * CH:(v + 1) * CH]
                dqt[...] += dot_tn(both(kg, t), dscore)

            def sweep(work):
                work(0, limits)

                def plain(t, c):
                    work(t)
                    return c

                lax.fori_loop(1, count // 2, plain, 0)

                @pl.when(odd)
                def _():
                    work(count // 2, tail)

            stat[0:1, :] = jnp.full((1, QB), neg_fill, jnp.float32)
            stat[1:3, :] = jnp.zeros((2, QB), jnp.float32)
            sweep(first)
            total_row = stat[1:2, :]
            stat[3:4, :] = stat[0:1, :] + jnp.log2(total_row)
            stat[4:5, :] = stat[2:3, :] / total_row
            dqt[...] = jnp.zeros_like(dqt)
            sweep(second)
            for r in range(GROUP):
                gq_all[pl.ds(pl.multiple_of(u * CH, CH), CH), r * HD:(r + 1) * HD] = (
                    (dqt[:, r * CH:(r + 1) * CH] * SCALE).T.astype(jnp.bfloat16)
                )

        return carry

    lax.fori_loop(0, 4, span_work, 0)

    stores = [
        pltpu.make_async_copy(gq_all.at[pl.ds(0, 2 * CH)], gq_ref, store_sems.at[4, 0]),
        pltpu.make_async_copy(gq_all.at[pl.ds(2 * CH, 2 * CH)], gqx_ref, store_sems.at[4, 1]),
    ]
    for copy in stores:
        copy.start()
    for n in range(4):
        part = pl.ds(n * quarter, quarter)

        def narrow(t, carry):
            kg[t, 0:2 * CH, :] = acck[t].astype(jnp.bfloat16)
            vg[t] = accv[t].astype(jnp.bfloat16)
            return carry

        lax.fori_loop(n * quarter, (n + 1) * quarter, narrow, 0)
        for side, (src, dst) in enumerate(((kg.at[part, pl.ds(0, 2 * CH)], pk_hbm), (vg.at[part], pv_hbm))):
            stores.append(pltpu.make_async_copy(src, dst.at[part], store_sems.at[n, side]))
            stores[-1].start()
    for copy in stores:
        copy.wait()


def attend(span_slot, queries, d_out, qx, dox, kg, vg, unit):
    vmem = pl.BlockSpec(memory_space=pltpu.VMEM)
    smem = pl.BlockSpec(memory_space=pltpu.SMEM)
    anyspace = pl.BlockSpec(memory_space=pl.ANY)
    blk = jnp.bfloat16
    return pl.pallas_call(
        attend_kernel,
        out_shape=(
            jax.ShapeDtypeStruct((2 * CH, GROUP * HD), blk),
            jax.ShapeDtypeStruct((2 * CH, GROUP * HD), blk),
            jax.ShapeDtypeStruct((CH, HD), blk),
            jax.ShapeDtypeStruct((NCTX, 2 * CH, HD), blk),
            jax.ShapeDtypeStruct((NCTX, 2 * CH, HD), blk),
        ),
        in_specs=[smem] + [anyspace] * 6 + [vmem],
        out_specs=(anyspace, anyspace, vmem, anyspace, anyspace),
        scratch_shapes=[
            pltpu.VMEM(kg.shape, blk),
            pltpu.VMEM(vg.shape, blk),
            pltpu.VMEM((4, GROUP * CH, HD), blk),
            pltpu.VMEM((4, GROUP * CH, HD), blk),
            pltpu.VMEM((4 * CH, GROUP * HD), blk),
            pltpu.VMEM((NCTX // 2, 4 * CH, HD), jnp.float32),
            pltpu.VMEM((NCTX // 2, 4 * CH, HD), jnp.float32),
            pltpu.VMEM((NCTX // 2, 1, HD), jnp.float32),
            pltpu.VMEM((8, QB), jnp.float32),
            pltpu.VMEM((NCTX, 2 * CH, HD), jnp.float32),
            pltpu.VMEM((NCTX, 2 * CH, HD), jnp.float32),
            pltpu.VMEM((HD, QB), jnp.float32),
            pltpu.VMEM((8, HD), jnp.int32),
            pltpu.SMEM((8, HD), jnp.int32),
            pltpu.SMEM((SPANS,), jnp.int32),
            pltpu.SMEM((SPANS + 8,), jnp.int32),
            pltpu.SemaphoreType.DMA((1,)),
            pltpu.SemaphoreType.DMA((2, 32)),
            pltpu.SemaphoreType.DMA((5, 2)),
            pltpu.SemaphoreType.DMA((5, 2)),
        ],
        compiler_params=pltpu.CompilerParams(vmem_limit_bytes=VMEM_MIB * MIB),
        cost_estimate=pl.CostEstimate(flops=8 * 10**9, bytes_accessed=32 * 10**6, transcendentals=4 * 10**6),
        name="attend",
    )(span_slot, queries, d_out, qx, dox, kg, vg, unit)


def plus(a, b):
    return (a.astype(jnp.float32) + b.astype(jnp.float32)).astype(jnp.bfloat16)


class Scatter:
    def __init__(self, first, parts, own, near, full, near_b, full_b, send, recv, own_sem):
        self.plane = Plane(first)
        self.parts, self.own, self.own_sem = parts, own, own_sem
        self.near, self.full, self.near_b, self.full_b = near, full, near_b, full_b
        self.copies = Copies(send, recv)

    def dev(self, da, db):
        return {"ctx": self.plane.at(da, db)}

    def load(self, q, e):
        return pltpu.make_async_copy(self.parts.at[self.plane.chip(e, q)], self.own.at[q, e], self.own_sem.at[4 * q + e])

    def far(self, q):
        block = self.parts.at[self.plane.chip(2, q)]
        self.copies.start(block.at[0], self.near.at[q, 0], 4 * q, self.dev(1, 0))
        self.copies.start(block.at[1], self.near.at[q, 1], 4 * q + 1, self.dev(-1, 0))

    def next(self, q):
        for side, step in enumerate((1, -1)):
            e = step % 4
            self.load(q, e).wait()
            self.copies.landed(self.near.at[q, side], 4 * q + side, self.dev(-step, 0))
            self.own[q, e, side] = plus(self.own[q, e, side], self.near[q, side])
            self.copies.start(self.own.at[q, e], self.full.at[q, side], 4 * q + 2 + side, self.dev(step, 0))

    def last(self, q):
        self.load(q, 0).wait()
        self.copies.landed(self.full.at[q, 0], 4 * q + 2, self.dev(-1, 0))
        self.copies.landed(self.full.at[q, 1], 4 * q + 3, self.dev(1, 0))
        return (
            self.own[q, 0].astype(jnp.float32)
            + self.full[q, 0].astype(jnp.float32)
            + self.full[q, 1].astype(jnp.float32)
        )

    def last_far(self):
        self.own[2, 0] = self.last(2).astype(jnp.bfloat16)
        for side, step in enumerate((1, -1)):
            self.copies.start(self.own.at[2, 0, side], self.near_b.at[side], 16 + side, self.dev(0, step))

    def last_near(self, side):
        step = (1, -1)[side]
        q = step % 4
        total = self.last(q)
        self.copies.landed(self.near_b.at[side], 16 + side, self.dev(0, -step))
        self.own[q, 0, 1 - side] = total[1 - side].astype(jnp.bfloat16)
        self.own[q, 0, side] = (total[side] + self.near_b[side].astype(jnp.float32)).astype(jnp.bfloat16)
        self.copies.start(self.own.at[q, 0], self.full_b.at[side], 18 + side, self.dev(0, step))

    def finish(self):
        total = self.last(0)
        self.copies.landed(self.full_b.at[0], 18, self.dev(0, -1))
        self.copies.landed(self.full_b.at[1], 19, self.dev(0, 1))
        return total + self.full_b[0].astype(jnp.float32) + self.full_b[1].astype(jnp.float32)


def scatter_kernel(
    pk_ref, pv_ref, near_ref, gqx_ref, wk_hbm, wv_hbm, gk_ref, gv_ref, gqo_ref, mid_ref, far_ref,
    k_own, k_near, k_full, k_near_b, k_full_b,
    v_own, v_near, v_full, v_near_b, v_full_b, sums, swap, swap_in,
    k_send, k_recv, v_send, v_recv, w_send, w_recv, c_send, c_recv, own_sems,
):
    barrier_with(ctx_targets() + head_targets((1, 2, 3)))
    core = lax.rem(lax.axis_index("ctx"), 2)
    sibling = {"ctx": Plane("x").at(0, 0, True)}
    ways = [
        Scatter("y", pk_ref, k_own, k_near, k_full, k_near_b, k_full_b, k_send, k_recv, own_sems.at[0]),
        Scatter("x", pv_ref, v_own, v_near, v_full, v_near_b, v_full_b, v_send, v_recv, own_sems.at[1]),
    ]
    order = (2, 1, 3, 0)
    for q in order:
        for way in ways:
            way.far(q)
    for e in (1, 3, 0):
        for q in order:
            for way in ways:
                way.load(q, e).start()

    me_z = lax.axis_index("head")
    piece = mid_ref.shape[1]
    moves = Copies(w_send, w_recv)
    two = turn(me_z, 2, NZ)
    start = pl.multiple_of((2 * two + core) * piece, piece)
    for n, ref in enumerate((wk_hbm, wv_hbm)):
        moves.start(ref.at[pl.ds(start, piece)], mid_ref.at[n], n, {"head": two})
    cross = Copies(c_send, c_recv)
    cross.start(gqx_ref, gqo_ref, 0, sibling)
    for side in range(2):
        cross.start(near_ref.at[side], far_ref.at[2 * side], 1 + side, sibling)

    for q in order:
        for way in ways:
            way.next(q)
    for way in ways:
        way.last_far()
    for side in range(2):
        for way in ways:
            way.last_near(side)
    cross.landed(gqo_ref, 0, sibling)
    for side in range(2):
        cross.landed(far_ref.at[2 * side], 1 + side, sibling)
    for n, (way, factor) in enumerate(zip(ways, (SCALE, 1.0))):
        sums[...] = way.finish() * factor
        swap[n] = sums[1 - core].astype(jnp.bfloat16)
        cross.start(swap.at[n], swap_in.at[n], 4 + n, sibling)
        out = (gk_ref, gv_ref)[n]
        out[:, pl.ds(pl.multiple_of(core * HD, HD), HD)] = sums[core].astype(jnp.bfloat16)
    for n in range(2):
        moves.landed(mid_ref.at[n], n, {"head": two})
    cross.start(mid_ref, far_ref.at[1], 3, sibling)
    for n, out in enumerate((gk_ref, gv_ref)):
        cross.landed(swap_in.at[n], 4 + n, sibling)
        out[:, pl.ds(pl.multiple_of((1 - core) * HD, HD), HD)] = swap_in[n]
    cross.landed(far_ref.at[1], 3, sibling)
    for way in ways:
        way.copies.finish()
    moves.finish()
    cross.finish()


def scatter_sums(pk, pv, near, gqx, w_key, w_value):
    vmem = pl.BlockSpec(memory_space=pltpu.VMEM)
    anyspace = pl.BlockSpec(memory_space=pl.ANY)
    blk = jnp.bfloat16
    block = (2, 2 * CH, HD)
    one = [
        pltpu.VMEM((4, 4) + block, blk),
        pltpu.VMEM((4,) + block, blk),
        pltpu.VMEM((4, 2) + block, blk),
        pltpu.VMEM(block, blk),
        pltpu.VMEM((2,) + block, blk),
    ]
    return pl.pallas_call(
        scatter_kernel,
        out_shape=(jax.ShapeDtypeStruct((2 * CH, 2 * HD), blk),) * 2 + (
            jax.ShapeDtypeStruct(gqx.shape, blk),
            jax.ShapeDtypeStruct(near.shape[1:], blk),
            jax.ShapeDtypeStruct((3,) + near.shape[1:], blk),
        ),
        in_specs=[anyspace] * 6,
        out_specs=(vmem,) * 2 + (anyspace,) * 3,
        scratch_shapes=one + one
        + [pltpu.VMEM(block, jnp.float32), pltpu.VMEM(block, blk), pltpu.VMEM(block, blk)]
        + [pltpu.SemaphoreType.DMA((20,))] * 4
        + [pltpu.SemaphoreType.DMA((2,))] * 2
        + [pltpu.SemaphoreType.DMA((6,))] * 2
        + [pltpu.SemaphoreType.DMA((2, 16))],
        compiler_params=pltpu.CompilerParams(
            collective_id=1, has_side_effects=True, vmem_limit_bytes=VMEM_MIB * MIB
        ),
        name="scatter_dkv",
    )(pk, pv, near, gqx, w_key, w_value)


def project_kernel(
    gk_ref, gv_ref, hdq_ref, wk_hbm, wv_hbm, near_ref, mid_ref, far_ref, gx_ref, hg_ref,
    grads, weights, total, half, g_send, g_recv, o_send, o_recv, h_send, h_recv, w_sem, own_sem,
):
    me_z = lax.axis_index("head")
    y, x, core = ctx_coords()
    plane = Plane("x")
    barrier_with(
        [{"head": turn(me_z, d, NZ)} for d in (1, 2, 3)] + ctx_targets()
    )
    width = weights.shape[2]
    piece = width // 2
    sends = Copies(g_send, g_recv)
    for d in (1, 2, 3):
        sends.start(gk_ref, grads.at[d, 0], 2 * d - 2, {"head": turn(me_z, d, NZ)})
        sends.start(gv_ref, grads.at[d, 1], 2 * d - 1, {"head": turn(me_z, d, NZ)})

    units = Copies(h_send, h_recv)
    me = plane.at(0, 0)
    rows = [pl.ds(0, CH // 2), pl.ds(CH // 2, CH // 2)]
    own_copy = pltpu.make_async_copy(hdq_ref, hg_ref.at[y, x, core], own_sem.at[4])
    own_copy.start()
    own_copy.wait()
    for d in (1, 2, 3):
        for n, (da, db) in enumerate(((d, 0), (0, d))):
            units.start(
                hg_ref.at[y, x, core, rows[n]], hg_ref.at[y, x, core, rows[n]], 2 * d - 2 + n,
                {"ctx": plane.at(da, db)},
            )

    wrows = pl.ds(pl.multiple_of(me_z * width, width), width)
    fetches = [[
        pltpu.make_async_copy(wk_hbm.at[wrows], weights.at[0, 0], w_sem.at[0]),
        pltpu.make_async_copy(wv_hbm.at[wrows], weights.at[0, 1], w_sem.at[1]),
    ]]
    mine_rows = pl.ds(pl.multiple_of(core * piece, piece), piece)
    other_rows = pl.ds(pl.multiple_of((1 - core) * piece, piece), piece)
    nears = (near_ref.at[0], mid_ref, near_ref.at[1])
    for d, near in enumerate(nears, start=1):
        far = far_ref.at[d - 1]
        fetches.append([
            pltpu.make_async_copy(near, weights.at[d, :, mine_rows], w_sem.at[2 * d]),
            pltpu.make_async_copy(far, weights.at[d, :, other_rows], w_sem.at[2 * d + 1]),
        ])
    for pair in fetches:
        for copy in pair:
            copy.start()

    def partial(d, cols):
        left = (gk_ref[...], gv_ref[...]) if d == 0 else (grads[d, 0], grads[d, 1])
        return dot_nt(left[0], weights[d, 0, cols, :]) + dot_nt(left[1], weights[d, 1, cols, :])

    step = 512
    for copy in fetches[0]:
        copy.wait()

    def own_part(n, carry):
        cols = pl.ds(pl.multiple_of(n * step, step), step)
        total[:, cols] = partial(0, cols)
        return carry

    lax.fori_loop(0, width // step, own_part, 0)

    for d in (1, 2, 3):
        for n, (da, db) in enumerate(((-d, 0), (0, -d))):
            at = hg_ref.at[turn(y, db, NY), turn(x, da, NX), core, rows[n]]
            units.landed(at, 2 * d - 2 + n, {"ctx": plane.at(da, db)})
    for d in (1, 2, 3):
        units.start(
            hg_ref.at[y, :, core, rows[0]], hg_ref.at[y, :, core, rows[0]], 4 + 2 * d, {"ctx": plane.at(0, d)}
        )
        units.start(
            hg_ref.at[:, x, core, rows[1]], hg_ref.at[:, x, core, rows[1]], 5 + 2 * d, {"ctx": plane.at(d, 0)}
        )

    for d in (1, 3):
        for n in range(2):
            sends.landed(grads.at[d, n], 2 * d - 2 + n, {"head": turn(me_z, -d, NZ)})
        for copy in fetches[d]:
            copy.wait()

        def next_part(n, carry):
            cols = pl.ds(pl.multiple_of(n * step, step), step)
            total[:, cols] += partial(d, cols)
            return carry

        lax.fori_loop(0, width // step, next_part, 0)

    for n in range(2):
        sends.landed(grads.at[2, n], 2 + n, {"head": turn(me_z, -2, NZ)})
    for copy in fetches[2]:
        copy.wait()
    outs = Copies(o_send, o_recv)
    quarter = half.shape[0] // NZ
    own_copies = []
    for n in range(width // step):
        cols = pl.ds(n * step, step)
        half[:, n * step:(n + 1) * step] = (total[:, n * step:(n + 1) * step] + partial(2, cols)).astype(jnp.bfloat16)
        out_cols = pl.ds(pl.multiple_of(me_z * width + n * step, step), step)
        for d in (1, 2, 3):
            to = turn(me_z, d, NZ)
            outs.start(
                half.at[pl.ds(pl.multiple_of(to * quarter, quarter), quarter), cols],
                gx_ref.at[:, out_cols], 4 * (d - 1) + n, {"head": to},
            )
        own = pltpu.make_async_copy(
            half.at[pl.ds(pl.multiple_of(me_z * quarter, quarter), quarter), cols],
            gx_ref.at[:, out_cols], own_sem.at[n],
        )
        own.start()
        own_copies.append(own)

    for d in (1, 2, 3):
        units.landed(
            hg_ref.at[turn(y, -d, NY), :, core, rows[0]], 4 + 2 * d, {"ctx": plane.at(0, -d)}
        )
        units.landed(
            hg_ref.at[:, turn(x, -d, NX), core, rows[1]], 5 + 2 * d, {"ctx": plane.at(-d, 0)}
        )
    sibling = {"ctx": plane.at(0, 0, True)}
    units.start(hg_ref.at[:, :, core], hg_ref.at[:, :, core], 12, sibling)
    units.landed(hg_ref.at[:, :, 1 - core], 12, sibling)

    for n in range(width // step):
        for d in (1, 2, 3):
            origin = turn(me_z, -d, NZ)
            out_cols = pl.ds(pl.multiple_of(origin * width + n * step, step), step)
            outs.landed(gx_ref.at[:, out_cols], 4 * (d - 1) + n, {"head": origin})
    sends.finish()
    outs.finish()
    units.finish()
    for copy in own_copies:
        copy.wait()


def project(gk, gv, hdq, w_key, w_value, near, mid, far):
    vmem = pl.BlockSpec(memory_space=pltpu.VMEM)
    hbm = pl.BlockSpec(memory_space=pl.ANY)
    blk = jnp.bfloat16
    depth = w_key.shape[0]
    width = depth // NZ
    return pl.pallas_call(
        project_kernel,
        out_shape=(
            jax.ShapeDtypeStruct((2 * CH // NZ, depth), blk),
            jax.ShapeDtypeStruct((NY, NX, 2, CH, HD), blk),
        ),
        in_specs=[vmem, vmem, vmem] + [hbm] * 5,
        out_specs=(vmem, vmem),
        scratch_shapes=[
            pltpu.VMEM((NZ, 2, 2 * CH, 2 * HD), blk),
            pltpu.VMEM((NZ, 2, width, 2 * HD), blk),
            pltpu.VMEM((2 * CH, width), jnp.float32),
            pltpu.VMEM((2 * CH, width), blk),
            pltpu.SemaphoreType.DMA((6,)),
            pltpu.SemaphoreType.DMA((6,)),
            pltpu.SemaphoreType.DMA((12,)),
            pltpu.SemaphoreType.DMA((12,)),
            pltpu.SemaphoreType.DMA((13,)),
            pltpu.SemaphoreType.DMA((13,)),
            pltpu.SemaphoreType.DMA((8,)),
            pltpu.SemaphoreType.DMA((5,)),
        ],
        compiler_params=pltpu.CompilerParams(
            collective_id=2, has_side_effects=True, vmem_limit_bytes=VMEM_MIB * MIB
        ),
        name="project",
    )(gk, gv, hdq, w_key, w_value, near, mid, far)


def finish_kernel(span_slot, gq_hbm, gqo_hbm, hg_hbm, gk_hbm, gv_hbm, gx_hbm, oq, ok, ov, ox, vq, vk, vv, vx, sems, head_sems):
    me = lax.axis_index("ctx")
    core = lax.rem(me, 2)
    ways = ((gx_hbm, vx, ox), (gk_hbm, vk, ok), (gv_hbm, vv, ov))
    loads = [pltpu.make_async_copy(src, mid, sems.at[n]) for n, (src, mid, _) in enumerate(ways)]
    for copy in loads:
        copy.start()
    for i in range(2):
        rows = pl.ds(i * CH, CH)
        dense = [span_slot[SPANS - 2 + s] == 2 * me + i for s in range(2)]
        light = jnp.logical_not(jnp.logical_or(dense[0], dense[1]))

        @pl.when(light)
        def _():
            pair = []
            for n, (src, which) in enumerate(((gq_hbm, core), (gqo_hbm, 1 - core))):
                cols = pl.ds(pl.multiple_of(which * GROUP * HD, GROUP * HD), GROUP * HD)
                pair.append(pltpu.make_async_copy(src.at[rows], vq.at[rows, cols], head_sems.at[n]))
                pair[-1].start()
            for copy in pair:
                copy.wait()

        for s in range(2):
            @pl.when(dense[s])
            def _():
                heads = []
                for h in range(2 * GROUP):
                    chip = s * GROUP + h % GROUP
                    heads.append(pltpu.make_async_copy(
                        hg_hbm.at[chip // NX, chip % NX, h // GROUP], vq.at[rows, pl.ds(h * HD, HD)], head_sems.at[h]
                    ))
                    heads[-1].start()
                for copy in heads:
                    copy.wait()

    stores = [pltpu.make_async_copy(vq, oq, sems.at[3])]
    stores[0].start()
    for n, (_, mid, dst) in enumerate(ways):
        loads[n].wait()
        stores.append(pltpu.make_async_copy(mid, dst, sems.at[n]))
        stores[-1].start()
    for copy in stores:
        copy.wait()


def finish(span_slot, gq, gqo, units, grad_k, grad_v, grad_x):
    anyspace = pl.BlockSpec(memory_space=pl.ANY)
    return pl.pallas_call(
        finish_kernel,
        out_shape=(
            jax.ShapeDtypeStruct((2 * CH, 2 * GROUP * HD), gq.dtype),
            jax.ShapeDtypeStruct(grad_k.shape, grad_k.dtype),
            jax.ShapeDtypeStruct(grad_v.shape, grad_v.dtype),
            jax.ShapeDtypeStruct(grad_x.shape, grad_x.dtype),
        ),
        in_specs=[pl.BlockSpec(memory_space=pltpu.SMEM)] + [anyspace] * 6,
        out_specs=(anyspace,) * 4,
        scratch_shapes=[
            pltpu.VMEM((2 * CH, 2 * GROUP * HD), gq.dtype),
            pltpu.VMEM(grad_k.shape, grad_k.dtype),
            pltpu.VMEM(grad_v.shape, grad_v.dtype),
            pltpu.VMEM(grad_x.shape, grad_x.dtype),
            pltpu.SemaphoreType.DMA((4,)),
            pltpu.SemaphoreType.DMA((2 * GROUP,)),
        ],
        compiler_params=pltpu.CompilerParams(vmem_limit_bytes=VMEM_MIB * MIB),
        name="finish",
    )(span_slot, gq, gqo, units, grad_k, grad_v, grad_x)


def per_device(queries, keys, values, d_out, w_key, w_value, pair_list, span_slot):
    me = lax.axis_index("ctx")
    own_slots = 2 * me + jnp.arange(2, dtype=jnp.int32)
    select = jnp.broadcast_to(
        (span_slot[SPANS - 2:, None, None] == own_slots[None, :, None]).astype(jnp.bfloat16), (2, 2, HD)
    )
    pair_rows = jnp.pad(pair_list.astype(jnp.bfloat16), ((0, 0), (0, HD - 2)))
    keys_pad = jnp.concatenate([keys, jnp.concatenate([pair_rows, pair_rows], axis=1)], axis=0)
    kg, vg, unit, qx, dox, near = gather_all(keys_pad, values, queries, d_out, select, w_key, w_value)
    kg = kg.reshape((NCTX,) + kg.shape[2:])
    vg = vg.reshape((NCTX,) + vg.shape[2:])
    gq, gqx, hdq, pk, pv = attend(span_slot, queries, d_out, qx, dox, kg, vg, unit)
    pk = pk.reshape((CHIPS, 2) + pk.shape[1:])
    pv = pv.reshape((CHIPS, 2) + pv.shape[1:])
    grad_k, grad_v, gqo, mid, far = scatter_sums(pk, pv, near, gqx, w_key, w_value)
    grad_x, units = project(grad_k, grad_v, hdq, w_key, w_value, near, mid, far)
    return finish(span_slot, gq, gqo, units, grad_k, grad_v, grad_x)


def solution(mesh):
    return jax.shard_map(
        per_device,
        mesh=mesh,
        in_specs=(
            P("ctx", "head"),
            P("ctx", "head"),
            P("ctx", "head"),
            P("ctx", "head"),
            P(None, "head"),
            P(None, "head"),
            P("ctx", None),
            P(),
        ),
        out_specs=(P("ctx", "head"), P("ctx", "head"), P("ctx", "head"), P(("ctx", "head"), None)),
        check_vma=False,
    )
```

time: 181 us -> 163 us (0.901)
  Pallas kernels: 168 us -> 158 us
  local copies, waits for them, and re-layouts: 4.96 us -> 1.47 us
  between operations: 3.34 us -> 0.68 us
  other arithmetic: 4.49 us -> 2.34 us
    pallas_call x2 -> x3, Pallas kernels: 95.5 us -> 78.6 us  [the longest x1 43.3 us: gather_all(): pl.pallas_call(gather_kernel, out_shape=(jax.ShapeDtypeStruct((CHIPS, 2,...]
    pallas_call x1, Pallas kernels: 36.1 us -> 46.5 us  [scatter_sums(): pl.pallas_call(scatter_kernel, out_shape=(jax.ShapeDtypeStruct((2 * CH, 2...]
    pallas_call x1, Pallas kernels: 36.6 us -> 32.8 us  [project(): pl.pallas_call(project_kernel, out_shape=(jax.ShapeDtypeStruct((2 * CH //...]
    unnamed x12 -> x0, local copies, waits for them, and re-layouts: 3.64 us -> none
where the time goes in v3:
time: 163 us; the launch traced here: 162 us
  Pallas kernels  158 us (97%)
  other arithmetic  2.34 us (1%)
    pallas_call x1, Pallas kernels, scatter_sums(): pl.pallas_call(scatter_kernel, out_shape=(jax.ShapeDtypeStruct((2 * CH, 2...  46.5 us
    pallas_call x1, Pallas kernels, gather_all(): pl.pallas_call(gather_kernel, out_shape=(jax.ShapeDtypeStruct((CHIPS, 2,...  43.3 us
    pallas_call x1, Pallas kernels, project(): pl.pallas_call(project_kernel, out_shape=(jax.ShapeDtypeStruct((2 * CH //...  32.8 us
    pallas_call x1, Pallas kernels, attend(): pl.pallas_call(attend_kernel, out_shape=(jax.ShapeDtypeStruct((2 * CH, GR...  30.6 us
    pallas_call x1, Pallas kernels, finish(): pl.pallas_call(finish_kernel, out_shape=(jax.ShapeDtypeStruct((2 * CH, 2...  4.68 us

profile of v3, /device:TPU:1, one launch (start us, length us, event | category | flops | bytes accessed | tf_op | source)
XLA Modules:
  0.0 162.4 jit_solution(7915789642766967498)
XLA Ops:
  0.6 0.7 convert_element_type.13
  1.3 0.7 slice.3
  2.1 0.1 compare_convert_fusion
  2.1 0.6 broadcast_in_dim.2.sel_ref
  2.8 0.1 copy.13
  2.9 1.6 maximum_maximum_fusion.keys_ref
  4.4 43.3 %gather_kv.1 = (bf16[16,2,272,128]{3,2,1,0:T(8,128)(2,1)}, bf16[16,2,256,128]{3,2,1,0:T(8,128)(2,1)}, bf16[2,128,128]{2,1,0:T(8,128)(2,1)}, bf16[256,1024]{1,0:T...) custom-call(bf16[272,256]{1,0:T(8,128)(2,1)} %maximum_maximum_fusion.keys_ref, ...), custom_call_target="tpu_custom_call" | custom-call | tf_op jit(solution)/shard_map/gather_kv/pallas_call | solution.py:284
  47.8 30.6 %attend.1 = (bf16[256,1024]{1,0:T(8,128)(2,1)}, bf16[256,1024]{1,0:T(8,128)(2,1)}, bf16[128,128]{1,0:T(8,128)(2,1)}, bf16[32,256,128]{2,1,0:T(8,128)(2,1)}, bf16[32,256,128]{2,1,0:T(8,128)(2,1)}) custom-call(s32[64]{0:T(128)} %span_slot.3, bf16[256,2048]{1,0:T(8,128)(2,1)} %q_hbm.1, bf16[256,2048]{1,0:T(8,128)(2,1)} %do_hbm.1, ...), custom_call_target="tpu_custom_call" | custom-call | flops 8000000000 | bytes 32000000 | tf_op jit(solution)/shard_map/attend/pallas_call | solution.py:558
  78.4 46.5 %scatter_dkv.1 = (bf16[256,256]{1,0:T(8,128)(2,1)}, bf16[256,256]{1,0:T(8,128)(2,1)}, bf16[256,1024]{1,0:T(8,128)(2,1)}, bf16[2,1024,256]{2,1,0:T(8,128)(2,1)}, bf16[3,2,1024,256]{3,2,1,0:T(8,128)(2,1)}) custom-call(bf16[16,2,256,128]{3,2,1,0:T(8,128)(2,1)} %bitcast.4, bf16[16,2,256,128]{3,2,1,0:T(8,128)(2,1)} %bitcast.5, ...), custom_call_target="tpu_custom_call" | custom-call | tf_op jit(solution)/shard_map/scatter_dkv/pallas_call | solution.py:734
  124.9 32.8 %project.1 = (bf16[64,8192]{1,0:T(8,128)(2,1)}, bf16[4,4,2,128,128]{4,3,2,1,0:T(8,128)(2,1)}) custom-call(bf16[256,256]{1,0:T(8,128)(2,1)} %get-tuple-element.33.gk_ref.gk_hbm, bf16[256,256]{1,0:T(8,128)(2,1)} %get-tuple-element.34.gv_ref.gv_hbm, bf16[128,128]{1,0:T(8,128)(2,1)} %get-tuple-element.35.hdq_ref, bf16[8192,256]{1,0:T(8,128)(2,1)} %wk_hbm.5, ...), custom_call_target="tpu_custom_call" | custom-call | tf_op jit(solution)/shard_map/project/pallas_call | solution.py:897
  157.7 4.7 %finish.1 = (bf16[256,2048]{1,0:T(8,128)(2,1)}, bf16[256,256]{1,0:T(8,128)(2,1)}, bf16[256,256]{1,0:T(8,128)(2,1)}, bf16[64,8192]{1,0:T(8,128)(2,1)}) custom-call(s32[64]{0:T(128)} %span_slot.3, bf16[256,1024]{1,0:T(8,128)(2,1)} %get-tuple-element.27.gq_hbm, bf16[256,1024]{1,0:T(8,128)(2,1)} %get-tuple-element.32.gqo_hbm, ...), custom_call_target="tpu_custom_call" | custom-call | tf_op jit(solution)/shard_map/finish/pallas_call | solution.py:973
  (2 shorter events, 0.0 us)

commit v4 on v3

--- a/solution.py
+++ b/solution.py
@@ -17,6 +17,8 @@
 NCTX = NX * NY * 2
 CHIPS = NX * NY
 GROUP = 8
+PARTS = 2
+WIDE = 4
 NPAD = 16
 SCALE = HD ** -0.5
 EXP_SCALE = SCALE * 1.4426950408889634
@@ -146,11 +148,14 @@
 
 
 def gather_kernel(
-    keys_ref, values_ref, q_ref, do_ref, sel_ref, wk_hbm, wv_hbm,
+    span_slot, pairs_ref, keys_ref, values_ref, q_ref, do_ref, wk_hbm, wv_hbm,
     kg_ref, vg_ref, unit_ref, qx_ref, dox_ref, near_ref,
-    give, held, from_core, first_in, mid, last_in,
+    keys_pad, give, held, from_core, first_in, mid, last_in,
     k_send, k_recv, v_send, v_recv, u_send, u_recv, w_send, w_recv, c_send, c_recv, own_sem,
 ):
+    keys_pad[0:2 * CH, :] = keys_ref[...]
+    for g in range(2):
+        keys_pad[2 * CH:2 * CH + NPAD, g * HD:(g + 1) * HD] = pairs_ref[...]
     barrier_with(ctx_targets() + head_targets((1, 3)))
     y, x, core = ctx_coords()
     plane = Plane("x")
@@ -166,11 +171,11 @@
 
     cross = Copies(c_send, c_recv)
     other = group_cols(1 - core, HD)
-    cross.start(keys_ref.at[:, other], kg_ref.at[chip, core], 0, sibling)
+    cross.start(keys_pad.at[:, other], kg_ref.at[chip, core], 0, sibling)
     cross.start(values_ref.at[:, other], vg_ref.at[chip, core], 1, sibling)
     mine = group_cols(core, HD)
     own_copies = [
-        pltpu.make_async_copy(keys_ref.at[:, mine], kg_ref.at[chip, core], own_sem.at[0]),
+        pltpu.make_async_copy(keys_pad.at[:, mine], kg_ref.at[chip, core], own_sem.at[0]),
         pltpu.make_async_copy(values_ref.at[:, mine], vg_ref.at[chip, core], own_sem.at[1]),
     ]
     for copy in own_copies:
@@ -179,8 +184,11 @@
     def pick(dst, group):
         def unit(j, carry):
             cols = pl.ds(pl.multiple_of((group * GROUP + lax.rem(j, GROUP)) * HD, HD), HD)
-            first = sel_ref[j // GROUP, 0:1, :]
-            second = sel_ref[j // GROUP, 1:2, :]
+            dense = span_slot[SPANS - 2 + j // GROUP]
+            first, second = [
+                jnp.full((1, HD), (dense == 4 * chip + 2 * core + i).astype(jnp.float32)).astype(jnp.bfloat16)
+                for i in range(2)
+            ]
             for n, ref in enumerate((q_ref, do_ref)):
                 dst[n, j // NX, lax.rem(j, NX)] = ref[0:CH, cols] * first + ref[CH:2 * CH, cols] * second
             return carry
@@ -208,7 +216,6 @@
             to = turn(me_z, step, NZ)
             start = pl.multiple_of((2 * to + core) * piece, piece)
             moves.start(ref.at[pl.ds(start, piece)], near_ref.at[side, n], 2 * side + n, {"head": to})
-
     qcols = group_cols(1 - core, GROUP * HD)
     cross.start(q_ref.at[:, qcols], qx_ref, 2, sibling)
     cross.start(do_ref.at[:, qcols], dox_ref, 3, sibling)
@@ -265,7 +272,8 @@
     cross.landed(dox_ref, 3, sibling)
     for n in range(2):
         for side, step in enumerate((1, -1)):
-            moves.landed(near_ref.at[side, n], 2 * side + n, {"head": turn(me_z, -step, NZ)})
+            origin = {"head": turn(me_z, -step, NZ)}
+            moves.landed(near_ref.at[side, n], 2 * side + n, origin)
     for m in range(4):
         for gather in gathers:
             gather.got_b_far(m)
@@ -276,7 +284,7 @@
     moves.finish()
 
 
-def gather_all(keys_pad, values, queries, d_out, select, w_key, w_value):
+def gather_all(span_slot, pair_rows, keys, values, queries, d_out, w_key, w_value):
     vmem = pl.BlockSpec(memory_space=pltpu.VMEM)
     anyspace = pl.BlockSpec(memory_space=pl.ANY)
     blk = jnp.bfloat16
@@ -284,16 +292,17 @@
     return pl.pallas_call(
         gather_kernel,
         out_shape=(
-            jax.ShapeDtypeStruct((CHIPS, 2, keys_pad.shape[0], HD), blk),
+            jax.ShapeDtypeStruct((CHIPS, 2, keys.shape[0] + NPAD, HD), blk),
             jax.ShapeDtypeStruct((CHIPS, 2, values.shape[0], HD), blk),
             jax.ShapeDtypeStruct((2, CH, HD), blk),
             jax.ShapeDtypeStruct((2 * CH, GROUP * HD), blk),
             jax.ShapeDtypeStruct((2 * CH, GROUP * HD), blk),
             jax.ShapeDtypeStruct((2, 2, piece) + w_key.shape[1:], blk),
         ),
-        in_specs=[vmem] * 5 + [anyspace] * 2,
-        out_specs=(anyspace, anyspace, vmem, anyspace, anyspace, anyspace),
+        in_specs=[pl.BlockSpec(memory_space=pltpu.SMEM)] + [vmem] * 5 + [anyspace] * 2,
+        out_specs=(anyspace, anyspace, vmem) + (anyspace,) * 3,
         scratch_shapes=[
+            pltpu.VMEM((keys.shape[0] + NPAD, keys.shape[1]), blk),
             pltpu.VMEM((2, NY, NX, CH, HD), blk),
             pltpu.VMEM((2, NY, NX, CH, HD), blk),
             pltpu.VMEM((2, NY, NX, CH, HD), blk),
@@ -306,8 +315,8 @@
             pltpu.SemaphoreType.DMA((20,)),
             pltpu.SemaphoreType.DMA((13,)),
             pltpu.SemaphoreType.DMA((13,)),
-            pltpu.SemaphoreType.DMA((4,)),
-            pltpu.SemaphoreType.DMA((4,)),
+            pltpu.SemaphoreType.DMA((8,)),
+            pltpu.SemaphoreType.DMA((8,)),
             pltpu.SemaphoreType.DMA((4,)),
             pltpu.SemaphoreType.DMA((4,)),
             pltpu.SemaphoreType.DMA((2,)),
@@ -316,7 +325,7 @@
             collective_id=0, has_side_effects=True, vmem_limit_bytes=VMEM_MIB * MIB
         ),
         name="gather_kv",
-    )(keys_pad, values, queries, d_out, select, w_key, w_value)
+    )(span_slot, pair_rows, keys, values, queries, d_out, w_key, w_value)
 
 
 def dot_nt(a, b):
@@ -334,7 +343,7 @@
 def attend_kernel(
     span_slot, q_hbm, do_hbm, qx_hbm, dox_hbm, kg_hbm, vg_hbm, unit_ref,
     gq_ref, gqx_ref, hdq_ref, pk_hbm, pv_hbm,
-    kg, vg, qs, ds, gq_all, probs, dprob, tops, stat, acck, accv, dqt, found, flags, slot_label, todo,
+    kg, vg, qs, ds, gq_all, stage, probs, dprob, tops, stat, acck, accv, dqt, found, flags, slot_label, todo,
     flag_sem, qsems, load_sems, store_sems,
 ):
     me = lax.axis_index("ctx")
@@ -386,17 +395,19 @@
     q_unit = unit_ref[0]
     do_unit = unit_ref[1]
 
-    def four(ref, t):
-        return jnp.concatenate([ref[2 * t, 0:2 * CH, :], ref[2 * t + 1, 0:2 * CH, :]], axis=0)
+    steps = NCTX // WIDE
+
+    def many(ref, t):
+        return jnp.concatenate([ref[WIDE * t + u, 0:2 * CH, :] for u in range(WIDE)], axis=0)
 
     def unit_first(t, carry):
         top, total, mix = carry
-        scores = dot_nt(four(kg, t), q_unit) * EXP_SCALE
-        mixed = dot_nt(four(vg, t), do_unit)
+        scores = dot_nt(many(kg, t), q_unit) * EXP_SCALE
+        mixed = dot_nt(many(vg, t), do_unit)
         diff = lax.broadcasted_iota(jnp.int32, (CH, HD), 0) - lax.broadcasted_iota(jnp.int32, (CH, HD), 1)
         scores = jnp.concatenate([
-            jnp.where(diff <= (label - slot_label[4 * t + u]) * CH, scores[u * CH:(u + 1) * CH], neg_fill)
-            for u in range(4)
+            jnp.where(diff <= (label - slot_label[2 * WIDE * t + u]) * CH, scores[u * CH:(u + 1) * CH], neg_fill)
+            for u in range(2 * WIDE)
         ], axis=0)
         new_top = jnp.maximum(top, jnp.max(scores, axis=0, keepdims=True))
         weights = jnp.exp2(scores - new_top)
@@ -415,7 +426,7 @@
     for n in range(4):
         for copy in loads[2 * n:2 * n + 2]:
             copy.wait()
-        state = lax.fori_loop(n * quarter // 2, (n + 1) * quarter // 2, unit_first, state)
+        state = lax.fori_loop(n * steps // 4, (n + 1) * steps // 4, unit_first, state)
     top, total, mix = state
     over = 1.0 / total
     delta = mix * over
@@ -426,12 +437,12 @@
         dscore = (weights * (dprob[t] - delta)).astype(jnp.bfloat16)
         value_part = dot_nn(weights.astype(jnp.bfloat16), do_unit)
         key_part = dot_nn(dscore, q_unit)
-        for u in range(2):
-            accv[2 * t + u] = value_part[2 * u * CH:2 * (u + 1) * CH]
-            acck[2 * t + u] = key_part[2 * u * CH:2 * (u + 1) * CH]
-        return acc + dot_tn(four(kg, t), dscore)
-
-    acc = lax.fori_loop(0, NCTX // 2, unit_second, jnp.zeros((HD, CH), jnp.float32))
+        for u in range(WIDE):
+            accv[WIDE * t + u] = value_part[2 * u * CH:2 * (u + 1) * CH]
+            acck[WIDE * t + u] = key_part[2 * u * CH:2 * (u + 1) * CH]
+        return acc + dot_tn(many(kg, t), dscore)
+
+    acc = lax.fori_loop(0, steps, unit_second, jnp.zeros((HD, CH), jnp.float32))
     hdq_ref[...] = (acc * SCALE).T.astype(jnp.bfloat16)
 
     flag_copy.wait()
@@ -457,27 +468,28 @@
             def rows_at(slot):
                 return pl.ds(pl.multiple_of(lax.rem(slot, 2) * CH, CH), CH)
 
-            def both(ref, t):
-                a, b = todo[2 * t], todo[2 * t + 1]
-                return jnp.concatenate([ref[a // 2, rows_at(a), :], ref[b // 2, rows_at(b), :]], axis=0)
-
-            limits = (0, jnp.where(count >= 2, CH, -CH))
-            tail = (CH, -CH)
-            odd = jnp.logical_and(lax.rem(count, 2) == 1, count > 1)
-
-            def dots(t, limits):
-                scores = dot_nt(both(kg, t), qs[u]) * EXP_SCALE
-                if limits is not None:
+            todo[count + 1] = own_slot
+
+            def some(ref, base, size):
+                slots = [todo[base + v] for v in range(size)]
+                return jnp.concatenate([ref[slot // 2, rows_at(slot), :] for slot in slots], axis=0)
+
+            def dots(base, size, masked):
+                scores = dot_nt(some(kg, base, size), qs[u]) * EXP_SCALE
+                if masked:
                     diff = lax.broadcasted_iota(jnp.int32, (CH, QB), 0) - lax.rem(
                         lax.broadcasted_iota(jnp.int32, (CH, QB), 1), CH
                     )
+                    limits = [
+                        jnp.where(base + v == 0, 0, jnp.where(base + v < count, CH, -CH)) for v in range(size)
+                    ]
                     scores = jnp.concatenate([
-                        jnp.where(diff <= limits[v], scores[v * CH:(v + 1) * CH], neg_fill) for v in range(2)
+                        jnp.where(diff <= limits[v], scores[v * CH:(v + 1) * CH], neg_fill) for v in range(size)
                     ], axis=0)
-                return scores, dot_nt(both(vg, t), ds[u])
-
-            def first(t, limits=None):
-                scores, mixed = dots(t, limits)
+                return scores, dot_nt(some(vg, base, size), ds[u])
+
+            def first(base, size, masked):
+                scores, mixed = dots(base, size, masked)
                 old_top = stat[0:1, :]
                 new_top = jnp.maximum(old_top, jnp.max(scores, axis=0, keepdims=True))
                 weights = jnp.exp2(scores - new_top)
@@ -486,30 +498,39 @@
                 stat[1:2, :] = stat[1:2, :] * factor + jnp.sum(weights, axis=0, keepdims=True)
                 stat[2:3, :] = stat[2:3, :] * factor + jnp.sum(weights * mixed, axis=0, keepdims=True)
 
-            def second(t, limits=None):
-                scores, mixed = dots(t, limits)
+            def second(base, size, masked):
+                scores, mixed = dots(base, size, masked)
                 weights = jnp.exp2(scores - stat[3:4, :])
                 dscore = (weights * (mixed - stat[4:5, :])).astype(jnp.bfloat16)
                 value_part = dot_nn(weights.astype(jnp.bfloat16), ds[u])
                 key_part = dot_nn(dscore, qs[u])
-                for v in range(2):
-                    slot = todo[2 * t + v]
+                for v in range(size):
+                    slot = todo[base + v]
                     accv[slot // 2, rows_at(slot), :] += value_part[v * CH:(v + 1) * CH]
                     acck[slot // 2, rows_at(slot), :] += key_part[v * CH:(v + 1) * CH]
-                dqt[...] += dot_tn(both(kg, t), dscore)
+                dqt[...] += dot_tn(some(kg, base, size), dscore)
+
+            fours = (count + 1) // 4
 
             def sweep(work):
-                work(0, limits)
-
-                def plain(t, c):
-                    work(t)
+                def step(t, c):
+                    masked = jnp.logical_or(t == 0, 4 * t + 4 > count)
+
+                    @pl.when(masked)
+                    def _():
+                        work(4 * t, 4, True)
+
+                    @pl.when(jnp.logical_not(masked))
+                    def _():
+                        work(4 * t, 4, False)
+
                     return c
 
-                lax.fori_loop(1, count // 2, plain, 0)
-
-                @pl.when(odd)
+                lax.fori_loop(0, fours, step, 0)
+
+                @pl.when(4 * fours < count)
                 def _():
-                    work(count // 2, tail)
+                    work(4 * fours, 2, True)
 
             stat[0:1, :] = jnp.full((1, QB), neg_fill, jnp.float32)
             stat[1:3, :] = jnp.zeros((2, QB), jnp.float32)
@@ -538,13 +559,17 @@
         part = pl.ds(n * quarter, quarter)
 
         def narrow(t, carry):
-            kg[t, 0:2 * CH, :] = acck[t].astype(jnp.bfloat16)
-            vg[t] = accv[t].astype(jnp.bfloat16)
+            for side, ref in enumerate((acck, accv)):
+                rows = ref[t].astype(jnp.bfloat16).reshape(NZ, PARTS, 2 * CH // NZ // PARTS, HD)
+                for m in range(PARTS):
+                    stage[side, m, t] = rows[:, m]
             return carry
 
         lax.fori_loop(n * quarter, (n + 1) * quarter, narrow, 0)
-        for side, (src, dst) in enumerate(((kg.at[part, pl.ds(0, 2 * CH)], pk_hbm), (vg.at[part], pv_hbm))):
-            stores.append(pltpu.make_async_copy(src, dst.at[part], store_sems.at[n, side]))
+        for side, dst in enumerate((pk_hbm, pv_hbm)):
+            stores.append(
+                pltpu.make_async_copy(stage.at[side, :, part], dst.at[:, part], store_sems.at[n, side])
+            )
             stores[-1].start()
     for copy in stores:
         copy.wait()
@@ -561,8 +586,8 @@
             jax.ShapeDtypeStruct((2 * CH, GROUP * HD), blk),
             jax.ShapeDtypeStruct((2 * CH, GROUP * HD), blk),
             jax.ShapeDtypeStruct((CH, HD), blk),
-            jax.ShapeDtypeStruct((NCTX, 2 * CH, HD), blk),
-            jax.ShapeDtypeStruct((NCTX, 2 * CH, HD), blk),
+            jax.ShapeDtypeStruct((PARTS, NCTX, NZ, 2 * CH // NZ // PARTS, HD), blk),
+            jax.ShapeDtypeStruct((PARTS, NCTX, NZ, 2 * CH // NZ // PARTS, HD), blk),
         ),
         in_specs=[smem] + [anyspace] * 6 + [vmem],
         out_specs=(anyspace, anyspace, vmem, anyspace, anyspace),
@@ -572,9 +597,10 @@
             pltpu.VMEM((4, GROUP * CH, HD), blk),
             pltpu.VMEM((4, GROUP * CH, HD), blk),
             pltpu.VMEM((4 * CH, GROUP * HD), blk),
-            pltpu.VMEM((NCTX // 2, 4 * CH, HD), jnp.float32),
-            pltpu.VMEM((NCTX // 2, 4 * CH, HD), jnp.float32),
-            pltpu.VMEM((NCTX // 2, 1, HD), jnp.float32),
+            pltpu.VMEM((2, PARTS, NCTX, NZ, 2 * CH // NZ // PARTS, HD), blk),
+            pltpu.VMEM((NCTX // WIDE, 2 * WIDE * CH, HD), jnp.float32),
+            pltpu.VMEM((NCTX // WIDE, 2 * WIDE * CH, HD), jnp.float32),
+            pltpu.VMEM((NCTX // WIDE, 1, HD), jnp.float32),
             pltpu.VMEM((8, QB), jnp.float32),
             pltpu.VMEM((NCTX, 2 * CH, HD), jnp.float32),
             pltpu.VMEM((NCTX, 2 * CH, HD), jnp.float32),
@@ -655,272 +681,267 @@
         return total + self.full_b[0].astype(jnp.float32) + self.full_b[1].astype(jnp.float32)
 
 
-def scatter_kernel(
-    pk_ref, pv_ref, near_ref, gqx_ref, wk_hbm, wv_hbm, gk_ref, gv_ref, gqo_ref, mid_ref, far_ref,
+def reduce_project_kernel(
+    pk_ref, pv_ref, near_ref, gqx_ref, hdq_ref, wk_hbm, wv_hbm,
+    gk_ref, gv_ref, gqo_ref, gx_ref, hg_ref,
     k_own, k_near, k_full, k_near_b, k_full_b,
-    v_own, v_near, v_full, v_near_b, v_full_b, sums, swap, swap_in,
-    k_send, k_recv, v_send, v_recv, w_send, w_recv, c_send, c_recv, own_sems,
+    v_own, v_near, v_full, v_near_b, v_full_b,
+    sums, swap, swap_in, grads, weights, total, half,
+    k_send, k_recv, v_send, v_recv, w_send, w_recv, c_send, c_recv, g_send, g_recv, o_send, o_recv, h_send, h_recv,
+    own_sems, w_sem, hg_sem, o_sem,
 ):
     barrier_with(ctx_targets() + head_targets((1, 2, 3)))
-    core = lax.rem(lax.axis_index("ctx"), 2)
-    sibling = {"ctx": Plane("x").at(0, 0, True)}
+    me_z = lax.axis_index("head")
+    y, x, core = ctx_coords()
+    plane = Plane("x")
+    sibling = {"ctx": plane.at(0, 0, True)}
     ways = [
-        Scatter("y", pk_ref, k_own, k_near, k_full, k_near_b, k_full_b, k_send, k_recv, own_sems.at[0]),
-        Scatter("x", pv_ref, v_own, v_near, v_full, v_near_b, v_full_b, v_send, v_recv, own_sems.at[1]),
+        [
+            Scatter("y", pk_ref.at[m], *(ref.at[m] for ref in (
+                k_own, k_near, k_full, k_near_b, k_full_b, k_send, k_recv)), own_sems.at[m, 0]),
+            Scatter("x", pv_ref.at[m], *(ref.at[m] for ref in (
+                v_own, v_near, v_full, v_near_b, v_full_b, v_send, v_recv)), own_sems.at[m, 1]),
+        ]
+        for m in range(PARTS)
     ]
     order = (2, 1, 3, 0)
-    for q in order:
-        for way in ways:
-            way.far(q)
-    for e in (1, 3, 0):
+
+    def far(m):
         for q in order:
-            for way in ways:
-                way.load(q, e).start()
-
-    me_z = lax.axis_index("head")
-    piece = mid_ref.shape[1]
+            for way in ways[m]:
+                way.far(q)
+        for e in (1, 3, 0):
+            for q in order:
+                for way in ways[m]:
+                    way.load(q, e).start()
+
+    def next_hop(m):
+        for q in order:
+            for way in ways[m]:
+                way.next(q)
+
+    def last_hop(m):
+        for way in ways[m]:
+            way.last_far()
+        for side in range(2):
+            for way in ways[m]:
+                way.last_near(side)
+
+    far(0)
+
+    width = weights.shape[2]
+    piece = width // 2
     moves = Copies(w_send, w_recv)
     two = turn(me_z, 2, NZ)
     start = pl.multiple_of((2 * two + core) * piece, piece)
     for n, ref in enumerate((wk_hbm, wv_hbm)):
-        moves.start(ref.at[pl.ds(start, piece)], mid_ref.at[n], n, {"head": two})
+        moves.start(
+            ref.at[pl.ds(start, piece)], weights.at[2, n, pl.ds(pl.multiple_of(core * piece, piece), piece)], n,
+            {"head": two},
+        )
+    mine_rows = pl.ds(pl.multiple_of(core * piece, piece), piece)
+    other_rows = pl.ds(pl.multiple_of((1 - core) * piece, piece), piece)
     cross = Copies(c_send, c_recv)
-    cross.start(gqx_ref, gqo_ref, 0, sibling)
-    for side in range(2):
-        cross.start(near_ref.at[side], far_ref.at[2 * side], 1 + side, sibling)
-
-    for q in order:
-        for way in ways:
-            way.next(q)
-    for way in ways:
-        way.last_far()
-    for side in range(2):
-        for way in ways:
-            way.last_near(side)
-    cross.landed(gqo_ref, 0, sibling)
-    for side in range(2):
-        cross.landed(far_ref.at[2 * side], 1 + side, sibling)
-    for n, (way, factor) in enumerate(zip(ways, (SCALE, 1.0))):
-        sums[...] = way.finish() * factor
-        swap[n] = sums[1 - core].astype(jnp.bfloat16)
-        cross.start(swap.at[n], swap_in.at[n], 4 + n, sibling)
-        out = (gk_ref, gv_ref)[n]
-        out[:, pl.ds(pl.multiple_of(core * HD, HD), HD)] = sums[core].astype(jnp.bfloat16)
-    for n in range(2):
-        moves.landed(mid_ref.at[n], n, {"head": two})
-    cross.start(mid_ref, far_ref.at[1], 3, sibling)
-    for n, out in enumerate((gk_ref, gv_ref)):
-        cross.landed(swap_in.at[n], 4 + n, sibling)
-        out[:, pl.ds(pl.multiple_of((1 - core) * HD, HD), HD)] = swap_in[n]
-    cross.landed(far_ref.at[1], 3, sibling)
-    for way in ways:
-        way.copies.finish()
-    moves.finish()
-    cross.finish()
-
-
-def scatter_sums(pk, pv, near, gqx, w_key, w_value):
-    vmem = pl.BlockSpec(memory_space=pltpu.VMEM)
-    anyspace = pl.BlockSpec(memory_space=pl.ANY)
-    blk = jnp.bfloat16
-    block = (2, 2 * CH, HD)
-    one = [
-        pltpu.VMEM((4, 4) + block, blk),
-        pltpu.VMEM((4,) + block, blk),
-        pltpu.VMEM((4, 2) + block, blk),
-        pltpu.VMEM(block, blk),
-        pltpu.VMEM((2,) + block, blk),
+    for side, d in enumerate((1, 3)):
+        cross.start(near_ref.at[side], weights.at[d, :, mine_rows], side, sibling)
+    cross.start(gqx_ref, gqo_ref, 2, sibling)
+    wrows = pl.ds(pl.multiple_of(me_z * width, width), width)
+    fetches = [
+        pltpu.make_async_copy(wk_hbm.at[wrows], weights.at[0, 0], w_sem.at[0]),
+        pltpu.make_async_copy(wv_hbm.at[wrows], weights.at[0, 1], w_sem.at[1]),
+        pltpu.make_async_copy(near_ref.at[0], weights.at[1, :, mine_rows], w_sem.at[2]),
+        pltpu.make_async_copy(near_ref.at[1], weights.at[3, :, mine_rows], w_sem.at[3]),
     ]
-    return pl.pallas_call(
-        scatter_kernel,
-        out_shape=(jax.ShapeDtypeStruct((2 * CH, 2 * HD), blk),) * 2 + (
-            jax.ShapeDtypeStruct(gqx.shape, blk),
-            jax.ShapeDtypeStruct(near.shape[1:], blk),
-            jax.ShapeDtypeStruct((3,) + near.shape[1:], blk),
-        ),
-        in_specs=[anyspace] * 6,
-        out_specs=(vmem,) * 2 + (anyspace,) * 3,
-        scratch_shapes=one + one
-        + [pltpu.VMEM(block, jnp.float32), pltpu.VMEM(block, blk), pltpu.VMEM(block, blk)]
-        + [pltpu.SemaphoreType.DMA((20,))] * 4
-        + [pltpu.SemaphoreType.DMA((2,))] * 2
-        + [pltpu.SemaphoreType.DMA((6,))] * 2
-        + [pltpu.SemaphoreType.DMA((2, 16))],
-        compiler_params=pltpu.CompilerParams(
-            collective_id=1, has_side_effects=True, vmem_limit_bytes=VMEM_MIB * MIB
-        ),
-        name="scatter_dkv",
-    )(pk, pv, near, gqx, w_key, w_value)
-
-
-def project_kernel(
-    gk_ref, gv_ref, hdq_ref, wk_hbm, wv_hbm, near_ref, mid_ref, far_ref, gx_ref, hg_ref,
-    grads, weights, total, half, g_send, g_recv, o_send, o_recv, h_send, h_recv, w_sem, own_sem,
-):
-    me_z = lax.axis_index("head")
-    y, x, core = ctx_coords()
-    plane = Plane("x")
-    barrier_with(
-        [{"head": turn(me_z, d, NZ)} for d in (1, 2, 3)] + ctx_targets()
-    )
-    width = weights.shape[2]
-    piece = width // 2
+    for copy in fetches:
+        copy.start()
+    hg_copy = pltpu.make_async_copy(hdq_ref, hg_ref.at[y, x, core], hg_sem.at[0])
+    hg_copy.start()
+
+    rows_of_part = 2 * CH // NZ // PARTS
     sends = Copies(g_send, g_recv)
-    for d in (1, 2, 3):
-        sends.start(gk_ref, grads.at[d, 0], 2 * d - 2, {"head": turn(me_z, d, NZ)})
-        sends.start(gv_ref, grads.at[d, 1], 2 * d - 1, {"head": turn(me_z, d, NZ)})
+    outs = Copies(o_send, o_recv)
+    own_outs = []
+
+    def collect(m):
+        for n, (way, factor) in enumerate(zip(ways[m], (SCALE, 1.0))):
+            sums[...] = (way.finish() * factor).reshape(sums.shape)
+            swap[m, n] = sums[1 - core].astype(jnp.bfloat16)
+            cross.start(swap.at[m, n], swap_in.at[m, n], 4 + 2 * m + n, sibling)
+            grads[m, 0, n, :, pl.ds(pl.multiple_of(core * HD, HD), HD)] = sums[core].astype(jnp.bfloat16)
+
+    def share(m):
+        for n, out in enumerate((gk_ref, gv_ref)):
+            cross.landed(swap_in.at[m, n], 4 + 2 * m + n, sibling)
+            grads[m, 0, n, :, pl.ds(pl.multiple_of((1 - core) * HD, HD), HD)] = swap_in[m, n]
+        for d in (1, 3, 2):
+            sends.start(grads.at[m, 0], grads.at[m, d], 3 * m + d - 1, {"head": turn(me_z, d, NZ)})
+        for n, out in enumerate((gk_ref, gv_ref)):
+            for h in range(NZ):
+                at = (h * PARTS + m) * rows_of_part
+                out[at:at + rows_of_part, :] = grads[m, 0, n, h * rows_of_part:(h + 1) * rows_of_part, :]
+
+    step = 512
+
+    def partial(m, d, cols):
+        return dot_nt(grads[m, d, 0], weights[d, 0, cols, :]) + dot_nt(grads[m, d, 1], weights[d, 1, cols, :])
+
+    def columns(n):
+        return pl.ds(pl.multiple_of(n * step, step), step)
+
+    def multiply(m, d):
+        if d != 0:
+            sends.landed(grads.at[m, d], 3 * m + d - 1, {"head": turn(me_z, -d, NZ)})
+
+        def part(n, carry):
+            if d == 0:
+                total[m, :, columns(n)] = partial(m, d, columns(n))
+            else:
+                total[m, :, columns(n)] += partial(m, d, columns(n))
+            return carry
+
+        lax.fori_loop(0, width // step, part, 0)
+
+    def deliver(m):
+        sends.landed(grads.at[m, 2], 3 * m + 1, {"head": turn(me_z, -2, NZ)})
+        rows_out = pl.ds(m * rows_of_part, rows_of_part)
+        for n in range(width // step):
+            cols = pl.ds(n * step, step)
+            half[m, :, n * step:(n + 1) * step] = (
+                total[m, :, n * step:(n + 1) * step] + partial(m, 2, cols)
+            ).astype(jnp.bfloat16)
+            out_cols = pl.ds(pl.multiple_of(me_z * width + n * step, step), step)
+
+            def block(to):
+                return half.at[m, pl.ds(pl.multiple_of(to * rows_of_part, rows_of_part), rows_of_part), cols]
+
+            for d in (1, 3, 2):
+                to = turn(me_z, d, NZ)
+                outs.start(block(to), gx_ref.at[rows_out, out_cols], (m * 3 + d - 1) * 4 + n, {"head": to})
+            own_outs.append(pltpu.make_async_copy(block(me_z), gx_ref.at[rows_out, out_cols], o_sem.at[m * 4 + n]))
+            own_outs[-1].start()
+
+    next_hop(0)
+    far(1)
+    last_hop(0)
+    next_hop(1)
+    collect(0)
+    last_hop(1)
+    share(0)
+
+    for side, d in enumerate((1, 3)):
+        cross.landed(weights.at[d, :, other_rows], side, sibling)
+    for copy in fetches:
+        copy.wait()
+    multiply(0, 0)
+    collect(1)
+    share(1)
 
     units = Copies(h_send, h_recv)
-    me = plane.at(0, 0)
     rows = [pl.ds(0, CH // 2), pl.ds(CH // 2, CH // 2)]
-    own_copy = pltpu.make_async_copy(hdq_ref, hg_ref.at[y, x, core], own_sem.at[4])
-    own_copy.start()
-    own_copy.wait()
+    hg_copy.wait()
     for d in (1, 2, 3):
         for n, (da, db) in enumerate(((d, 0), (0, d))):
-            units.start(
-                hg_ref.at[y, x, core, rows[n]], hg_ref.at[y, x, core, rows[n]], 2 * d - 2 + n,
-                {"ctx": plane.at(da, db)},
-            )
-
-    wrows = pl.ds(pl.multiple_of(me_z * width, width), width)
-    fetches = [[
-        pltpu.make_async_copy(wk_hbm.at[wrows], weights.at[0, 0], w_sem.at[0]),
-        pltpu.make_async_copy(wv_hbm.at[wrows], weights.at[0, 1], w_sem.at[1]),
-    ]]
-    mine_rows = pl.ds(pl.multiple_of(core * piece, piece), piece)
-    other_rows = pl.ds(pl.multiple_of((1 - core) * piece, piece), piece)
-    nears = (near_ref.at[0], mid_ref, near_ref.at[1])
-    for d, near in enumerate(nears, start=1):
-        far = far_ref.at[d - 1]
-        fetches.append([
-            pltpu.make_async_copy(near, weights.at[d, :, mine_rows], w_sem.at[2 * d]),
-            pltpu.make_async_copy(far, weights.at[d, :, other_rows], w_sem.at[2 * d + 1]),
-        ])
-    for pair in fetches:
-        for copy in pair:
-            copy.start()
-
-    def partial(d, cols):
-        left = (gk_ref[...], gv_ref[...]) if d == 0 else (grads[d, 0], grads[d, 1])
-        return dot_nt(left[0], weights[d, 0, cols, :]) + dot_nt(left[1], weights[d, 1, cols, :])
-
-    step = 512
-    for copy in fetches[0]:
-        copy.wait()
-
-    def own_part(n, carry):
-        cols = pl.ds(pl.multiple_of(n * step, step), step)
-        total[:, cols] = partial(0, cols)
-        return carry
-
-    lax.fori_loop(0, width // step, own_part, 0)
+            block = hg_ref.at[y, x, core, rows[n]]
+            units.start(block, block, 2 * d - 2 + n, {"ctx": plane.at(da, db)})
+
+    multiply(0, 1)
+    multiply(0, 3)
+    for n in range(2):
+        moves.landed(weights.at[2, n, mine_rows], n, {"head": two})
+    cross.start(weights.at[2, :, mine_rows], weights.at[2, :, mine_rows], 3, sibling)
+    multiply(1, 0)
+    cross.landed(weights.at[2, :, other_rows], 3, sibling)
+    deliver(0)
 
     for d in (1, 2, 3):
         for n, (da, db) in enumerate(((-d, 0), (0, -d))):
             at = hg_ref.at[turn(y, db, NY), turn(x, da, NX), core, rows[n]]
             units.landed(at, 2 * d - 2 + n, {"ctx": plane.at(da, db)})
     for d in (1, 2, 3):
-        units.start(
-            hg_ref.at[y, :, core, rows[0]], hg_ref.at[y, :, core, rows[0]], 4 + 2 * d, {"ctx": plane.at(0, d)}
-        )
-        units.start(
-            hg_ref.at[:, x, core, rows[1]], hg_ref.at[:, x, core, rows[1]], 5 + 2 * d, {"ctx": plane.at(d, 0)}
-        )
-
-    for d in (1, 3):
-        for n in range(2):
-            sends.landed(grads.at[d, n], 2 * d - 2 + n, {"head": turn(me_z, -d, NZ)})
-        for copy in fetches[d]:
-            copy.wait()
-
-        def next_part(n, carry):
-            cols = pl.ds(pl.multiple_of(n * step, step), step)
-            total[:, cols] += partial(d, cols)
-            return carry
-
-        lax.fori_loop(0, width // step, next_part, 0)
-
-    for n in range(2):
-        sends.landed(grads.at[2, n], 2 + n, {"head": turn(me_z, -2, NZ)})
-    for copy in fetches[2]:
-        copy.wait()
-    outs = Copies(o_send, o_recv)
-    quarter = half.shape[0] // NZ
-    own_copies = []
-    for n in range(width // step):
-        cols = pl.ds(n * step, step)
-        half[:, n * step:(n + 1) * step] = (total[:, n * step:(n + 1) * step] + partial(2, cols)).astype(jnp.bfloat16)
-        out_cols = pl.ds(pl.multiple_of(me_z * width + n * step, step), step)
-        for d in (1, 2, 3):
-            to = turn(me_z, d, NZ)
-            outs.start(
-                half.at[pl.ds(pl.multiple_of(to * quarter, quarter), quarter), cols],
-                gx_ref.at[:, out_cols], 4 * (d - 1) + n, {"head": to},
-            )
-        own = pltpu.make_async_copy(
-            half.at[pl.ds(pl.multiple_of(me_z * quarter, quarter), quarter), cols],
-            gx_ref.at[:, out_cols], own_sem.at[n],
-        )
-        own.start()
-        own_copies.append(own)
+        block = hg_ref.at[y, :, core, rows[0]]
+        units.start(block, block, 4 + 2 * d, {"ctx": plane.at(0, d)})
+        block = hg_ref.at[:, x, core, rows[1]]
+        units.start(block, block, 5 + 2 * d, {"ctx": plane.at(d, 0)})
+
+    multiply(1, 1)
+    multiply(1, 3)
+    deliver(1)
 
     for d in (1, 2, 3):
-        units.landed(
-            hg_ref.at[turn(y, -d, NY), :, core, rows[0]], 4 + 2 * d, {"ctx": plane.at(0, -d)}
-        )
-        units.landed(
-            hg_ref.at[:, turn(x, -d, NX), core, rows[1]], 5 + 2 * d, {"ctx": plane.at(-d, 0)}
-        )
-    sibling = {"ctx": plane.at(0, 0, True)}
+        units.landed(hg_ref.at[turn(y, -d, NY), :, core, rows[0]], 4 + 2 * d, {"ctx": plane.at(0, -d)})
+        units.landed(hg_ref.at[:, turn(x, -d, NX), core, rows[1]], 5 + 2 * d, {"ctx": plane.at(-d, 0)})
     units.start(hg_ref.at[:, :, core], hg_ref.at[:, :, core], 12, sibling)
     units.landed(hg_ref.at[:, :, 1 - core], 12, sibling)
-
-    for n in range(width // step):
-        for d in (1, 2, 3):
-            origin = turn(me_z, -d, NZ)
-            out_cols = pl.ds(pl.multiple_of(origin * width + n * step, step), step)
-            outs.landed(gx_ref.at[:, out_cols], 4 * (d - 1) + n, {"head": origin})
-    sends.finish()
-    outs.finish()
-    units.finish()
-    for copy in own_copies:
+    cross.landed(gqo_ref, 2, sibling)
+
+    for m in range(PARTS):
+        rows_out = pl.ds(m * rows_of_part, rows_of_part)
+        for n in range(width // step):
+            for d in (1, 3, 2):
+                origin = turn(me_z, -d, NZ)
+                out_cols = pl.ds(pl.multiple_of(origin * width + n * step, step), step)
+                outs.landed(gx_ref.at[rows_out, out_cols], (m * 3 + d - 1) * 4 + n, {"head": origin})
+    for m in range(PARTS):
+        for way in ways[m]:
+            way.copies.finish()
+    for copies in (moves, cross, sends, outs, units):
+        copies.finish()
+    for copy in own_outs:
         copy.wait()
 
 
-def project(gk, gv, hdq, w_key, w_value, near, mid, far):
+def reduce_project(pk, pv, near, gqx, hdq, w_key, w_value):
     vmem = pl.BlockSpec(memory_space=pltpu.VMEM)
-    hbm = pl.BlockSpec(memory_space=pl.ANY)
+    anyspace = pl.BlockSpec(memory_space=pl.ANY)
     blk = jnp.bfloat16
     depth = w_key.shape[0]
     width = depth // NZ
+    rows = 2 * CH // PARTS
+    block = (2, NZ, rows // NZ, HD)
+    one = [
+        pltpu.VMEM((PARTS, 4, 4) + block, blk),
+        pltpu.VMEM((PARTS, 4) + block, blk),
+        pltpu.VMEM((PARTS, 4, 2) + block, blk),
+        pltpu.VMEM((PARTS,) + block, blk),
+        pltpu.VMEM((PARTS, 2) + block, blk),
+    ]
+
+    def pair(*shape):
+        return [pltpu.SemaphoreType.DMA(shape)] * 2
+
     return pl.pallas_call(
-        project_kernel,
+        reduce_project_kernel,
         out_shape=(
+            jax.ShapeDtypeStruct((2 * CH, 2 * HD), blk),
+            jax.ShapeDtypeStruct((2 * CH, 2 * HD), blk),
+            jax.ShapeDtypeStruct(gqx.shape, blk),
             jax.ShapeDtypeStruct((2 * CH // NZ, depth), blk),
             jax.ShapeDtypeStruct((NY, NX, 2, CH, HD), blk),
         ),
-        in_specs=[vmem, vmem, vmem] + [hbm] * 5,
-        out_specs=(vmem, vmem),
-        scratch_shapes=[
-            pltpu.VMEM((NZ, 2, 2 * CH, 2 * HD), blk),
+        in_specs=[anyspace] * 4 + [vmem] + [anyspace] * 2,
+        out_specs=(vmem, vmem, anyspace, vmem, vmem),
+        scratch_shapes=one + one
+        + [
+            pltpu.VMEM((2, rows, HD), jnp.float32),
+            pltpu.VMEM((PARTS, 2, rows, HD), blk),
+            pltpu.VMEM((PARTS, 2, rows, HD), blk),
+            pltpu.VMEM((PARTS, NZ, 2, rows, 2 * HD), blk),
             pltpu.VMEM((NZ, 2, width, 2 * HD), blk),
-            pltpu.VMEM((2 * CH, width), jnp.float32),
-            pltpu.VMEM((2 * CH, width), blk),
-            pltpu.SemaphoreType.DMA((6,)),
-            pltpu.SemaphoreType.DMA((6,)),
-            pltpu.SemaphoreType.DMA((12,)),
-            pltpu.SemaphoreType.DMA((12,)),
-            pltpu.SemaphoreType.DMA((13,)),
-            pltpu.SemaphoreType.DMA((13,)),
+            pltpu.VMEM((PARTS, rows, width), jnp.float32),
+            pltpu.VMEM((PARTS, rows, width), blk),
+        ]
+        + pair(PARTS, 20) + pair(PARTS, 20) + pair(2) + pair(8) + pair(6) + pair(24) + pair(13)
+        + [
+            pltpu.SemaphoreType.DMA((PARTS, 2, 16)),
+            pltpu.SemaphoreType.DMA((4,)),
+            pltpu.SemaphoreType.DMA((1,)),
             pltpu.SemaphoreType.DMA((8,)),
-            pltpu.SemaphoreType.DMA((5,)),
         ],
         compiler_params=pltpu.CompilerParams(
-            collective_id=2, has_side_effects=True, vmem_limit_bytes=VMEM_MIB * MIB
+            collective_id=1, has_side_effects=True, vmem_limit_bytes=VMEM_MIB * MIB
         ),
-        name="project",
-    )(gk, gv, hdq, w_key, w_value, near, mid, far)
+        name="reduce_project",
+    )(pk, pv, near, gqx, hdq, w_key, w_value)
 
 
 def finish_kernel(span_slot, gq_hbm, gqo_hbm, hg_hbm, gk_hbm, gv_hbm, gx_hbm, oq, ok, ov, ox, vq, vk, vv, vx, sems, head_sems):
@@ -994,21 +1015,14 @@
 
 
 def per_device(queries, keys, values, d_out, w_key, w_value, pair_list, span_slot):
-    me = lax.axis_index("ctx")
-    own_slots = 2 * me + jnp.arange(2, dtype=jnp.int32)
-    select = jnp.broadcast_to(
-        (span_slot[SPANS - 2:, None, None] == own_slots[None, :, None]).astype(jnp.bfloat16), (2, 2, HD)
-    )
     pair_rows = jnp.pad(pair_list.astype(jnp.bfloat16), ((0, 0), (0, HD - 2)))
-    keys_pad = jnp.concatenate([keys, jnp.concatenate([pair_rows, pair_rows], axis=1)], axis=0)
-    kg, vg, unit, qx, dox, near = gather_all(keys_pad, values, queries, d_out, select, w_key, w_value)
+    kg, vg, unit, qx, dox, near = gather_all(span_slot, pair_rows, keys, values, queries, d_out, w_key, w_value)
     kg = kg.reshape((NCTX,) + kg.shape[2:])
     vg = vg.reshape((NCTX,) + vg.shape[2:])
     gq, gqx, hdq, pk, pv = attend(span_slot, queries, d_out, qx, dox, kg, vg, unit)
-    pk = pk.reshape((CHIPS, 2) + pk.shape[1:])
-    pv = pv.reshape((CHIPS, 2) + pv.shape[1:])
-    grad_k, grad_v, gqo, mid, far = scatter_sums(pk, pv, near, gqx, w_key, w_value)
-    grad_x, units = project(grad_k, grad_v, hdq, w_key, w_value, near, mid, far)
+    pk = pk.reshape((PARTS, CHIPS, 2) + pk.shape[2:])
+    pv = pv.reshape((PARTS, CHIPS, 2) + pv.shape[2:])
+    grad_k, grad_v, gqo, grad_x, units = reduce_project(pk, pv, near, gqx, hdq, w_key, w_value)
     return finish(span_slot, gq, gqo, units, grad_k, grad_v, grad_x)
 
 

time: 163 us -> 146 us (0.90)
  Pallas kernels: 158 us -> 144 us
  other arithmetic: 2.34 us -> 0.68 us
    pallas_call x2 -> x1, Pallas kernels: 79.3 us -> 59.9 us  [reduce_project(): pl.pallas_call(reduce_project_kernel, out_shape=(jax.ShapeDtypeStruct((2...]
    pallas_call x1, Pallas kernels: 30.6 us -> 35.7 us  [attend(): pl.pallas_call(attend_kernel, out_shape=(jax.ShapeDtypeStruct((2 * CH, GR...]
where the time goes in v4:
time: 146 us
  Pallas kernels  144 us (99%)
    pallas_call x1, Pallas kernels, reduce_project(): pl.pallas_call(reduce_project_kernel, out_shape=(jax.ShapeDtypeStruct((2...  59.9 us
    pallas_call x1, Pallas kernels, gather_all(): pl.pallas_call(gather_kernel, out_shape=(jax.ShapeDtypeStruct((CHIPS, 2,...  43.6 us
    pallas_call x1, Pallas kernels, attend(): pl.pallas_call(attend_kernel, out_shape=(jax.ShapeDtypeStruct((2 * CH, GR...  35.7 us
    pallas_call x1, Pallas kernels, finish(): pl.pallas_call(finish_kernel, out_shape=(jax.ShapeDtypeStruct((2 * CH, 2...  4.68 us

profile of v4, /device:TPU:1, one launch (start us, length us, event | category | flops | bytes accessed | tf_op | source)
XLA Modules:
  0.0 146.0 jit_solution(18388937081108178391)
XLA Ops:
  0.6 0.7 convert_element_type.5
  1.3 0.1 copy.13
  1.4 0.6 pad.4.pairs_ref
  2.0 43.6 %gather_kv.1 = (bf16[16,2,272,128]{3,2,1,0:T(8,128)(2,1)}, bf16[16,2,256,128]{3,2,1,0:T(8,128)(2,1)}, bf16[2,128,128]{2,1,0:T(8,128)(2,1)}, bf16[256,1024]{1,0:T...) custom-call(s32[64]{0:T(128)} %span_slot.5, bf16[16,128]{1,0:T(8,128)(2,1)} %pad.4.pairs_ref, ...), custom_call_target="tpu_custom_call" | custom-call | tf_op jit(solution)/shard_map/gather_kv/pallas_call | solution.py:292
  45.6 35.7 %attend.1 = (bf16[256,1024]{1,0:T(8,128)(2,1)}, bf16[256,1024]{1,0:T(8,128)(2,1)}, bf16[128,128]{1,0:T(8,128)(2,1)}, bf16[2,32,4,32,128]{4,3,2,1,0:T(8,128)(2,1)}, bf16[2,32,4,32,128]{4,3,2,1,0:T(8,128)(2,1)}) custom-call(s32[64]{0:T(128)} %span_slot.5, bf16[256,2048]{1,0:T(8,128)(2,1)} %q_hbm.1, bf16[256,2048]{1,0:T(8,128)(2,1)} %do_hbm.1, ...), custom_call_target="tpu_custom_call" | custom-call | flops 8000000000 | bytes 32000000 | tf_op jit(solution)/shard_map/attend/pallas_call | solution.py:583
  81.3 59.9 %reduce_project.1 = (bf16[256,256]{1,0:T(8,128)(2,1)}, bf16[256,256]{1,0:T(8,128)(2,1)}, bf16[256,1024]{1,0:T(8,128)(2,1)}, bf16[64,8192]{1,0:T(8,128)(2,1)}, bf16[4,4,2,128,128]{4,3,2,1,0:T(8,128)(2,1)}) custom-call(bf16[2,16,2,4,32,128]{5,4,3,2,1,0:T(8,128)(2,1)} %bitcast.4, bf16[2,16,2,4,32,128]{5,4,3,2,1,0:T(8,128)(2,1)} %bitcast.5, ...), custom_call_target="tpu_custom_call" | custom-call | tf_op jit(solution)/shard_map/reduce_project/pallas_call | solution.py:912
  141.2 4.7 %finish.1 = (bf16[256,2048]{1,0:T(8,128)(2,1)}, bf16[256,256]{1,0:T(8,128)(2,1)}, bf16[256,256]{1,0:T(8,128)(2,1)}, bf16[64,8192]{1,0:T(8,128)(2,1)}) custom-call(s32[64]{0:T(128)} %span_slot.5, bf16[256,1024]{1,0:T(8,128)(2,1)} %get-tuple-element.25.gq_hbm, bf16[256,1024]{1,0:T(8,128)(2,1)} %get-tuple-element.31.gqo_hbm, ...), custom_call_target="tpu_custom_call" | custom-call | tf_op jit(solution)/shard_map/finish/pallas_call | solution.py:994

commit v5 on v4

--- a/solution.py
+++ b/solution.py
@@ -18,7 +18,8 @@
 CHIPS = NX * NY
 GROUP = 8
 PARTS = 2
-WIDE = 4
+WIDE = 8
+KEPT = 6
 NPAD = 16
 SCALE = HD ** -0.5
 EXP_SCALE = SCALE * 1.4426950408889634
@@ -343,7 +344,7 @@
 def attend_kernel(
     span_slot, q_hbm, do_hbm, qx_hbm, dox_hbm, kg_hbm, vg_hbm, unit_ref,
     gq_ref, gqx_ref, hdq_ref, pk_hbm, pv_hbm,
-    kg, vg, qs, ds, gq_all, stage, probs, dprob, tops, stat, acck, accv, dqt, found, flags, slot_label, todo,
+    kg, vg, qs, ds, gq_all, stage, probs, dprob, tops, kept_probs, kept_dprob, kept_tops, stat, acck, accv, dqt, found, flags, slot_label, todo,
     flag_sem, qsems, load_sems, store_sems,
 ):
     me = lax.axis_index("ctx")
@@ -376,7 +377,7 @@
         slot_label[span_slot[c]] = c
         return carry
 
-    lax.fori_loop(0, SPANS, name_slot, 0)
+    lax.fori_loop(0, SPANS, name_slot, 0, unroll=8)
 
     def slot_of(u):
         return 2 * (2 * unit + lax.rem(core + u // 2, 2)) + lax.rem(u, 2)
@@ -462,7 +463,7 @@
                 wanted = jnp.logical_and(flags[u, c] > 0, c != own_label)
                 return n + wanted.astype(jnp.int32)
 
-            count = lax.fori_loop(0, SPANS, note, jnp.int32(1))
+            count = lax.fori_loop(0, SPANS, note, jnp.int32(1), unroll=8)
             todo[count] = own_slot
 
             def rows_at(slot):
@@ -488,19 +489,27 @@
                     ], axis=0)
                 return scores, dot_nt(some(vg, base, size), ds[u])
 
-            def first(base, size, masked):
+            def first(keep, base, size, masked):
                 scores, mixed = dots(base, size, masked)
                 old_top = stat[0:1, :]
                 new_top = jnp.maximum(old_top, jnp.max(scores, axis=0, keepdims=True))
                 weights = jnp.exp2(scores - new_top)
                 factor = jnp.exp2(old_top - new_top)
+                if keep:
+                    kept_probs[base // 4, 0:size * CH, :] = weights
+                    kept_dprob[base // 4, 0:size * CH, :] = mixed
+                    kept_tops[base // 4] = new_top
                 stat[0:1, :] = new_top
                 stat[1:2, :] = stat[1:2, :] * factor + jnp.sum(weights, axis=0, keepdims=True)
                 stat[2:3, :] = stat[2:3, :] * factor + jnp.sum(weights * mixed, axis=0, keepdims=True)
 
-            def second(base, size, masked):
-                scores, mixed = dots(base, size, masked)
-                weights = jnp.exp2(scores - stat[3:4, :])
+            def second(keep, base, size, masked):
+                if keep:
+                    weights = kept_probs[base // 4, 0:size * CH, :] * jnp.exp2(kept_tops[base // 4] - stat[3:4, :])
+                    mixed = kept_dprob[base // 4, 0:size * CH, :]
+                else:
+                    scores, mixed = dots(base, size, masked)
+                    weights = jnp.exp2(scores - stat[3:4, :])
                 dscore = (weights * (mixed - stat[4:5, :])).astype(jnp.bfloat16)
                 value_part = dot_nn(weights.astype(jnp.bfloat16), ds[u])
                 key_part = dot_nn(dscore, qs[u])
@@ -511,35 +520,51 @@
                 dqt[...] += dot_tn(some(kg, base, size), dscore)
 
             fours = (count + 1) // 4
-
-            def sweep(work):
+            fits = (count + 3) // 4 <= KEPT
+
+            def sweep(work, keep):
                 def step(t, c):
                     masked = jnp.logical_or(t == 0, 4 * t + 4 > count)
 
                     @pl.when(masked)
                     def _():
-                        work(4 * t, 4, True)
+                        work(keep, 4 * t, 4, True)
 
                     @pl.when(jnp.logical_not(masked))
                     def _():
-                        work(4 * t, 4, False)
+                        work(keep, 4 * t, 4, False)
 
                     return c
 
-                lax.fori_loop(0, fours, step, 0)
+                def plain(t, c):
+                    work(keep, 4 * t, 4, False)
+                    return c
+
+                lax.fori_loop(0, fours, plain if keep and work is second else step, 0)
 
                 @pl.when(4 * fours < count)
                 def _():
-                    work(4 * fours, 2, True)
+                    work(keep, 4 * fours, 2, True)
 
             stat[0:1, :] = jnp.full((1, QB), neg_fill, jnp.float32)
             stat[1:3, :] = jnp.zeros((2, QB), jnp.float32)
-            sweep(first)
-            total_row = stat[1:2, :]
-            stat[3:4, :] = stat[0:1, :] + jnp.log2(total_row)
-            stat[4:5, :] = stat[2:3, :] / total_row
             dqt[...] = jnp.zeros_like(dqt)
-            sweep(second)
+
+            def both_sweeps(keep):
+                sweep(first, keep)
+                total_row = stat[1:2, :]
+                stat[3:4, :] = stat[0:1, :] + jnp.log2(total_row)
+                stat[4:5, :] = stat[2:3, :] / total_row
+                sweep(second, keep)
+
+            @pl.when(fits)
+            def _():
+                both_sweeps(True)
+
+            @pl.when(jnp.logical_not(fits))
+            def _():
+                both_sweeps(False)
+
             for r in range(GROUP):
                 gq_all[pl.ds(pl.multiple_of(u * CH, CH), CH), r * HD:(r + 1) * HD] = (
                     (dqt[:, r * CH:(r + 1) * CH] * SCALE).T.astype(jnp.bfloat16)
@@ -601,6 +626,9 @@
             pltpu.VMEM((NCTX // WIDE, 2 * WIDE * CH, HD), jnp.float32),
             pltpu.VMEM((NCTX // WIDE, 2 * WIDE * CH, HD), jnp.float32),
             pltpu.VMEM((NCTX // WIDE, 1, HD), jnp.float32),
+            pltpu.VMEM((KEPT, 4 * CH, QB), jnp.float32),
+            pltpu.VMEM((KEPT, 4 * CH, QB), jnp.float32),
+            pltpu.VMEM((KEPT, 1, QB), jnp.float32),
             pltpu.VMEM((8, QB), jnp.float32),
             pltpu.VMEM((NCTX, 2 * CH, HD), jnp.float32),
             pltpu.VMEM((NCTX, 2 * CH, HD), jnp.float32),

time: 146 us -> 139 us (0.952)
  Pallas kernels: 144 us -> 137 us
    pallas_call x1, Pallas kernels: 35.7 us -> 26.8 us  [attend(): pl.pallas_call(attend_kernel, out_shape=(jax.ShapeDtypeStruct((2 * CH, GR...]
    pallas_call x1, Pallas kernels: 59.9 us -> 61.6 us  [reduce_project(): pl.pallas_call(reduce_project_kernel, out_shape=(jax.ShapeDtypeStruct((2...]
where the time goes in v5:
time: 139 us
  Pallas kernels  137 us (99%)
    pallas_call x1, Pallas kernels, reduce_project(): pl.pallas_call(reduce_project_kernel, out_shape=(jax.ShapeDtypeStruct((2...  61.6 us
    pallas_call x1, Pallas kernels, gather_all(): pl.pallas_call(gather_kernel, out_shape=(jax.ShapeDtypeStruct((CHIPS, 2,...  43.6 us
    pallas_call x1, Pallas kernels, attend(): pl.pallas_call(attend_kernel, out_shape=(jax.ShapeDtypeStruct((2 * CH, GR...  26.8 us
    pallas_call x1, Pallas kernels, finish(): pl.pallas_call(finish_kernel, out_shape=(jax.ShapeDtypeStruct((2 * CH, 2...  4.68 us

profile of v5, /device:TPU:1, one launch (start us, length us, event | category | flops | bytes accessed | tf_op | source)
XLA Modules:
  0.0 138.8 jit_solution(2238831743840871100)
XLA Ops:
  0.6 0.7 convert_element_type.5
  1.3 0.1 copy.13
  1.4 0.6 pad.4.pairs_ref
  2.0 43.6 %gather_kv.1 = (bf16[16,2,272,128]{3,2,1,0:T(8,128)(2,1)}, bf16[16,2,256,128]{3,2,1,0:T(8,128)(2,1)}, bf16[2,128,128]{2,1,0:T(8,128)(2,1)}, bf16[256,1024]{1,0:T...) custom-call(s32[64]{0:T(128)} %span_slot.5, bf16[16,128]{1,0:T(8,128)(2,1)} %pad.4.pairs_ref, ...), custom_call_target="tpu_custom_call" | custom-call | tf_op jit(solution)/shard_map/gather_kv/pallas_call | solution.py:293
  45.6 26.8 %attend.1 = (bf16[256,1024]{1,0:T(8,128)(2,1)}, bf16[256,1024]{1,0:T(8,128)(2,1)}, bf16[128,128]{1,0:T(8,128)(2,1)}, bf16[2,32,4,32,128]{4,3,2,1,0:T(8,128)(2,1)}, bf16[2,32,4,32,128]{4,3,2,1,0:T(8,128)(2,1)}) custom-call(s32[64]{0:T(128)} %span_slot.5, bf16[256,2048]{1,0:T(8,128)(2,1)} %q_hbm.1, bf16[256,2048]{1,0:T(8,128)(2,1)} %do_hbm.1, ...), custom_call_target="tpu_custom_call" | custom-call | flops 8000000000 | bytes 32000000 | tf_op jit(solution)/shard_map/attend/pallas_call | solution.py:608
  72.4 61.6 %reduce_project.1 = (bf16[256,256]{1,0:T(8,128)(2,1)}, bf16[256,256]{1,0:T(8,128)(2,1)}, bf16[256,1024]{1,0:T(8,128)(2,1)}, bf16[64,8192]{1,0:T(8,128)(2,1)}, bf16[4,4,2,128,128]{4,3,2,1,0:T(8,128)(2,1)}) custom-call(bf16[2,16,2,4,32,128]{5,4,3,2,1,0:T(8,128)(2,1)} %bitcast.4, bf16[2,16,2,4,32,128]{5,4,3,2,1,0:T(8,128)(2,1)} %bitcast.5, ...), custom_call_target="tpu_custom_call" | custom-call | tf_op jit(solution)/shard_map/reduce_project/pallas_call | solution.py:940
  133.9 4.7 %finish.1 = (bf16[256,2048]{1,0:T(8,128)(2,1)}, bf16[256,256]{1,0:T(8,128)(2,1)}, bf16[256,256]{1,0:T(8,128)(2,1)}, bf16[64,8192]{1,0:T(8,128)(2,1)}) custom-call(s32[64]{0:T(128)} %span_slot.5, bf16[256,1024]{1,0:T(8,128)(2,1)} %get-tuple-element.25.gq_hbm, bf16[256,1024]{1,0:T(8,128)(2,1)} %get-tuple-element.31.gqo_hbm, ...), custom_call_target="tpu_custom_call" | custom-call | tf_op jit(solution)/shard_map/finish/pallas_call | solution.py:1022

commit v6 on v5

--- a/solution.py
+++ b/solution.py
@@ -196,10 +196,6 @@
 
         lax.fori_loop(0, CHIPS, unit, 0)
 
-    units = Copies(u_send, u_recv)
-    pick(give, 1 - core)
-    units.start(give, from_core, 0, sibling)
-
     for copy in own_copies:
         copy.wait()
     cross.landed(kg_ref.at[chip, 1 - core], 0, sibling)
@@ -208,6 +204,10 @@
         gather.begin_a()
     for gather in gathers:
         gather.spread(0)
+
+    units = Copies(u_send, u_recv)
+    pick(give, 1 - core)
+    units.start(give, from_core, 0, sibling)
 
     me_z = lax.axis_index("head")
     piece = near_ref.shape[2]
@@ -979,33 +979,36 @@
     loads = [pltpu.make_async_copy(src, mid, sems.at[n]) for n, (src, mid, _) in enumerate(ways)]
     for copy in loads:
         copy.start()
-    for i in range(2):
+    def span_copies(i):
         rows = pl.ds(i * CH, CH)
+        pair = []
+        for n, (src, which) in enumerate(((gq_hbm, core), (gqo_hbm, 1 - core))):
+            cols = pl.ds(pl.multiple_of(which * GROUP * HD, GROUP * HD), GROUP * HD)
+            pair.append(pltpu.make_async_copy(src.at[rows], vq.at[rows, cols], head_sems.at[i, n]))
+        heads = []
+        for s in range(2):
+            heads.append([])
+            for h in range(2 * GROUP):
+                chip = s * GROUP + h % GROUP
+                heads[s].append(pltpu.make_async_copy(
+                    hg_hbm.at[chip // NX, chip % NX, h // GROUP], vq.at[rows, pl.ds(h * HD, HD)], head_sems.at[i, h]
+                ))
         dense = [span_slot[SPANS - 2 + s] == 2 * me + i for s in range(2)]
         light = jnp.logical_not(jnp.logical_or(dense[0], dense[1]))
-
-        @pl.when(light)
+        return [(light, pair), (dense[0], heads[0]), (dense[1], heads[1])]
+
+    choices = span_copies(0) + span_copies(1)
+    for chosen, group in choices:
+        @pl.when(chosen)
         def _():
-            pair = []
-            for n, (src, which) in enumerate(((gq_hbm, core), (gqo_hbm, 1 - core))):
-                cols = pl.ds(pl.multiple_of(which * GROUP * HD, GROUP * HD), GROUP * HD)
-                pair.append(pltpu.make_async_copy(src.at[rows], vq.at[rows, cols], head_sems.at[n]))
-                pair[-1].start()
-            for copy in pair:
+            for copy in group:
+                copy.start()
+
+    for chosen, group in choices:
+        @pl.when(chosen)
+        def _():
+            for copy in group:
                 copy.wait()
-
-        for s in range(2):
-            @pl.when(dense[s])
-            def _():
-                heads = []
-                for h in range(2 * GROUP):
-                    chip = s * GROUP + h % GROUP
-                    heads.append(pltpu.make_async_copy(
-                        hg_hbm.at[chip // NX, chip % NX, h // GROUP], vq.at[rows, pl.ds(h * HD, HD)], head_sems.at[h]
-                    ))
-                    heads[-1].start()
-                for copy in heads:
-                    copy.wait()
 
     stores = [pltpu.make_async_copy(vq, oq, sems.at[3])]
     stores[0].start()
@@ -1035,7 +1038,7 @@
             pltpu.VMEM(grad_v.shape, grad_v.dtype),
             pltpu.VMEM(grad_x.shape, grad_x.dtype),
             pltpu.SemaphoreType.DMA((4,)),
-            pltpu.SemaphoreType.DMA((2 * GROUP,)),
+            pltpu.SemaphoreType.DMA((2, 2 * GROUP)),
         ],
         compiler_params=pltpu.CompilerParams(vmem_limit_bytes=VMEM_MIB * MIB),
         name="finish",

time: 139 us -> 138 us (level)
    pallas_call x1, Pallas kernels: 26.8 us -> 29.1 us  [attend(): pl.pallas_call(attend_kernel, out_shape=(jax.ShapeDtypeStruct((2 * CH, GR...]
where the time goes in v6:
time: 138 us; the launch traced here: 139 us
  Pallas kernels  136 us (99%)
    pallas_call x1, Pallas kernels, reduce_project(): pl.pallas_call(reduce_project_kernel, out_shape=(jax.ShapeDtypeStruct((2...  60.2 us
    pallas_call x1, Pallas kernels, gather_all(): pl.pallas_call(gather_kernel, out_shape=(jax.ShapeDtypeStruct((CHIPS, 2,...  43.4 us
    pallas_call x1, Pallas kernels, attend(): pl.pallas_call(attend_kernel, out_shape=(jax.ShapeDtypeStruct((2 * CH, GR...  29.1 us
    pallas_call x1, Pallas kernels, finish(): pl.pallas_call(finish_kernel, out_shape=(jax.ShapeDtypeStruct((2 * CH, 2...  3.66 us

profile of v6, /device:TPU:1, one launch (start us, length us, event | category | flops | bytes accessed | tf_op | source)
XLA Modules:
  0.0 138.6 jit_solution(9709207983490633071)
XLA Ops:
  0.6 0.7 convert_element_type.5
  1.3 0.1 copy.13
  1.4 0.6 pad.4.pairs_ref
  2.0 43.4 %gather_kv.1 = (bf16[16,2,272,128]{3,2,1,0:T(8,128)(2,1)}, bf16[16,2,256,128]{3,2,1,0:T(8,128)(2,1)}, bf16[2,128,128]{2,1,0:T(8,128)(2,1)}, bf16[256,1024]{1,0:T...) custom-call(s32[64]{0:T(128)} %span_slot.5, bf16[16,128]{1,0:T(8,128)(2,1)} %pad.4.pairs_ref, ...), custom_call_target="tpu_custom_call" | custom-call | tf_op jit(solution)/shard_map/gather_kv/pallas_call | solution.py:293
  45.4 29.1 %attend.1 = (bf16[256,1024]{1,0:T(8,128)(2,1)}, bf16[256,1024]{1,0:T(8,128)(2,1)}, bf16[128,128]{1,0:T(8,128)(2,1)}, bf16[2,32,4,32,128]{4,3,2,1,0:T(8,128)(2,1)}, bf16[2,32,4,32,128]{4,3,2,1,0:T(8,128)(2,1)}) custom-call(s32[64]{0:T(128)} %span_slot.5, bf16[256,2048]{1,0:T(8,128)(2,1)} %q_hbm.1, bf16[256,2048]{1,0:T(8,128)(2,1)} %do_hbm.1, ...), custom_call_target="tpu_custom_call" | custom-call | flops 8000000000 | bytes 32000000 | tf_op jit(solution)/shard_map/attend/pallas_call | solution.py:608
  74.5 60.2 %reduce_project.1 = (bf16[256,256]{1,0:T(8,128)(2,1)}, bf16[256,256]{1,0:T(8,128)(2,1)}, bf16[256,1024]{1,0:T(8,128)(2,1)}, bf16[64,8192]{1,0:T(8,128)(2,1)}, bf16[4,4,2,128,128]{4,3,2,1,0:T(8,128)(2,1)}) custom-call(bf16[2,16,2,4,32,128]{5,4,3,2,1,0:T(8,128)(2,1)} %bitcast.4, bf16[2,16,2,4,32,128]{5,4,3,2,1,0:T(8,128)(2,1)} %bitcast.5, ...), custom_call_target="tpu_custom_call" | custom-call | tf_op jit(solution)/shard_map/reduce_project/pallas_call | solution.py:940
  134.8 3.7 %finish.1 = (bf16[256,2048]{1,0:T(8,128)(2,1)}, bf16[256,256]{1,0:T(8,128)(2,1)}, bf16[256,256]{1,0:T(8,128)(2,1)}, bf16[64,8192]{1,0:T(8,128)(2,1)}) custom-call(s32[64]{0:T(128)} %span_slot.5, bf16[256,1024]{1,0:T(8,128)(2,1)} %get-tuple-element.25.gq_hbm, bf16[256,1024]{1,0:T(8,128)(2,1)} %get-tuple-element.31.gqo_hbm, ...), custom_call_target="tpu_custom_call" | custom-call | tf_op jit(solution)/shard_map/finish/pallas_call | solution.py:1025

commit v7 on v6

--- a/solution.py
+++ b/solution.py
@@ -155,8 +155,11 @@
     k_send, k_recv, v_send, v_recv, u_send, u_recv, w_send, w_recv, c_send, c_recv, own_sem,
 ):
     keys_pad[0:2 * CH, :] = keys_ref[...]
+    lanes = lax.broadcasted_iota(jnp.int32, (NPAD, HD), 1)
+    pairs = pairs_ref[...].astype(jnp.float32)
+    pair_rows = jnp.where(lanes == 0, pairs[:, 0:1], jnp.where(lanes == 1, pairs[:, 1:2], 0.0)).astype(jnp.bfloat16)
     for g in range(2):
-        keys_pad[2 * CH:2 * CH + NPAD, g * HD:(g + 1) * HD] = pairs_ref[...]
+        keys_pad[2 * CH:2 * CH + NPAD, g * HD:(g + 1) * HD] = pair_rows
     barrier_with(ctx_targets() + head_targets((1, 3)))
     y, x, core = ctx_coords()
     plane = Plane("x")
@@ -285,7 +288,7 @@
     moves.finish()
 
 
-def gather_all(span_slot, pair_rows, keys, values, queries, d_out, w_key, w_value):
+def gather_all(span_slot, pair_list, keys, values, queries, d_out, w_key, w_value):
     vmem = pl.BlockSpec(memory_space=pltpu.VMEM)
     anyspace = pl.BlockSpec(memory_space=pl.ANY)
     blk = jnp.bfloat16
@@ -326,7 +329,7 @@
             collective_id=0, has_side_effects=True, vmem_limit_bytes=VMEM_MIB * MIB
         ),
         name="gather_kv",
-    )(span_slot, pair_rows, keys, values, queries, d_out, w_key, w_value)
+    )(span_slot, pair_list, keys, values, queries, d_out, w_key, w_value)
 
 
 def dot_nt(a, b):
@@ -1046,8 +1049,7 @@
 
 
 def per_device(queries, keys, values, d_out, w_key, w_value, pair_list, span_slot):
-    pair_rows = jnp.pad(pair_list.astype(jnp.bfloat16), ((0, 0), (0, HD - 2)))
-    kg, vg, unit, qx, dox, near = gather_all(span_slot, pair_rows, keys, values, queries, d_out, w_key, w_value)
+    kg, vg, unit, qx, dox, near = gather_all(span_slot, pair_list, keys, values, queries, d_out, w_key, w_value)
     kg = kg.reshape((NCTX,) + kg.shape[2:])
     vg = vg.reshape((NCTX,) + vg.shape[2:])
     gq, gqx, hdq, pk, pv = attend(span_slot, queries, d_out, qx, dox, kg, vg, unit)

time: 138 us -> 139 us (level)
    pallas_call x1, Pallas kernels: 60.2 us -> 65.2 us  [reduce_project(): pl.pallas_call(reduce_project_kernel, out_shape=(jax.ShapeDtypeStruct((2...]
    pallas_call x1, Pallas kernels: 29.1 us -> 25.3 us  [attend(): pl.pallas_call(attend_kernel, out_shape=(jax.ShapeDtypeStruct((2 * CH, GR...]
where the time goes in v7:
time: 139 us; the launch traced here: 140 us
  Pallas kernels  137 us (99%)
    pallas_call x1, Pallas kernels, reduce_project(): pl.pallas_call(reduce_project_kernel, out_shape=(jax.ShapeDtypeStruct((2...  65.2 us
    pallas_call x1, Pallas kernels, gather_all(): pl.pallas_call(gather_kernel, out_shape=(jax.ShapeDtypeStruct((CHIPS, 2,...  43.4 us
    pallas_call x1, Pallas kernels, attend(): pl.pallas_call(attend_kernel, out_shape=(jax.ShapeDtypeStruct((2 * CH, GR...  25.3 us
    pallas_call x1, Pallas kernels, finish(): pl.pallas_call(finish_kernel, out_shape=(jax.ShapeDtypeStruct((2 * CH, 2...  3.62 us

profile of v7, /device:TPU:1, one launch (start us, length us, event | category | flops | bytes accessed | tf_op | source)
XLA Modules:
  0.0 139.7 jit_solution(2535163131178473062)
XLA Ops:
  0.6 1.4 copy.12.pairs_ref
  2.0 43.4 %gather_kv.1 = (bf16[16,2,272,128]{3,2,1,0:T(8,128)(2,1)}, bf16[16,2,256,128]{3,2,1,0:T(8,128)(2,1)}, bf16[2,128,128]{2,1,0:T(8,128)(2,1)}, bf16[256,1024]{1,0:T...) custom-call(s32[64]{0:T(128)} %span_slot.5, s32[16,2]{1,0:T(8,128)} %copy.12.pairs_ref, ...), custom_call_target="tpu_custom_call" | custom-call | tf_op jit(solution)/shard_map/gather_kv/pallas_call | solution.py:296
  45.4 25.3 %attend.1 = (bf16[256,1024]{1,0:T(8,128)(2,1)}, bf16[256,1024]{1,0:T(8,128)(2,1)}, bf16[128,128]{1,0:T(8,128)(2,1)}, bf16[2,32,4,32,128]{4,3,2,1,0:T(8,128)(2,1)}, bf16[2,32,4,32,128]{4,3,2,1,0:T(8,128)(2,1)}) custom-call(s32[64]{0:T(128)} %span_slot.5, bf16[256,2048]{1,0:T(8,128)(2,1)} %q_hbm.1, bf16[256,2048]{1,0:T(8,128)(2,1)} %do_hbm.1, ...), custom_call_target="tpu_custom_call" | custom-call | flops 8000000000 | bytes 32000000 | tf_op jit(solution)/shard_map/attend/pallas_call | solution.py:611
  70.7 65.2 %reduce_project.1 = (bf16[256,256]{1,0:T(8,128)(2,1)}, bf16[256,256]{1,0:T(8,128)(2,1)}, bf16[256,1024]{1,0:T(8,128)(2,1)}, bf16[64,8192]{1,0:T(8,128)(2,1)}, bf16[4,4,2,128,128]{4,3,2,1,0:T(8,128)(2,1)}) custom-call(bf16[2,16,2,4,32,128]{5,4,3,2,1,0:T(8,128)(2,1)} %bitcast.4, bf16[2,16,2,4,32,128]{5,4,3,2,1,0:T(8,128)(2,1)} %bitcast.5, ...), custom_call_target="tpu_custom_call" | custom-call | tf_op jit(solution)/shard_map/reduce_project/pallas_call | solution.py:943
  135.9 3.6 %finish.1 = (bf16[256,2048]{1,0:T(8,128)(2,1)}, bf16[256,256]{1,0:T(8,128)(2,1)}, bf16[256,256]{1,0:T(8,128)(2,1)}, bf16[64,8192]{1,0:T(8,128)(2,1)}) custom-call(s32[64]{0:T(128)} %span_slot.5, bf16[256,1024]{1,0:T(8,128)(2,1)} %get-tuple-element.25.gq_hbm, bf16[256,1024]{1,0:T(8,128)(2,1)} %get-tuple-element.31.gqo_hbm, ...), custom_call_target="tpu_custom_call" | custom-call | tf_op jit(solution)/shard_map/finish/pallas_call | solution.py:1028
